TPU v7x, 128 devices: a whole 4x4x4 slice. The times are simulated.
128 devices in a mesh: space: 32 (over x, z, core), chan: 4 (over y).
Axes of the slice: x: 4, y: 4, z: 4, core: 2. Of those that a mesh axis runs over, the one named last changes fastest.
Arguments:
- pages: bfloat16 [3584, 84, 256], P(('space', 'chan')), may hold values from -6 to 6
- merge_gain: bfloat16 [1024], replicated, may hold values from 0.25 to 1.75
- merge_shift: bfloat16 [1024], replicated, may hold values from -1.75 to 1.75
- merge_weight: bfloat16 [1024, 512], replicated, may hold values from -0.1875 to 0.1875
- norm_gain: bfloat16 [2, 512], replicated, may hold values from 0.25 to 1.75
- norm_shift: bfloat16 [2, 512], replicated, may hold values from -1.75 to 1.75
- qkv_weight: bfloat16 [512, 3, 512], P(None, None, 'chan'), may hold values from -0.25 to 0.25
- qv_bias: bfloat16 [2, 512], P(None, 'chan'), may hold values from -1.75 to 1.75
- rel_table: bfloat16 [16, 169], P('chan'), may hold values from -6 to 6
- out_weight: bfloat16 [512, 512], P('chan'), may hold values from -1 to 1
- out_bias: bfloat16 [512], P('chan'), may hold values from -1.75 to 1.75
- up_weight: bfloat16 [512, 2048], P(None, 'chan'), may hold values from -0.25 to 0.25
- up_bias: bfloat16 [2048], P('chan'), may hold values from -1.75 to 1.75
- down_weight: bfloat16 [2048, 512], P('chan'), may hold values from -0.125 to 0.125
- down_bias: bfloat16 [512], P('chan'), may hold values from -1.75 to 1.75
- cotangent: bfloat16 [1792, 42, 512], P('space', None, 'chan'), may hold values from -6 to 6
Outputs:
- block_out: float32 [1792, 42, 512], P('space', None, 'chan')
- pages_grad: float32 [3584, 84, 256], P(('space', 'chan'))
- merge_gain_grad: float32 [1024], replicated
- merge_shift_grad: float32 [1024], replicated
- merge_weight_grad: float32 [1024, 512], replicated
- norm_gain_grad: float32 [2, 512], replicated
- norm_shift_grad: float32 [2, 512], replicated
- qkv_weight_grad: float32 [512, 3, 512], P(None, None, 'chan')
- qv_bias_grad: float32 [2, 512], P(None, 'chan')
- rel_table_grad: float32 [16, 169], P('chan')
- out_weight_grad: float32 [512, 512], P('chan')
- out_bias_grad: float32 [512], P('chan')
- up_weight_grad: float32 [512, 2048], P(None, 'chan')
- up_bias_grad: float32 [2048], P('chan')
- down_weight_grad: float32 [2048, 512], P('chan')
- down_bias_grad: float32 [512], P('chan')
- branch_rms: float32 [3], replicated
All inputs are finite; a program needn't handle non-finite values.
Results may differ from a plain program's by a relative error of at most 0.025.
Values may be sent and summed in bfloat16 or wider, within the bound.
A program may use at most 128 MiB of HBM per device.

v0:
```python
import jax
import jax.numpy as jnp
from jax import lax
from jax.sharding import PartitionSpec as P

D = 512
HEADS = 16
HD = 32
WIN = 7
SHIFT = 3
PAGE_ROWS = 56


norm_epsilon = 1e-05
masked_score = -1000000000.0
highest = lax.Precision.HIGHEST


def shifted_2(shard, axis, by):
    count = lax.axis_size(axis)
    return lax.ppermute(shard, axis, [(i, (i + by) % count) for i in range(count)])


def to_windows(grid_values):
    rows_all, cols_all, channels = grid_values.shape
    blocks = grid_values.reshape(rows_all // WIN, WIN, cols_all // WIN, WIN, channels)
    return blocks.transpose(0, 2, 1, 3, 4).reshape(-1, WIN * WIN, channels)


def from_windows(blocks, rows_all, cols_all):
    channels = blocks.shape[-1]
    grid_values = blocks.reshape(rows_all // WIN, cols_all // WIN, WIN, WIN, channels)
    return grid_values.transpose(0, 2, 1, 3, 4).reshape(rows_all, cols_all, channels)


def relative_onehot():
    places = jnp.arange(WIN * WIN, dtype=jnp.int32)
    row_place = places // WIN
    col_place = places % WIN
    position_code = (
        (row_place[:, None] - row_place[None, :] + WIN - 1) * (2 * WIN - 1)
        + col_place[:, None]
        - col_place[None, :]
        + WIN
        - 1
    )
    entries = jnp.arange((2 * WIN - 1) ** 2, dtype=jnp.int32)
    return (entries[:, None] == position_code.reshape(1, -1)).astype(jnp.float32)


def region_codes(first_row, rows_band, cols_all, total_rows):
    row_global = first_row + jnp.arange(rows_band, dtype=jnp.int32)
    page_number = (row_global + SHIFT) % total_rows // PAGE_ROWS
    col_part = (jnp.arange(cols_all, dtype=jnp.int32) + SHIFT) // cols_all
    return page_number[:, None] * 2 + col_part[None, :]


def norm_forward(inputs, gain_vector, offset):
    average = jnp.mean(inputs, -1, keepdims=True)
    centered = inputs - average
    inverse = lax.rsqrt(jnp.mean(centered * centered, -1, keepdims=True) + norm_epsilon)
    unit_values = centered * inverse
    return (unit_values * gain_vector + offset, unit_values, inverse)


def norm_backward(grad_out, unit_values, inverse, gain_vector):
    scaled = grad_out * gain_vector
    first_mean = jnp.mean(scaled, -1, keepdims=True)
    second_mean = jnp.mean(scaled * unit_values, -1, keepdims=True)
    return inverse * (scaled - first_mean - unit_values * second_mean)


def gelu_exact(pre_values):
    return jax.nn.gelu(pre_values, approximate=False)


def body(
    pages,
    merge_gain,
    merge_shift,
    merge_weight,
    norm_gain,
    norm_shift,
    qkv_weight,
    qv_bias,
    rel_table,
    out_weight,
    out_bias,
    up_weight,
    up_bias,
    down_weight,
    down_bias,
    cotangent,
):
    chan_count = lax.axis_size("chan")
    space_count = lax.axis_size("space")
    chan_width = D // chan_count
    heads_here = HEADS // chan_count
    quad_rows = pages.shape[0] // 2
    cols_all = pages.shape[1] // 2
    band_rows = quad_rows * chan_count
    tokens_band = band_rows * cols_all
    page_lift = 2 * SHIFT
    offset_chan = lax.axis_index("chan") * chan_width
    scale_factor = HD ** (-0.5)

    def gather_features(shard_values):
        return lax.all_gather(shard_values, "chan", axis=1, tiled=True)

    def reduce_branch(partial_sum):
        return lax.psum_scatter(
            partial_sum.astype(jnp.bfloat16), "chan", scatter_dimension=1, tiled=True
        ).astype(jnp.float32)

    def gather_grads(shard_values):
        return lax.all_gather(shard_values, "chan", axis=1, tiled=True)

    def norm_back(partial_sum, unit_full, inverse, gain_full):
        summed = lax.psum(partial_sum.astype(jnp.bfloat16), "chan").astype(jnp.float32)
        grad_full = norm_backward(summed, unit_full, inverse, gain_full)
        grad_in = lax.dynamic_slice_in_dim(grad_full, offset_chan, chan_width, 1)
        gain_grad = lax.dynamic_slice_in_dim(
            jnp.sum(summed * unit_full, 0), offset_chan, chan_width, 0
        )
        shift_grad = lax.dynamic_slice_in_dim(jnp.sum(summed, 0), offset_chan, chan_width, 0)
        return (grad_in, gain_grad, shift_grad)

    def to_heads(flat_values):
        grid_values = flat_values.astype(jnp.bfloat16).reshape(band_rows, cols_all, chan_width)
        return to_windows(grid_values).reshape(-1, WIN * WIN, heads_here, chan_width // heads_here)

    def to_tokens(head_values):
        return from_windows(
            head_values.reshape(-1, WIN * WIN, chan_width), band_rows, cols_all
        ).reshape(tokens_band, chan_width)

    shifted = jnp.concatenate(
        [pages[page_lift:], shifted_2(pages[:page_lift], ("space", "chan"), -1)], 0
    )
    shifted = jnp.roll(shifted, -page_lift, axis=1)
    quad_tokens = (
        shifted.reshape(quad_rows, 2, cols_all, 2, pages.shape[2])
        .transpose(0, 2, 3, 1, 4)
        .reshape(quad_rows * cols_all, -1)
        .astype(jnp.float32)
    )
    merge_gain_float = merge_gain.astype(jnp.float32)
    merge_raw, merge_unit, merge_inverse = norm_forward(
        quad_tokens, merge_gain_float, merge_shift.astype(jnp.float32)
    )
    merge_normed = merge_raw.astype(jnp.bfloat16)
    merged_local = (
        jnp.dot(merge_normed, merge_weight, preferred_element_type=jnp.float32)
        .astype(jnp.bfloat16)
        .reshape(quad_rows, cols_all, D)
    )
    merged = lax.all_to_all(merged_local, "chan", split_axis=2, concat_axis=0, tiled=True)
    resid_zero = merged.reshape(tokens_band, chan_width)
    gains = norm_gain.astype(jnp.float32)
    shifts_norm = norm_shift.astype(jnp.float32)
    full_zero = gather_features(resid_zero).astype(jnp.float32)
    normed_raw, unit_one, inverse_one = norm_forward(full_zero, gains[0], shifts_norm[0])
    normed_one = normed_raw.astype(jnp.bfloat16)
    qkv_local = qkv_weight.reshape(D, 3 * chan_width)
    projected = jnp.dot(normed_one, qkv_local, preferred_element_type=jnp.float32).reshape(
        tokens_band, 3, chan_width
    )
    biases = qv_bias.astype(jnp.float32)
    queries = to_heads(projected[:, 0] + biases[0])
    key_heads = to_heads(projected[:, 1])
    values = to_heads(projected[:, 2] + biases[1])
    onehot_table = relative_onehot()
    position_bias = jnp.dot(rel_table.astype(jnp.float32), onehot_table, precision=highest).reshape(
        heads_here, WIN * WIN, WIN * WIN
    )
    region_grid = region_codes(
        lax.axis_index("space") * band_rows, band_rows, cols_all, band_rows * space_count
    )
    region_win = to_windows(region_grid[:, :, None])[:, :, 0]
    allowed = (region_win[:, :, None] == region_win[:, None, :])[:, None]

    def masked_scores(query_win, key_win):
        raw_scores = jnp.einsum(
            "tqhd,tkhd->thqk", query_win, key_win, preferred_element_type=jnp.float32
        )
        return jnp.where(allowed, raw_scores * scale_factor + position_bias, masked_score)

    scores = masked_scores(queries, key_heads)
    row_peak = jnp.max(scores, -1, keepdims=True)
    log_total = row_peak + jnp.log(jnp.sum(jnp.exp(scores - row_peak), -1, keepdims=True))
    weights = jnp.exp(scores - log_total)
    attended_win = jnp.einsum(
        "thqk,tkhd->tqhd", weights.astype(jnp.bfloat16), values, preferred_element_type=jnp.float32
    ).astype(jnp.bfloat16)
    attended = to_tokens(attended_win)
    branch_one = reduce_branch(
        jnp.dot(attended, out_weight, preferred_element_type=jnp.float32)
    ) + out_bias.astype(jnp.float32)
    resid_one = resid_zero.astype(jnp.float32) + branch_one
    full_one = gather_features(resid_one.astype(jnp.bfloat16)).astype(jnp.float32)
    normed_raw_two, unit_two, inverse_two = norm_forward(full_one, gains[1], shifts_norm[1])
    normed_two = normed_raw_two.astype(jnp.bfloat16)
    hidden_pre = jnp.dot(
        normed_two, up_weight, preferred_element_type=jnp.float32
    ) + up_bias.astype(jnp.float32)
    hidden = gelu_exact(hidden_pre).astype(jnp.bfloat16)
    branch_two = reduce_branch(
        jnp.dot(hidden, down_weight, preferred_element_type=jnp.float32)
    ) + down_bias.astype(jnp.float32)
    resid_two = resid_one + branch_two
    result_grid = jnp.roll(resid_two.reshape(band_rows, cols_all, chan_width), SHIFT, axis=1)
    block_out = jnp.concatenate(
        [
            shifted_2(result_grid[-SHIFT:].astype(jnp.bfloat16), "space", 1).astype(jnp.float32),
            result_grid[:-SHIFT],
        ],
        0,
    )
    cotangent_grid = jnp.roll(cotangent, -SHIFT, axis=1)
    cotangent_grid = jnp.concatenate(
        [cotangent_grid[SHIFT:], shifted_2(cotangent_grid[:SHIFT], "space", -1)], 0
    )
    grad_two = cotangent_grid.reshape(tokens_band, chan_width).astype(jnp.float32)
    down_bias_grad = jnp.sum(grad_two, 0)
    grad_two_full = gather_grads(grad_two.astype(jnp.bfloat16))
    down_weight_grad = jnp.einsum(
        "tf,td->fd", hidden, grad_two_full, preferred_element_type=jnp.float32
    )
    grad_hidden = jnp.einsum(
        "td,fd->tf", grad_two_full, down_weight, preferred_element_type=jnp.float32
    )
    grad_pre = jax.vjp(gelu_exact, hidden_pre)[1](grad_hidden)[0].astype(jnp.bfloat16)
    up_bias_grad = jnp.sum(grad_pre.astype(jnp.float32), 0)
    up_weight_grad = jnp.einsum(
        "tc,tf->cf", normed_two, grad_pre, preferred_element_type=jnp.float32
    )
    norm_partial_two = jnp.einsum(
        "tf,cf->tc", grad_pre, up_weight, preferred_element_type=jnp.float32
    )
    grad_norm_two, gain_two_grad, shift_two_grad = norm_back(
        norm_partial_two, unit_two, inverse_two, gains[1]
    )
    grad_one = grad_two + grad_norm_two
    out_bias_grad = jnp.sum(grad_one, 0)
    grad_one_full = gather_grads(grad_one.astype(jnp.bfloat16))
    out_weight_grad = jnp.einsum(
        "tc,td->cd", attended, grad_one_full, preferred_element_type=jnp.float32
    )
    grad_attended = to_heads(
        jnp.einsum("td,cd->tc", grad_one_full, out_weight, preferred_element_type=jnp.float32)
    )
    weights_again = jnp.exp(masked_scores(queries, key_heads) - log_total)
    grad_weights = jnp.einsum(
        "tqhd,tkhd->thqk", grad_attended, values, preferred_element_type=jnp.float32
    )
    values_grad = jnp.einsum(
        "thqk,tqhd->tkhd",
        weights_again.astype(jnp.bfloat16),
        grad_attended,
        preferred_element_type=jnp.float32,
    ).astype(jnp.bfloat16)
    inner_sum = jnp.sum(grad_weights * weights_again, -1, keepdims=True)
    grad_scores = (weights_again * (grad_weights - inner_sum)).astype(jnp.bfloat16)
    table_grad = jnp.dot(
        jnp.sum(grad_scores.astype(jnp.float32), 0).reshape(heads_here, -1),
        onehot_table.T,
        precision=highest,
    )
    queries_grad = (
        jnp.einsum("thqk,tkhd->tqhd", grad_scores, key_heads, preferred_element_type=jnp.float32)
        * scale_factor
    ).astype(jnp.bfloat16)
    keys_grad = (
        jnp.einsum("thqk,tqhd->tkhd", grad_scores, queries, preferred_element_type=jnp.float32)
        * scale_factor
    ).astype(jnp.bfloat16)
    queries_tokens = to_tokens(queries_grad)
    values_tokens = to_tokens(values_grad)
    grad_project = jnp.stack([queries_tokens, to_tokens(keys_grad), values_tokens], 1).reshape(
        tokens_band, 3 * chan_width
    )
    qkv_weight_grad = jnp.einsum(
        "tc,tk->ck", normed_one, grad_project, preferred_element_type=jnp.float32
    ).reshape(D, 3, chan_width)
    qv_bias_grad = jnp.stack(
        [
            jnp.sum(queries_tokens.astype(jnp.float32), 0),
            jnp.sum(values_tokens.astype(jnp.float32), 0),
        ],
        0,
    )
    norm_partial_one = jnp.einsum(
        "tk,ck->tc", grad_project, qkv_local, preferred_element_type=jnp.float32
    )
    grad_norm_one, gain_one_grad, shift_one_grad = norm_back(
        norm_partial_one, unit_one, inverse_one, gains[0]
    )
    grad_zero = (
        (grad_one + grad_norm_one).astype(jnp.bfloat16).reshape(band_rows, cols_all, chan_width)
    )
    grad_merged = lax.all_to_all(
        grad_zero, "chan", split_axis=0, concat_axis=2, tiled=True
    ).reshape(quad_rows * cols_all, D)
    merge_weight_grad = jnp.einsum(
        "tc,td->cd", merge_normed, grad_merged, preferred_element_type=jnp.float32
    )
    grad_merge_normed = jnp.einsum(
        "td,cd->tc", grad_merged, merge_weight, preferred_element_type=jnp.float32
    )
    merge_gain_grad = jnp.sum(grad_merge_normed * merge_unit, 0)
    merge_shift_grad = jnp.sum(grad_merge_normed, 0)
    grad_quads = norm_backward(grad_merge_normed, merge_unit, merge_inverse, merge_gain_float)
    grad_pages = (
        grad_quads.reshape(quad_rows, cols_all, 2, 2, -1)
        .transpose(0, 3, 1, 2, 4)
        .reshape(2 * quad_rows, 2 * cols_all, -1)
    )
    grad_pages = jnp.roll(grad_pages, page_lift, axis=1)
    pages_grad = jnp.concatenate(
        [
            shifted_2(grad_pages[-page_lift:].astype(jnp.bfloat16), ("space", "chan"), 1).astype(
                jnp.float32
            ),
            grad_pages[:-page_lift],
        ],
        0,
    )

    def padded(share_values):
        return lax.dynamic_update_slice_in_dim(
            jnp.zeros((D,), jnp.float32), share_values, offset_chan, 0
        )

    squares = jnp.stack(
        [
            jnp.sum(block_out * block_out),
            jnp.sum(branch_one * branch_one),
            jnp.sum(branch_two * branch_two),
        ]
    )
    shared = lax.psum(
        (
            merge_weight_grad,
            merge_gain_grad,
            merge_shift_grad,
            jnp.stack([padded(gain_one_grad), padded(gain_two_grad)], 0),
            jnp.stack([padded(shift_one_grad), padded(shift_two_grad)], 0),
            squares,
        ),
        ("space", "chan"),
    )
    sharded = (
        lax.psum(qkv_weight_grad.astype(jnp.bfloat16), "space").astype(jnp.float32),
        lax.psum(qv_bias_grad.astype(jnp.bfloat16), "space").astype(jnp.float32),
        lax.psum(table_grad.astype(jnp.bfloat16), "space").astype(jnp.float32),
        lax.psum(out_weight_grad.astype(jnp.bfloat16), "space").astype(jnp.float32),
        lax.psum(out_bias_grad.astype(jnp.bfloat16), "space").astype(jnp.float32),
        lax.psum(up_weight_grad.astype(jnp.bfloat16), "space").astype(jnp.float32),
        lax.psum(up_bias_grad.astype(jnp.bfloat16), "space").astype(jnp.float32),
        lax.psum(down_weight_grad.astype(jnp.bfloat16), "space").astype(jnp.float32),
        lax.psum(down_bias_grad.astype(jnp.bfloat16), "space").astype(jnp.float32),
    )
    element_total = float(band_rows * cols_all * D * space_count)
    branch_rms = jnp.sqrt(shared[5] / element_total)
    return (
        block_out,
        pages_grad,
        shared[1],
        shared[2],
        shared[0],
        shared[3],
        shared[4],
        sharded[0],
        sharded[1],
        sharded[2],
        sharded[3],
        sharded[4],
        sharded[5],
        sharded[6],
        sharded[7],
        sharded[8],
        branch_rms,
    )


def solution(mesh):
    placed = (
        P(("space", "chan"), None, None),
        P(),
        P(),
        P(),
        P(),
        P(),
        P(None, None, "chan"),
        P(None, "chan"),
        P("chan", None),
        P("chan", None),
        P("chan"),
        P(None, "chan"),
        P("chan"),
        P("chan", None),
        P("chan"),
        P("space", None, "chan"),
    )
    return jax.shard_map(
        body,
        mesh=mesh,
        in_specs=placed,
        out_specs=(
            P("space", None, "chan"),
            P(("space", "chan"), None, None),
            P(),
            P(),
            P(),
            P(),
            P(),
            P(None, None, "chan"),
            P(None, "chan"),
            P("chan", None),
            P("chan", None),
            P("chan"),
            P(None, "chan"),
            P("chan"),
            P("chan", None),
            P("chan"),
            P(),
        ),
        check_vma=False,
    )
```

profile of v0, /device:TPU:1, one launch (start us, length us, event | category | flops | bytes accessed | tf_op | source)
XLA Modules:
  0.0 865.7 jit_solution(13993496858138666856)
XLA Ops:
  23.2 8.7 %multiply_reduce_fusion.5 = f32[14,42]{1,0:T(8,128)S(1)} fusion(f32[14,42]{1,0:T(8,128)S(1)} %broadcast_multiply_fusion.6, f32[14,2,42,2,256]{4,3,2,1,0:T(2,128)S(1)} %reshape.364), kind=kLoop, calls=%fused_computation.68 | loop fusion | flops 1805748 | bytes 2413152 | tf_op jit(solution)/shard_map/reduce_sum | solution.py:61
  48.2 5.2 reshape.371
  53.3 15.7 %all_to_all.30 = bf16[4,2,37632]{2,1,0:T(2,128)(2,1)} all-to-all(bf16[4,2,37632]{2,1,0:T(2,128)(2,1)} %reshape.371), channel_id=1, replica_groups=mesh['space'=32,'chan'=4] {'chan'}, dimensions={0} | all-to-all | bytes 1204224 | tf_op jit(solution)/shard_map/all_to_all | solution.py:157
  69.0 5.2 reshape.372
  91.1 30.8 %all-gather.5.cloned.1.call-done = bf16[2352,512]{1,0:T(8,128)(2,1)} async-done(((bf16[2352,128]{1,0:T(8,128)(2,1)}), bf16[2352,512]{1,0:T(8,128)(2,1)}) %all-gather.5.cloned.1.call-update) | async-done | bytes 2408464 | tf_op jit(solution)/shard_map/all_gather | solution.py:108
  142.4 4.7 reshape_reshape.36
  147.1 5.0 copy.126
  152.1 4.7 reshape_reshape.35
  156.7 5.0 copy.129
  161.8 4.7 reshape_reshape.37
  166.4 5.2 copy.127
  180.2 5.0 copy.131
  202.4 33.8 %reduce-scatter.7.cloned.1.call-done = bf16[128,2352]{1,0:T(8,128)(2,1)} async-done(((bf16[512,2352]{1,0:T(8,128)(2,1)}), bf16[128,2352]{1,0:T(8,128)(2,1)}) %reduce-scatter.7.cloned.1.call-update) | async-done | bytes 602128
  251.1 25.6 %all-gather.7.cloned.1.call-done = bf16[2352,512]{1,0:T(8,128)(2,1)} async-done(((bf16[2352,128]{1,0:T(8,128)(2,1)}), bf16[2352,512]{1,0:T(8,128)(2,1)}) %all-gather.7.cloned.1.call-update) | async-done | bytes 2408464 | tf_op jit(solution)/shard_map/all_gather | solution.py:108
  284.8 31.5 %all-gather.9.cloned.1.call-done = bf16[2352,512]{1,0:T(8,128)(2,1)} async-done(((bf16[2352,128]{1,0:T(8,128)(2,1)}), bf16[2352,512]{1,0:T(8,128)(2,1)}) %all-gather.9.cloned.1.call-update) | async-done | bytes 2408464 | tf_op jit(solution)/shard_map/all_gather | solution.py:116
  316.3 15.8 %fusion.75 = (bf16[512]{0:T(512)(128)(2,1)}, bf16[2352,512]{1,0:T(8,128)(2,1)S(1)}, f32[2352,512]{1,0:T(8,128)}) fusion(f32[2352,512]{1,0:T(8,128)} %convolution_add_fusion, bf16[2352,512]{1,0:T(8,128)(2,1)} %all-gather.9.cloned.1.call-done, bf16[512,512]{1,0:T(8,128)(2,1)} %param.29), kind=kOutput, calls=%fused_computation.189 | convolution fusion | flops 1321033216 | bytes 14976000 | tf_op jit(solution)/shard_map/td,fd->tf/dot_general | solution.py:229
  336.4 65.8 %all-reduce.8.cloned.1.call-done = bf16[2352,512]{1,0:T(8,128)(2,1)} async-done(((bf16[2352,512]{1,0:T(8,128)(2,1)}), bf16[2352,512]{1,0:T(8,128)(2,1)}) %all-reduce.8.cloned.1.call-update) | async-done | bytes 2408464 | tf_op jit(solution)/shard_map/psum | solution.py:119
  402.2 6.2 fusion.7
  412.5 5.2 multiply_convert_fusion.1
  441.2 7.4 all-gather.11.cloned.1.call-done
  458.0 6.4 fusion.83
  464.4 5.0 copy.147
  473.8 5.7 multiply_reduce_fusion
  486.2 5.0 copy.143
  499.6 5.0 copy.139
  512.8 4.9 convolution_convert_fusion.7
  545.5 33.0 %all-reduce.10.cloned.1.call-done = bf16[2352,512]{1,0:T(8,128)(2,1)} async-done(((bf16[2352,512]{1,0:T(8,128)(2,1)}), bf16[2352,512]{1,0:T(8,128)(2,1)}) %all-reduce.10.cloned.1.call-update) | async-done | bytes 2408464 | tf_op jit(solution)/shard_map/psum | solution.py:119
  578.5 4.8 fusion.8
  591.4 64.4 %all-reduce.1 = (bf16[2,128]{1,0:T(2,128)(2,1)S(1)}, bf16[4,169]{1,0:T(4,128)(2,1)S(1)}, bf16[128]{0:T(256)(128)(2,1)S(1)}, bf16[512]{0:T(512)(128)(2,1)S(1)}, bf16[128]{0:T(256)(128)(2,1)S(1)}) all-reduce(bf16[2,128]{1,0:T(2,128)(2,1)S(1)} %pad_maximum_fusion.7, ...), channel_id=1, replica_groups=mesh['space'=32,'chan'=4] {'space'}, use_global_device_ids=true, to_apply=%region_33.34 | all-reduce | flops 1700 | bytes 6800 | tf_op jit(solution)/shard_map/psum | solution.py:354
  658.6 31.5 %all-reduce.14.cloned.1.call-done = (bf16[512,3,128]{2,0,1:T(8,128)(2,1)}, bf16[128,512]{1,0:T(8,128)(2,1)}, bf16[512,512]{1,0:T(8,128)(2,1)}, bf16[512,512]{1,0:T(8,128)(2,1)}) async-done(((bf16[512,3,128]{2,0,1:T(8,128)(2,1)}, bf16[128,512]{1,0:T(8,128)(2,1)}, bf16[512,512]{1,0:T(8,128)(2,1)}, bf16[512,512]{1,0:T(8,128)(2,1)}), (bf16[512,3,128]{2,0,1:T(8,128)(2,1)}, bf16[128,512]{1,0:T(8,128)(2,1)}, ...) | async-done | bytes 1572880 | tf_op jit(solution)/shard_map/psum | solution.py:353
  722.9 66.9 %all-reduce = (f32[1024]{0:T(1024)}, f32[1024]{0:T(1024)}, f32[2,512]{1,0:T(2,128)}, f32[2,512]{1,0:T(2,128)}, f32[3]{0:T(128)S(1)}) all-reduce(f32[1024]{0:T(1024)S(1)} %get-tuple-element.68, f32[1024]{0:T(1024)S(1)} %get-tuple-element.75, ...), channel_id=1, replica_groups=mesh['space'=32,'chan'=4] {'space','chan'}, use_global_device_ids=true, to_apply=%region_20.21 | all-reduce | flops 4099 | bytes 32792 | tf_op jit(solution)/shard_map/psum | solution.py:341
  793.9 61.5 %all-reduce.12.cloned.1.call-done = f32[1024,512]{1,0:T(8,128)} async-done(((f32[1024,512]{1,0:T(8,128)}), f32[1024,512]{1,0:T(8,128)}) %all-reduce.12.cloned.1.call-update) | async-done | bytes 2097168 | tf_op jit(solution)/shard_map/psum | solution.py:341
  (350 shorter events, 265.2 us)
Async XLA Ops:
  7.2 31.8 %copy-start = (bf16[1024,512]{1,0:T(8,128)(2,1)S(1)}, bf16[1024,512]{1,0:T(8,128)(2,1)}, u32[]{:S(2)}) copy-start(bf16[1024,512]{1,0:T(8,128)(2,1)} %param.19) | copy-start | bytes 3145732
  7.2 114.7 %all-gather.5.cloned.1.call-start = ((), (), s32[]{:S(2)}) async-start(), calls=%async_computation.4 | async-start | bytes 3010560 | tf_op jit(solution)/shard_map/all_gather | solution.py:108
  8.3 8.0 collective-permute-start
  13.8 25.1 %copy-start.42 = (f32[1024]{0:T(1024)}, f32[1024]{0:T(1024)S(1)}, u32[]{:S(2)}) copy-start(f32[1024]{0:T(1024)S(1)} %convert_element_type.234) | copy-start | bytes 12292
  23.1 11.5 %copy-start.27 = (f32[14,42]{1,0:T(8,128)}, f32[14,42]{1,0:T(8,128)S(1)}, u32[]{:S(2)}) copy-start(f32[14,42]{1,0:T(8,128)S(1)} %broadcast_multiply_fusion.6) | copy-start | bytes 7060
  23.2 15.8 %copy-start.38 = (f32[588]{0:T(1024)}, f32[588]{0:T(1024)S(1)}, u32[]{:S(2)}) copy-start(f32[588]{0:T(1024)S(1)} %div.78) | copy-start | bytes 7060
  74.2 8.0 copy-start.68
  77.7 11.0 %copy-start.52 = (bf16[2,512]{1,0:T(2,128)(2,1)S(1)}, bf16[2,512]{1,0:T(2,128)(2,1)}, u32[]{:S(2)}) copy-start(bf16[2,512]{1,0:T(2,128)(2,1)} %param.20) | copy-start | bytes 6148
  77.7 11.6 %copy-start.53 = (bf16[2,512]{1,0:T(2,128)(2,1)S(1)}, bf16[2,512]{1,0:T(2,128)(2,1)}, u32[]{:S(2)}) copy-start(bf16[2,512]{1,0:T(2,128)(2,1)} %param.21) | copy-start | bytes 6148
  81.8 154.4 %reduce-scatter.7.cloned.1.call-start = ((), (), s32[]{:S(2)}) async-start(), calls=%async_computation.11 | async-start | bytes 3112960
  82.1 42.0 %copy-start.44 = (s32[2401]{0:T(1024)}, s32[2401]{0:T(1024)S(1)}, u32[]{:S(2)}) copy-start(s32[2401]{0:T(1024)S(1)} %reshape.360) | copy-start | bytes 28816
  89.3 36.1 %copy-start.46 = (f32[1,512]{1,0:T(1,128)}, f32[1,512]{1,0:T(1,128)S(1)}, u32[]{:S(2)}) copy-start(f32[1,512]{1,0:T(1,128)S(1)} %get-tuple-element.114) | copy-start | bytes 6148
  89.9 35.5 %copy-start.56 = (f32[1,512]{1,0:T(1,128)}, f32[1,512]{1,0:T(1,128)S(1)}, u32[]{:S(2)}) copy-start(f32[1,512]{1,0:T(1,128)S(1)} %get-tuple-element.116) | copy-start | bytes 6148
  201.2 75.5 %all-gather.7.cloned.1.call-start = ((), (), s32[]{:S(2)}) async-start(), calls=%async_computation.5 | async-start | bytes 3010560 | tf_op jit(solution)/shard_map/all_gather | solution.py:108
  240.6 75.7 %all-gather.9.cloned.1.call-start = ((), (), s32[]{:S(2)}) async-start(), calls=%async_computation.6 | async-start | bytes 3010560 | tf_op jit(solution)/shard_map/all_gather | solution.py:116
  242.6 3.5 collective-permute-start.2
  249.8 152.5 %all-reduce.8.cloned.1.call-start = ((), (), s32[]{:S(2)}) async-start(), calls=%async_computation.7 | async-start | bytes 4816896 | tf_op jit(solution)/shard_map/psum | solution.py:119
  316.3 17.2 %copy-start.66 = (bf16[512,512]{1,0:T(8,128)(2,1)S(1)}, bf16[512,512]{1,0:T(8,128)(2,1)}, u32[]{:S(2)}) copy-start(bf16[512,512]{1,0:T(8,128)(2,1)} %param.27) | copy-start | bytes 1572868
  336.4 112.3 %all-gather.11.cloned.1.call-start = ((), (), s32[]{:S(2)}) async-start(), calls=%async_computation.8 | async-start | bytes 3010560 | tf_op jit(solution)/shard_map/all_gather | solution.py:116
  412.5 109.2 %reduce-scatter.9.cloned.1.call-start = ((), (), s32[]{:S(2)}) async-start(), calls=%async_computation.12 | async-start | bytes 3112960
  426.4 152.1 %all-reduce.10.cloned.1.call-start = ((), (), s32[]{:S(2)}) async-start(), calls=%async_computation.9 | async-start | bytes 4816896 | tf_op jit(solution)/shard_map/psum | solution.py:119
  437.1 11.5 %copy-start.21 = (bf16[128,512]{1,0:T(8,128)(2,1)S(1)}, bf16[128,512]{1,0:T(8,128)(2,1)}, u32[]{:S(2)}) copy-start(bf16[128,512]{1,0:T(8,128)(2,1)} %param.25) | copy-start | bytes 393220
  512.7 177.4 %all-reduce.14.cloned.1.call-start = ((), (), s32[]{:S(2)}) async-start(), calls=%async_computation.13 | async-start | bytes 3145728 | tf_op jit(solution)/shard_map/psum | solution.py:353
  527.9 4.1 collective-permute-start.1
  533.0 9.3 %copy-start.4 = (bf16[2352,512]{1,0:T(8,128)(2,1)S(1)}, bf16[2352,512]{1,0:T(8,128)(2,1)}, u32[]{:S(2)}) copy-start(bf16[2352,512]{1,0:T(8,128)(2,1)} %all-gather.5.cloned.1.call-done) | copy-start | bytes 7225348
  533.0 9.3 %copy-start.29 = (f32[2352]{0:T(1024)S(1)}, f32[2352]{0:T(1024)}, u32[]{:S(2)}) copy-start(f32[2352]{0:T(1024)} %copy-done.28) | copy-start | bytes 28228
  533.0 9.3 %copy-start.36 = (f32[2352]{0:T(1024)S(1)}, f32[2352]{0:T(1024)}, u32[]{:S(2)}) copy-start(f32[2352]{0:T(1024)} %copy-done.35) | copy-start | bytes 28228
  533.0 9.3 %copy-start.47 = (f32[1,512]{1,0:T(1,128)S(1)}, f32[1,512]{1,0:T(1,128)}, u32[]{:S(2)}) copy-start(f32[1,512]{1,0:T(1,128)} %copy-done.46) | copy-start | bytes 6148
  533.0 9.3 %copy-start.57 = (f32[1,512]{1,0:T(1,128)S(1)}, f32[1,512]{1,0:T(1,128)}, u32[]{:S(2)}) copy-start(f32[1,512]{1,0:T(1,128)} %copy-done.56) | copy-start | bytes 6148
  586.0 111.1 %all-to-all-start.1 = ((bf16[56,42,128]{2,1,0:T(8,128)(2,1)}), bf16[56,42,128]{2,1,0:T(8,128)(2,1)}, u32[]{:S(2)}, u32[]{:S(2)}) async-start(bf16[56,42,128]{2,1,0:T(8,128)(2,1)} %reshape.349), calls=%async_computation.1 | async-start | bytes 1376256 | tf_op jit(solution)/shard_map/all_to_all | solution.py:301
  590.2 265.1 %all-reduce.12.cloned.1.call-start = ((), (), s32[]{:S(2)}) async-start(), calls=%async_computation.10 | async-start | bytes 4194304 | tf_op jit(solution)/shard_map/psum | solution.py:341
  721.7 68.6 %collective-permute-start.3 = (bf16[6,84,256]{2,1,0:T(8,128)(2,1)}, bf16[6,84,256]{2,1,0:T(8,128)(2,1)}, u32[]{:S(2)}, u32[]{:S(2)}) collective-permute-start(bf16[6,84,256]{2,1,0:T(8,128)(2,1)} %fusion.56), channel_id=1, source_target_pairs={{0,1},{1,2},{2,3},{3,4},{4,5},{5,6},{6,7},{7,8},{8,9},{9,10},{10,1... | collective-permute-start | bytes 774152 | tf_op jit(solution)/shard_map/ppermute | solution.py:21
  (57 other events, 232.8 us)
Sparse Core Ops, SparseCore 0:
  82.0 39.9 all-gather.4
  201.3 34.8 reduce-scatter.6
  240.7 35.8 all-gather.6
  278.2 38.0 all-gather.8
  336.5 65.6 all-reduce.7
  412.6 35.9 all-gather.10
  451.8 34.7 reduce-scatter.8
  512.8 65.6 all-reduce.9
  583.4 106.7 all-reduce.13
  704.0 151.3 all-reduce.11
where the time goes:
time: 877 us; the launch traced here: 866 us
  waiting for transfers between devices  326 us (37%)
  local copies, waits for them, and re-layouts  193 us (22%)
  blocking collectives  147 us (17%)
  other arithmetic  86.5 us (10%)
  matrix products  84.2 us (10%)
  between operations  15.7 us (2%)
  starting transfers between devices  13.7 us (2%)
    psum x2, waiting for transfers between devices, norm_back(): lax.psum(partial_sum.astype(jnp.bfloat16), 'chan').astype(jnp.float32)  98.8 us
    psum x1, blocking collectives, body(): lax.psum((merge_weight_grad, merge_gain_grad, merge_shift_grad, jnp.stack...  66.9 us
    psum x1, blocking collectives, body(): lax.psum(qv_bias_grad.astype(jnp.bfloat16), 'space').astype(jnp.float32)  64.4 us
    psum x1, waiting for transfers between devices, body(): lax.psum((merge_weight_grad, merge_gain_grad, merge_shift_grad, jnp.stack...  61.5 us
    all_gather x2, waiting for transfers between devices, gather_features(): return lax.all_gather(shard_values, 'chan', axis=1, tiled=True)  56.4 us
    all_gather x2, waiting for transfers between devices, gather_grads(): return lax.all_gather(shard_values, 'chan', axis=1, tiled=True)  38.9 us
    unnamed x161, local copies, waits for them, and re-layouts  38.6 us
    another operation x8, local copies, waits for them, and re-layouts, to_heads(): to_windows(grid_values)  35.7 us
  transfers between devices with their start and end apart: 15, of which 12 were waited for; matrix products, arithmetic and copies ran while one was open for 21% of the time, Pallas kernels for 0%

commit v1 on v0

v1 whole, which is shorter than its diff:
```python
import functools

import jax
import jax.numpy as jnp
import numpy as np
from jax import lax
from jax.experimental import pallas as pl
from jax.experimental.pallas import tpu as pltpu
from jax.sharding import PartitionSpec as P

D = 512
HEADS = 16
HD = 32
FF = 2048
WIN = 7
SHIFT = 3
COLS = 42
ROWS = 14
WC = COLS // WIN
SLOT = 8
PAIR = 2 * WIN * SLOT
NPAIR = WC
T = PAIR * NPAIR
BAND = WC * WIN * SLOT
CHUNKS = 4
CH = D // CHUNKS
HEADS_C = HEADS // CHUNKS
LIFT = 2 * SHIFT
EPS = 1e-05
MASKED = -1e9
SCALE = HD ** (-0.5)
F32 = jnp.float32
BF16 = jnp.bfloat16


def dot(a, b):
    return jnp.dot(a, b, preferred_element_type=F32)


def dot_nt(a, b):
    return lax.dot_general(a, b, (((1,), (1,)), ((), ())), preferred_element_type=F32)


def dot_tn(a, b):
    return lax.dot_general(a, b, (((0,), (0,)), ((), ())), preferred_element_type=F32)


def constants():
    slots = np.arange(WC * SLOT)
    column = slots // SLOT * WIN + slots % SLOT
    real = slots % SLOT < WIN
    pages_sel = np.zeros((2, WC * SLOT, 2 * COLS), np.float32)
    for parity in range(2):
        source = (2 * column + parity + LIFT) % (2 * COLS)
        pages_sel[parity, slots[real], source[real]] = 1
    pages_sel = pages_sel.reshape(2 * WC * SLOT, 2 * COLS)
    token_sel = np.zeros((WC * SLOT, COLS), np.float32)
    source = (column + SHIFT) % COLS
    token_sel[slots[real], source[real]] = 1
    table_sel = np.zeros((256, SLOT, 128), np.float32)
    for b_q in range(WIN):
        for i in range(2 * WIN - 1):
            for b_k in range(WIN):
                code = (12 - i) * 13 + b_q - b_k + 6
                table_sel[code, b_q, i * SLOT + b_k] = 1
    table_sel = table_sel.reshape(256, SLOT * 128)
    return [jnp.asarray(a, BF16) for a in (pages_sel, pages_sel.T, token_sel, token_sel.T, table_sel)]


def iota(shape, dim):
    return lax.broadcasted_iota(jnp.int32, shape, dim)


def gelu_parts(x):
    z = jnp.abs(x) * (0.5**0.5)
    t = 1.0 / (1.0 + 0.3275911 * z)
    e = jnp.exp(-z * z)
    poly = t * (0.254829592 + t * (-0.284496736 + t * (1.421413741 + t * (-1.453152027 + t * 1.061405429))))
    tail = 0.5 * poly * e
    cdf = jnp.where(x >= 0, 1.0 - tail, tail)
    return x * cdf, cdf + x * e * 0.3989422804014327


def unit_of(x):
    centered = x - jnp.mean(x, -1, keepdims=True)
    inverse = lax.rsqrt(jnp.mean(centered * centered, -1, keepdims=True) + EPS)
    return centered * inverse, inverse


def norm_back(dy, u, inverse, gain):
    scaled = dy * gain
    first = jnp.mean(scaled, -1, keepdims=True)
    second = jnp.mean(scaled * u, -1, keepdims=True)
    return inverse * (scaled - first - u * second)


def col_sum(x):
    return jnp.sum(x, 0, keepdims=True)


def pair_mask(p, last_chan):
    q, k = iota((PAIR, 128), 0), iota((PAIR, 128), 1)
    half = PAIR // 2
    win_q, win_k = q // half, k // half
    a_q, a_k = (q % half) // SLOT, (k % half) // SLOT
    b_q, b_k = q % SLOT, k % SLOT
    w_col = (2 * p + win_q) % WC
    row_cut = jnp.logical_and(last_chan, 2 * p >= WC)
    ok = (win_q == win_k) & (k < PAIR) & (b_k < WIN)
    cut_r = WIN - SHIFT
    ok &= ((a_q < cut_r) == (a_k < cut_r)) | jnp.logical_not(row_cut)
    ok &= ((b_q < cut_r) == (b_k < cut_r)) | (w_col != WC - 1)
    return jnp.where(ok, 0.0, MASKED)


def head_lanes(x, h):
    lane = iota((1, CH), 1)
    return jnp.where(lane // HD == h, x, jnp.zeros_like(x))


def spread(x):
    padded = jnp.concatenate([x, jnp.zeros((128 - PAIR, CH), x.dtype)], 0)
    return jnp.concatenate([head_lanes(padded, h) for h in range(HEADS_C)], 0)


def stacked(x):
    return jnp.concatenate([head_lanes(x, h) for h in range(HEADS_C)], 0)


def by_head(x):
    return jnp.concatenate([x[:, 128 * h : 128 * h + 128] for h in range(HEADS_C)], 0)


def tile4(x):
    return jnp.concatenate([x] * HEADS_C, 1)


def rows_of(p, count=PAIR):
    return pl.ds(pl.multiple_of(p * count, 16), count)


SM_QV, SM_TABLE, SM_OUT_B, SM_UP_B, SM_DOWN_B = 0, 2, 10, 11, 15
RP_GAIN0, RP_SHIFT0, RP_GAIN, RP_SHIFT = 0, 1, 2, 4


def row_of(ref, c, first, count):
    return jnp.concatenate([ref[c, first + i : first + i + 1, :] for i in range(count)], 1)


def compute(
    pages, cot, merge_w, qkv_w, out_w, up_w, down_w, small, repl,
    pages_sel, pages_sel_t, token_sel, token_sel_t, table_sel,
    block_o, pages_o, d_merge_o, d_qkv_o, d_out_o, d_up_o, d_down_o, d_small_o, d_repl_o, squares_o,
    x0, inv0, mn, mt, u1, inv1, n1, qkv, prob, att, r1, u2, inv2, n2, g2, br2, dy2,
    gelu_d, hid, dpre, bias, lmat, gsum, dqkv, dy1, g1, g1f, gz, tmp,
):
    chan = lax.axis_index("chan")
    last_chan = chan == CHUNKS - 1
    valid = (iota((PAIR, 1), 0) % SLOT < WIN).astype(F32)

    def quads(i, _):
        base = (i // WIN) * BAND + (i % WIN) * SLOT
        for q in range(2):
            y = dot(pages_sel[...], pages[2 * i + q + LIFT])
            for par in range(2):
                for wc in range(WC):
                    lanes = par * 512 + q * 256
                    at = pl.multiple_of(base + wc * WIN * SLOT, SLOT)
                    first = par * WC * SLOT + wc * SLOT
                    x0[pl.ds(at, SLOT), lanes : lanes + 256] = y[first : first + SLOT]
        y = jnp.concatenate([dot(token_sel[...], cot[c, i]) for c in range(CHUNKS)], 1)
        for wc in range(WC):
            at = pl.multiple_of(base + wc * WIN * SLOT, SLOT)
            tmp[pl.ds(at, SLOT), 0:D] = y[wc * SLOT : wc * SLOT + SLOT]
        return 0

    lax.fori_loop(0, ROWS, quads, 0)

    def norm0(p, _):
        r = rows_of(p)
        u, inverse = unit_of(x0[r, :])
        x0[r, :] = u
        inv0[r, :] = inverse
        mn[r, :] = (u * repl[RP_GAIN0 : RP_GAIN0 + 1, :] + repl[RP_SHIFT0 : RP_SHIFT0 + 1, :]).astype(BF16)
        g2[r, :] = tmp[r, 0:D].astype(BF16)
        return 0

    lax.fori_loop(0, NPAIR, norm0, 0)
    mt[...] = dot(mn[...], merge_w[...]).astype(BF16)

    gain = [repl[RP_GAIN + i : RP_GAIN + i + 1, 0:D] for i in range(2)]
    shift = [repl[RP_SHIFT + i : RP_SHIFT + i + 1, 0:D] for i in range(2)]

    def norm1(p, _):
        r = rows_of(p)
        u, inverse = unit_of(mt[r, :].astype(F32))
        u1[r, :] = u
        inv1[r, :] = inverse
        n1[r, :] = (u * gain[0] + shift[0]).astype(BF16)
        return 0

    lax.fori_loop(0, NPAIR, norm1, 0)

    bias[...] = jnp.zeros_like(bias)

    def tables(c, _):
        table = jnp.concatenate([small[c, SM_TABLE : SM_TABLE + 4, :], small[c, SM_TABLE + 4 : SM_TABLE + 8, :]], 1)
        table = jnp.concatenate([table, jnp.zeros_like(table)], 0).astype(BF16)
        placed = dot(table, table_sel[...])
        for b_q in range(WIN):
            for h in range(HEADS_C):
                lmat[h * SLOT + b_q : h * SLOT + b_q + 1, :] = placed[h : h + 1, b_q * 128 : b_q * 128 + 128]
        for h in range(HEADS_C):
            tab = lmat[h * SLOT : h * SLOT + SLOT, :]
            lane = iota((SLOT, 128), 1)
            for a in range(WIN):
                moved = pltpu.roll(tab, (128 - (WIN - 1 - a) * SLOT) % 128, 1) if a < WIN - 1 else tab
                low = jnp.where(lane < WIN * SLOT, moved, 0.0)
                both = low + pltpu.roll(low, WIN * SLOT, 1)
                for half in range(2):
                    at = half * WIN * SLOT + a * SLOT
                    bias[c, at : at + SLOT, h * 128 : h * 128 + 128] = both
        return 0

    lmat[...] = jnp.zeros_like(lmat)
    lax.fori_loop(0, CHUNKS, tables, 0)

    def attend(c, _):
        projected = dot(n1[...], qkv_w[c])
        zeros = jnp.zeros((1, CH), F32)
        offset = jnp.concatenate([small[c, SM_QV : SM_QV + 1, :], zeros, small[c, SM_QV + 1 : SM_QV + 2, :]], 1)
        qkv[c] = (projected + offset).astype(BF16)

        def window_pair(p, _):
            r = rows_of(p)
            q, k, v = (qkv[c, r, i * CH : i * CH + CH] for i in range(3))
            s = dot_nt(q, spread(k)) * SCALE + bias[c] + tile4(pair_mask(p, last_chan))
            weights = []
            for h in range(HEADS_C):
                sh = s[:, 128 * h : 128 * h + 128]
                e = jnp.exp(sh - jnp.max(sh, -1, keepdims=True))
                weights.append((e * (1.0 / jnp.sum(e, -1, keepdims=True))).astype(BF16))
            w = jnp.concatenate(weights, 1)
            prob[c, p] = w
            att[c, r, :] = dot(w, spread(v)).astype(BF16)
            return 0

        lax.fori_loop(0, NPAIR, window_pair, 0)
        return 0

    lax.fori_loop(0, CHUNKS, attend, 0)

    def out_proj(j, _):
        tmp[:, 0:D] += dot(att[j], out_w[j])
        return 0

    tmp[:, 0:D] = jnp.zeros((T, D), F32)
    lax.fori_loop(0, CHUNKS, out_proj, 0)
    out_b = jnp.concatenate([small[c, SM_OUT_B : SM_OUT_B + 1, :] for c in range(CHUNKS)], 1)
    down_b = jnp.concatenate([small[c, SM_DOWN_B : SM_DOWN_B + 1, :] for c in range(CHUNKS)], 1)

    def norm2(p, total):
        r = rows_of(p)
        branch = tmp[r, 0:D] + out_b
        resid = mt[r, :].astype(F32) + branch
        r1[r, :] = resid
        u, inverse = unit_of(resid.astype(BF16).astype(F32))
        u2[r, :] = u
        inv2[r, :] = inverse
        n2[r, :] = (u * gain[1] + shift[1]).astype(BF16)
        return total + col_sum(branch * branch * valid)

    sq_one = lax.fori_loop(0, NPAIR, norm2, jnp.zeros((1, D), F32))

    br2[...] = jnp.zeros_like(br2)
    dy2[...] = jnp.zeros_like(dy2)

    def feed(c, _):
        tmp[:, 0:512] = dot(n2[...], up_w[c])
        tmp[:, 512:1024] = dot_nt(g2[...], down_w[c])
        up_b = row_of(small, c, SM_UP_B, 4)

        def gelus(p, total):
            r = rows_of(p)
            value, slope = gelu_parts(tmp[r, 0:512] + up_b)
            hid[r, :] = value.astype(BF16)
            d = slope * tmp[r, 512:1024]
            dpre[r, :] = d.astype(BF16)
            return total + col_sum(d)

        d_up_b = lax.fori_loop(0, NPAIR, gelus, jnp.zeros((1, 512), F32))
        for i in range(4):
            d_small_o[c, SM_UP_B + i : SM_UP_B + i + 1, :] = d_up_b[:, i * 128 : i * 128 + 128]
        br2[...] += dot(hid[...], down_w[c])
        d_down_o[c] = dot_tn(hid[...], g2[...]).astype(BF16)
        d_up_o[c] = dot_tn(n2[...], dpre[...]).astype(BF16)
        dy2[...] += dot_nt(dpre[...], up_w[c])
        return 0

    lax.fori_loop(0, CHUNKS, feed, 0)

    def norm2_back(p, carry):
        sq_two, sq_out, d_down_b, d_gain, d_shift, d_out_b = carry
        r = rows_of(p)
        branch = br2[r, :] + down_b
        result = r1[r, :] + branch
        r1[r, :] = result
        u = u2[r, :]
        dy = dy2[r, :]
        g = g2[r, :].astype(F32)
        grad = g + norm_back(dy, u, inv2[r, :], gain[1])
        g1f[r, :] = grad
        g1[r, :] = grad.astype(BF16)
        return (
            sq_two + col_sum(branch * branch * valid),
            sq_out + col_sum(result * result * valid),
            d_down_b + col_sum(g),
            d_gain + col_sum(dy * u),
            d_shift + col_sum(dy),
            d_out_b + col_sum(grad),
        )

    start = (jnp.zeros((1, D), F32),) * 6
    sq_two, sq_out, d_down_b, d_gain1, d_shift1, d_out_b = lax.fori_loop(0, NPAIR, norm2_back, start)
    for c in range(CHUNKS):
        d_small_o[c, SM_DOWN_B : SM_DOWN_B + 1, :] = d_down_b[:, c * CH : c * CH + CH]
        d_small_o[c, SM_OUT_B : SM_OUT_B + 1, :] = d_out_b[:, c * CH : c * CH + CH]
    squares_o[...] = jnp.zeros_like(squares_o)
    for i, sq in enumerate((sq_out, sq_one, sq_two)):
        squares_o[i : i + 1, :] = sq

    def block_rows(i, _):
        base = (i // WIN) * BAND + (i % WIN) * SLOT
        parts = [r1[pl.ds(pl.multiple_of(base + wc * WIN * SLOT, SLOT), SLOT), :] for wc in range(WC)]
        block_o[i] = dot(token_sel_t[...], jnp.concatenate(parts, 0).astype(BF16)).astype(BF16)
        return 0

    lax.fori_loop(0, ROWS, block_rows, 0)

    dy1[...] = jnp.zeros_like(dy1)

    def attend_back(c, _):
        d_out_o[c] = dot_tn(att[c], g1[...]).astype(BF16)
        hid[:, 0:CH] = dot_nt(g1[...], out_w[c]).astype(BF16)
        gsum[...] = jnp.zeros_like(gsum)

        def window_pair(p, _):
            r = rows_of(p)
            q, k, v = (qkv[c, r, i * CH : i * CH + CH] for i in range(3))
            d_att = hid[r, 0:CH]
            w = prob[c, p]
            d_w = dot_nt(d_att, spread(v))
            d_s = []
            for h in range(HEADS_C):
                wh = w[:, 128 * h : 128 * h + 128].astype(F32)
                gh = d_w[:, 128 * h : 128 * h + 128]
                d_s.append(wh * (gh - jnp.sum(gh * wh, -1, keepdims=True)))
            d_s = jnp.concatenate(d_s, 1)
            gsum[...] += d_s
            d_s = d_s.astype(BF16)
            d_q = dot(d_s, spread(k)) * SCALE
            d_k = dot_tn(by_head(d_s), stacked(q))[0:PAIR] * SCALE
            d_v = dot_tn(by_head(w), stacked(d_att))[0:PAIR]
            dqkv[r, :] = jnp.concatenate([d_q, d_k, d_v], 1).astype(BF16)
            return 0

        lax.fori_loop(0, NPAIR, window_pair, 0)
        d_qkv_o[c] = dot_tn(n1[...], dqkv[...]).astype(BF16)
        dy1[...] += dot_nt(dqkv[...], qkv_w[c])

        def sums(p, total):
            return total + col_sum(dqkv[rows_of(p), :].astype(F32))

        total = lax.fori_loop(0, NPAIR, sums, jnp.zeros((1, 3 * CH), F32))
        d_small_o[c, SM_QV : SM_QV + 1, :] = total[:, 0:CH]
        d_small_o[c, SM_QV + 1 : SM_QV + 2, :] = total[:, 2 * CH : 3 * CH]

        half = WIN * SLOT
        for h in range(HEADS_C):
            lanes = slice(h * 128, h * 128 + 128)
            folded = gsum[0:half, lanes] + pltpu.roll(gsum[half:PAIR, lanes], 128 - half, 1)
            acc = jnp.zeros((SLOT, 128), F32)
            for a in range(WIN):
                slab = folded[a * SLOT : a * SLOT + SLOT]
                moved = (WIN - 1 - a) * SLOT
                acc += pltpu.roll(slab, moved, 1) if moved else slab
            lmat[h * SLOT : h * SLOT + SLOT, :] = acc
        d_table = jnp.zeros((SLOT, 256), F32)
        for b_q in range(WIN):
            rows = [lmat[h * SLOT + b_q : h * SLOT + b_q + 1, :] for h in range(HEADS_C)]
            rows = jnp.concatenate(rows + [jnp.zeros((SLOT - HEADS_C, 128), F32)], 0)
            d_table += dot_nt(rows.astype(BF16), table_sel[:, b_q * 128 : b_q * 128 + 128])
        d_small_o[c, SM_TABLE : SM_TABLE + 4, :] = d_table[0:4, 0:128]
        d_small_o[c, SM_TABLE + 4 : SM_TABLE + 8, :] = d_table[0:4, 128:256]
        return 0

    lax.fori_loop(0, CHUNKS, attend_back, 0)

    def norm1_back(p, carry):
        d_gain, d_shift = carry
        r = rows_of(p)
        u = u1[r, :]
        dy = dy1[r, :]
        gz[r, :] = (g1f[r, :] + norm_back(dy, u, inv1[r, :], gain[0])).astype(BF16)
        return d_gain + col_sum(dy * u), d_shift + col_sum(dy)

    d_gain0, d_shift0 = lax.fori_loop(0, NPAIR, norm1_back, start[:2])

    d_merge_o[...] = dot_tn(mn[...], gz[...]).astype(BF16)
    tmp[...] = dot_nt(gz[...], merge_w[...])

    def norm0_back(p, carry):
        d_gain, d_shift = carry
        r = rows_of(p)
        u = x0[r, :]
        dy = tmp[r, :]
        tmp[r, :] = norm_back(dy, u, inv0[r, :], repl[RP_GAIN0 : RP_GAIN0 + 1, :])
        return d_gain + col_sum(dy * u), d_shift + col_sum(dy)

    start0 = (jnp.zeros((1, 1024), F32),) * 2
    d_gain_m, d_shift_m = lax.fori_loop(0, NPAIR, norm0_back, start0)
    d_repl_o[0:1, :] = d_gain_m
    d_repl_o[1:2, :] = d_shift_m
    d_repl_o[2:3, :] = jnp.concatenate([d_gain0, d_gain1], 1)
    d_repl_o[3:4, :] = jnp.concatenate([d_shift0, d_shift1], 1)
    d_repl_o[4:8, :] = jnp.zeros((4, 1024), F32)

    def page_rows(i, _):
        base = (i // WIN) * BAND + (i % WIN) * SLOT
        for q in range(2):
            parts = []
            for par in range(2):
                lanes = par * 512 + q * 256
                for wc in range(WC):
                    at = pl.multiple_of(base + wc * WIN * SLOT, SLOT)
                    parts.append(tmp[pl.ds(at, SLOT), lanes : lanes + 256])
            pages_o[2 * i + q] = dot(pages_sel_t[...], jnp.concatenate(parts, 0).astype(BF16))
        return 0

    lax.fori_loop(0, ROWS, page_rows, 0)


def kernel_call(args):
    vm = pl.BlockSpec(memory_space=pltpu.VMEM)
    s = jax.ShapeDtypeStruct
    outs = [
        s((ROWS, COLS, D), BF16),
        s((2 * ROWS, 2 * COLS, 256), F32),
        s((1024, D), BF16),
        s((CHUNKS, D, 3 * CH), BF16),
        s((CHUNKS, CH, D), BF16),
        s((CHUNKS, D, 512), BF16),
        s((CHUNKS, 512, D), BF16),
        s((CHUNKS, 16, 128), F32),
        s((8, 1024), F32),
        s((8, D), F32),
    ]
    v = pltpu.VMEM
    scratch = [
        v((T, 1024), F32), v((T, 1), F32), v((T, 1024), BF16), v((T, D), BF16),
        v((T, D), F32), v((T, 1), F32), v((T, D), BF16),
        v((CHUNKS, T, 3 * CH), BF16), v((CHUNKS, NPAIR, PAIR, 512), BF16), v((CHUNKS, T, CH), BF16),
        v((T, D), F32), v((T, D), F32), v((T, 1), F32), v((T, D), BF16), v((T, D), BF16),
        v((T, D), F32), v((T, D), F32),
        v((8, 128), F32), v((T, 512), BF16), v((T, 512), BF16),
        v((CHUNKS, PAIR, 512), F32), v((HEADS_C * SLOT, 128), F32), v((PAIR, 512), F32),
        v((T, 3 * CH), BF16), v((T, D), F32), v((T, D), BF16), v((T, D), F32), v((T, D), BF16),
        v((T, 1024), F32),
    ]
    return pl.pallas_call(
        compute,
        out_shape=outs,
        in_specs=[vm] * len(args),
        out_specs=[vm] * len(outs),
        scratch_shapes=scratch,
        compiler_params=pltpu.CompilerParams(vmem_limit_bytes=60 * 1024 * 1024),
    )(*args)


def shifted(shard, axis, by):
    count = lax.axis_size(axis)
    return lax.ppermute(shard, axis, [(i, (i + by) % count) for i in range(count)])


def pack_small(qv_bias, rel_table, out_bias, up_bias, down_bias):
    table = jnp.pad(rel_table, ((0, 0), (0, 256 - rel_table.shape[1])))
    parts = [qv_bias, table[:, :128], table[:, 128:], out_bias[None], up_bias.reshape(4, 128), down_bias[None]]
    return jnp.concatenate(parts, 0).astype(F32)


def body(
    pages, merge_gain, merge_shift, merge_weight, norm_gain, norm_shift, qkv_weight, qv_bias, rel_table,
    out_weight, out_bias, up_weight, up_bias, down_weight, down_bias, cotangent,
):
    small = pack_small(qv_bias, rel_table, out_bias, up_bias, down_bias)
    repl = jnp.concatenate(
        [merge_gain[None], merge_shift[None], jnp.pad(norm_gain, ((0, 0), (0, 512))), jnp.pad(norm_shift, ((0, 0), (0, 512)))], 0
    ).astype(F32)
    repl = jnp.pad(repl, ((0, 2), (0, 0)))
    gather = functools.partial(lax.all_gather, axis_name="chan", axis=0, tiled=False)
    pages_ext = jnp.concatenate([pages, shifted(pages[:LIFT], ("space", "chan"), -1)], 0)
    cot_ext = jnp.concatenate([cotangent[SHIFT:], shifted(cotangent[:SHIFT], "space", -1)], 0)
    cot = lax.all_to_all(cot_ext.reshape(CHUNKS, ROWS, COLS, CH), "chan", split_axis=0, concat_axis=0, tiled=True)
    args = [
        pages_ext, cot, merge_weight, gather(qkv_weight.reshape(D, 3 * CH)), gather(out_weight),
        gather(up_weight), gather(down_weight), gather(small), repl, *constants(),
    ]
    block, grad_pages, d_merge, d_qkv, d_out, d_up, d_down, d_small, d_repl, squares = kernel_call(args)
    block = lax.all_to_all(block, "chan", split_axis=2, concat_axis=0, tiled=True)
    block = jnp.concatenate([shifted(block[-SHIFT:], "space", 1), block[:-SHIFT]], 0).astype(F32)
    grad_pages = jnp.concatenate(
        [shifted(grad_pages[-LIFT:].astype(BF16), ("space", "chan"), 1).astype(F32), grad_pages[:-LIFT]], 0
    )

    def reduced(chunked):
        mine = lax.psum_scatter(chunked, "chan", scatter_dimension=0, tiled=False)
        return lax.psum(mine, "space").astype(F32)

    d_merge, d_repl, squares, d_small = lax.psum((d_merge, d_repl, squares, d_small), ("space", "chan"))
    d_small = lax.dynamic_index_in_dim(d_small, lax.axis_index("chan"), 0, keepdims=False)
    rms = jnp.sqrt(jnp.sum(squares[:3], 1) / float(1792 * COLS * D))
    table = jnp.concatenate([d_small[2:6], d_small[6:10]], 1)[:, :169]
    return (
        block, grad_pages, d_repl[0], d_repl[1], d_merge.astype(F32),
        d_repl[2].reshape(2, D), d_repl[3].reshape(2, D),
        reduced(d_qkv).reshape(D, 3, CH), d_small[0:2], table, reduced(d_out), d_small[10],
        reduced(d_up), d_small[11:15].reshape(512), reduced(d_down), d_small[15], rms,
    )


def solution(mesh):
    placed = (
        P(("space", "chan"), None, None), P(), P(), P(), P(), P(), P(None, None, "chan"), P(None, "chan"),
        P("chan", None), P("chan", None), P("chan"), P(None, "chan"), P("chan"), P("chan", None), P("chan"),
        P("space", None, "chan"),
    )
    outs = (
        P("space", None, "chan"), P(("space", "chan"), None, None), P(), P(), P(), P(), P(),
        P(None, None, "chan"), P(None, "chan"), P("chan", None), P("chan", None), P("chan"),
        P(None, "chan"), P("chan"), P("chan", None), P("chan"), P(),
    )
    return jax.shard_map(body, mesh=mesh, in_specs=placed, out_specs=outs, check_vma=False)
```

time: 877 us -> 726 us (0.83); the launches traced: 866 us -> 725 us
  waiting for transfers between devices: 326 us -> 531 us
  local copies, waits for them, and re-layouts: 193 us -> 26.7 us
  blocking collectives: 147 us -> 33 us
  matrix products: 84.2 us -> 0 us
  Pallas kernels: 0 us -> 83.2 us
  other arithmetic: 86.5 us -> 15.6 us
    psum x4 -> x3, waiting for transfers between devices: 192 us -> 366 us  [the longest x2 260 us: body(): lax.psum((d_merge, d_repl, squares, d_small), ('space', 'chan'))]
    psum x2 -> x0, blocking collectives: 131 us -> none  [the longest x1 66.9 us: body(): lax.psum((merge_weight_grad, merge_gain_grad, merge_shift_grad, jnp.stack...]
    reduce_scatter x0 -> x4, waiting for transfers between devices: none -> 108 us  [reduced(): mine = lax.psum_scatter(chunked, 'chan', scatter_dimension=0, tiled=False)]
    dot_general x23 -> x0, matrix products: 84.2 us -> none  [the longest x1 15.8 us: body(): jnp.einsum('td,fd->tf', grad_two_full, down_weight, preferred_element_typ...]
    pallas_call x0 -> x1, Pallas kernels: none -> 83.2 us  [kernel_call(): pl.pallas_call(compute, out_shape=outs, in_specs=[vm] * len(args), out_sp...]
    another operation x24 -> x3, local copies, waits for them, and re-layouts: 51.3 us -> 2.12 us  [the longest x1 0.92 us: body(): gather(qkv_weight.reshape(D, 3 * CH))]
    all_gather x4 -> x3, waiting for transfers between devices: 95.3 us -> 51 us  [the longest x1 31 us: body(): gather(down_weight)]
    reduce_sum x16 -> x1, other arithmetic: 42 us -> 0.12 us  [body(): rms = jnp.sqrt(jnp.sum(squares[:3], 1) / float(1792 * COLS * D))]
  transfers between devices with their start and end apart: 15 -> 16, of which waited for: 12 -> 10; matrix products, arithmetic and copies ran while one was open for 21% -> 5% of each run, Pallas kernels for 0% -> 0%
where the time goes in v1:
time: 726 us; the launch traced here: 725 us
  waiting for transfers between devices  531 us (73%)
  Pallas kernels  83.2 us (11%)
  blocking collectives  33 us (5%)
  local copies, waits for them, and re-layouts  26.7 us (4%)
  starting transfers between devices  21.2 us (3%)
  other arithmetic  15.6 us (2%)
  between operations  14.5 us (2%)
    psum x2, waiting for transfers between devices, body(): lax.psum((d_merge, d_repl, squares, d_small), ('space', 'chan'))  260 us
    reduce_scatter x4, waiting for transfers between devices, reduced(): mine = lax.psum_scatter(chunked, 'chan', scatter_dimension=0, tiled=False)  108 us
    psum x1, waiting for transfers between devices, reduced(): return lax.psum(mine, 'space').astype(F32)  107 us
    pallas_call x1, Pallas kernels, kernel_call(): pl.pallas_call(compute, out_shape=outs, in_specs=[vm] * len(args), out_sp...  83.2 us
    all_gather x1, waiting for transfers between devices, body(): gather(down_weight)  31 us
    all_gather x1, blocking collectives, body(): gather(small)  21.3 us
    all_gather x1, waiting for transfers between devices, body(): gather(up_weight)  20 us
  transfers between devices with their start and end apart: 16, of which 10 were waited for; matrix products, arithmetic and copies ran while one was open for 5% of the time, Pallas kernels for 0%

profile of v1, /device:TPU:1, one launch (start us, length us, event | category | flops | bytes accessed | tf_op | source)
XLA Modules:
  0.0 724.8 jit_solution(13345862849259697895)
XLA Ops:
  7.2 1.3 copy.49
  11.1 4.2 collective-permute-start
  15.3 5.6 collective-permute-start.1
  22.8 3.5 all-to-all-start
  27.1 21.3 %all_gather.32.small = f32[4,16,128]{2,1,0:T(8,128)} all-gather(f32[1,16,128]{2,1,0:T(8,128)S(1)} %convert_element_type.38), channel_id=1, replica_groups=mesh['space'=32,'chan'=4] {'chan'}, dimensions={0}, use_global_device_ids=true | all-gather | bytes 40960 | tf_op jit(solution)/shard_map/all_gather | solution.py:506
  48.4 11.7 %all-gather = bf16[512,512]{1,0:T(8,128)(2,1)} all-gather(bf16[128,512]{1,0:T(8,128)(2,1)S(1)} %copy-done.7), channel_id=2, replica_groups=mesh['space'=32,'chan'=4] {'chan'}, dimensions={0}, use_global_device_ids=true | all-gather | bytes 655360 | tf_op jit(solution)/shard_map/all_gather | solution.py:505
  60.2 1.3 pad_maximum_fusion.1.pages
  61.5 20.0 %all-gather.9.cloned.1.call-done = bf16[2048,512]{1,0:T(8,128)(2,1)} async-done(((bf16[512,512]{1,0:T(8,128)(2,1)}), bf16[2048,512]{1,0:T(8,128)(2,1)}) %all-gather.9.cloned.1.call-update) | async-done | bytes 2097168 | tf_op jit(solution)/shard_map/all_gather | solution.py:506
  81.4 31.0 %all-gather.11.cloned.1.call-done = bf16[2048,512]{1,0:T(8,128)(2,1)} async-done(((bf16[512,512]{1,0:T(8,128)(2,1)}), bf16[2048,512]{1,0:T(8,128)(2,1)}) %all-gather.11.cloned.1.call-update) | async-done | bytes 2097168 | tf_op jit(solution)/shard_map/all_gather | solution.py:506
  112.4 83.2 %shard_map.332 = (bf16[14,42,512]{2,1,0:T(8,128)(2,1)}, f32[28,84,256]{2,1,0:T(8,128)}, bf16[1024,512]{1,0:T(8,128)(2,1)}, bf16[4,512,384]{2,1,0:T(8,128)(2,1)},...) custom-call(bf16[34,84,256]{2,1,0:T(8,128)(2,1)} %pad_maximum_fusion, ...), custom_call_target="tpu_custom_call" | custom-call | tf_op jit(solution)/shard_map/pallas_call | solution.py:470
  199.3 1.4 slice.85
  201.3 2.1 copy.51
  203.4 3.8 reshape.160
  207.2 5.3 all-to-all-start.1
  212.5 124.4 %all-reduce.12.cloned.1.call-done = (f32[8,1024]{1,0:T(8,128)}, f32[4,16,128]{2,1,0:T(8,128)}, f32[8,512]{1,0:T(8,128)}) async-done(((f32[8,1024]{1,0:T(8,128)}, f32[4,16,128]{2,1,0:T(8,128)}, f32[8,512]{1,0:T(8,128)}), (f32[8,1024]{1,0:T(8,128)}, f32[4,16,128]{2,1,0:T(8,128)}, f32[8,512]{1,0:T(8,128)})) %all-reduce.12.cloned.1.call-update) | async-done | bytes 81936 | tf_op jit(solution)/shard_map/psum | solution.py:519
  336.8 1.3 dynamic-slice_bitcast_fusion
  338.7 1.5 slice_reduce_fusion.1
  340.3 20.5 %reduce-scatter.5.cloned.1.call-done = bf16[1,512,384]{2,1,0:T(8,128)(2,1)} async-done(((bf16[4,512,384]{2,1,0:T(8,128)(2,1)}), bf16[1,512,384]{2,1,0:T(8,128)(2,1)}) %reduce-scatter.5.cloned.1.call-update) | async-done | bytes 393232 | tf_op jit(solution)/shard_map/reduce_scatter | solution.py:516
  360.7 1.9 copy.53
  362.7 21.6 %reduce-scatter.7.cloned.1.call-done = bf16[1,128,512]{2,1,0:T(8,128)(2,1)} async-done(((bf16[4,128,512]{2,1,0:T(8,128)(2,1)}), bf16[1,128,512]{2,1,0:T(8,128)(2,1)}) %reduce-scatter.7.cloned.1.call-update) | async-done | bytes 131088 | tf_op jit(solution)/shard_map/reduce_scatter | solution.py:516
  384.2 34.3 %reduce-scatter.9.cloned.1.call-done = bf16[1,512,512]{2,1,0:T(8,128)(2,1)} async-done(((bf16[4,512,512]{2,1,0:T(8,128)(2,1)}), bf16[1,512,512]{2,1,0:T(8,128)(2,1)}) %reduce-scatter.9.cloned.1.call-update) | async-done | bytes 524304 | tf_op jit(solution)/shard_map/reduce_scatter | solution.py:516
  418.5 31.8 %reduce-scatter.11.cloned.1.call-done = bf16[1,512,512]{2,1,0:T(8,128)(2,1)} async-done(((bf16[4,512,512]{2,1,0:T(8,128)(2,1)}), bf16[1,512,512]{2,1,0:T(8,128)(2,1)}) %reduce-scatter.11.cloned.1.call-update) | async-done | bytes 524304 | tf_op jit(solution)/shard_map/reduce_scatter | solution.py:516
  450.4 1.3 fusion.5
  451.7 1.3 fusion.7
  455.7 3.3 reshape.161
  459.0 2.4 copy.52
  461.7 1.9 collective-permute-start.2
  463.5 3.3 pad_maximum_fusion
  468.0 135.4 %all-reduce.10.cloned.1.call-done = bf16[1024,512]{1,0:T(8,128)(2,1)} async-done(((bf16[1024,512]{1,0:T(8,128)(2,1)}), bf16[1024,512]{1,0:T(8,128)(2,1)}) %all-reduce.10.cloned.1.call-update) | async-done | bytes 1048592 | tf_op jit(solution)/shard_map/psum | solution.py:519
  603.4 2.8 convert_element_type.41
  606.3 106.5 %all-reduce.14.cloned.1.call-done = (bf16[512,3,128]{0,2,1:T(8,128)(2,1)}, bf16[128,512]{1,0:T(8,128)(2,1)}, bf16[512,512]{1,0:T(8,128)(2,1)}, bf16[512,512]{1,0:T(8,128)(2,1)}) async-done(((bf16[512,3,128]{0,2,1:T(8,128)(2,1)}, bf16[128,512]{1,0:T(8,128)(2,1)}, bf16[512,512]{1,0:T(8,128)(2,1)}, bf16[512,512]{1,0:T(8,128)(2,1)}), (bf16[512,3,128]{0,2,1:T(8,128)(2,1)}, bf16[128,512]{1,0:T(8,128)(2,1)}, ...) | async-done | bytes 1572880 | tf_op jit(solution)/shard_map/psum | solution.py:517
  712.8 2.2 convert_element_type.43
  (92 shorter events, 17.1 us)
Async XLA Ops:
  7.2 3.8 copy-start.2
  7.2 54.3 %all-gather.7.cloned.1.call-start = ((), (), s32[]{:S(2)}) async-start(), calls=%async_computation.6 | async-start | bytes 1966080 | tf_op jit(solution)/shard_map/all_gather | solution.py:505
  8.5 6.7 copy-start.3
  8.5 12.3 %copy-start.13 = (bf16[1024]{0:T(1024)(128)(2,1)S(1)}, bf16[1024]{0:T(1024)(128)(2,1)}, u32[]{:S(2)}) copy-start(bf16[1024]{0:T(1024)(128)(2,1)} %param.22) | copy-start | bytes 6148
  8.5 12.3 %copy-start.14 = (bf16[1024]{0:T(1024)(128)(2,1)S(1)}, bf16[1024]{0:T(1024)(128)(2,1)}, u32[]{:S(2)}) copy-start(bf16[1024]{0:T(1024)(128)(2,1)} %param.23) | copy-start | bytes 6148
  8.5 12.3 %copy-start.9 = (bf16[4,169]{1,0:T(4,128)(2,1)S(1)}, bf16[4,169]{1,0:T(4,128)(2,1)}, u32[]{:S(2)}) copy-start(bf16[4,169]{1,0:T(4,128)(2,1)} %param.29) | copy-start | bytes 4060
  8.6 12.3 %copy-start.11 = (bf16[2,512]{1,0:T(2,128)(2,1)S(1)}, bf16[2,512]{1,0:T(2,128)(2,1)}, u32[]{:S(2)}) copy-start(bf16[2,512]{1,0:T(2,128)(2,1)} %param.26) | copy-start | bytes 6148
  8.6 12.3 %copy-start.12 = (bf16[2,512]{1,0:T(2,128)(2,1)S(1)}, bf16[2,512]{1,0:T(2,128)(2,1)}, u32[]{:S(2)}) copy-start(bf16[2,512]{1,0:T(2,128)(2,1)} %param.25) | copy-start | bytes 6148
  9.5 71.9 %all-gather.9.cloned.1.call-start = ((), (), s32[]{:S(2)}) async-start(), calls=%async_computation.12 | async-start | bytes 2621440 | tf_op jit(solution)/shard_map/all_gather | solution.py:506
  10.3 102.1 %all-gather.11.cloned.1.call-start = ((), (), s32[]{:S(2)}) async-start(), calls=%async_computation.13 | async-start | bytes 2621440 | tf_op jit(solution)/shard_map/all_gather | solution.py:506
  11.1 49.1 %collective-permute-start = (bf16[6,84,256]{2,1,0:T(8,128)(2,1)S(1)}, bf16[6,84,256]{2,1,0:T(8,128)(2,1)S(1)}, u32[]{:S(2)}, u32[]{:S(2)}) collective-permute-start(bf16[6,84,256]{2,1,0:T(8,128)(2,1)S(1)} %slice.77), channel_id=1, source_target_pairs={{0,127},{1,0},{2,1},{3,2},{4,3},{5,4},{6,5},{7,6},{8,7},{9,8},{10,... | collective-permute-start | bytes 774152 | tf_op jit(solution)/shard_map/ppermute | solution.py:482
  15.3 6.4 collective-permute-start.1
  21.8 5.2 copy-start.15
  21.8 5.2 copy-start.16
  21.8 5.2 copy-start.17
  21.8 5.1 copy-start.18
  21.8 26.6 %copy-start.7 = (bf16[128,512]{1,0:T(8,128)(2,1)S(1)}, bf16[128,512]{1,0:T(8,128)(2,1)}, u32[]{:S(2)}) copy-start(bf16[128,512]{1,0:T(8,128)(2,1)} %param.30) | copy-start | bytes 393220
  22.8 38.7 %all-to-all-start = ((bf16[4,14,42,128]{3,2,1,0:T(8,128)(2,1)}), bf16[4,14,42,128]{3,2,1,0:T(8,128)(2,1)S(1)}, u32[]{:S(2)}, u32[]{:S(2)}) async-start(bf16[4,14,42,128]{3,2,1,0:T(8,128)(2,1)} %bitcast), calls=%async_computation | async-start | bytes 1376256 | tf_op jit(solution)/shard_map/all_to_all | solution.py:503
  26.3 310.5 %all-reduce.12.cloned.1.call-start = ((), (), s32[]{:S(2)}) async-start(), calls=%async_computation.14 | async-start | bytes 163840 | tf_op jit(solution)/shard_map/psum | solution.py:519
  61.5 51.0 %copy-start = (bf16[4,14,42,128]{3,2,1,0:T(8,128)(2,1)}, bf16[4,14,42,128]{3,2,1,0:T(8,128)(2,1)S(1)}, u32[]{:S(2)}) copy-start(bf16[4,14,42,128]{3,2,1,0:T(8,128)(2,1)S(1)} %all-to-all-done.cot) | copy-start | bytes 1806340
  195.7 165.1 %reduce-scatter.5.cloned.1.call-start = ((), (), s32[]{:S(2)}) async-start(), calls=%async_computation.8 | async-start | bytes 1966080 | tf_op jit(solution)/shard_map/reduce_scatter | solution.py:516
  196.3 188.0 %reduce-scatter.7.cloned.1.call-start = ((), (), s32[]{:S(2)}) async-start(), calls=%async_computation.9 | async-start | bytes 655360 | tf_op jit(solution)/shard_map/reduce_scatter | solution.py:516
  196.8 221.7 %reduce-scatter.9.cloned.1.call-start = ((), (), s32[]{:S(2)}) async-start(), calls=%async_computation.10 | async-start | bytes 2621440 | tf_op jit(solution)/shard_map/reduce_scatter | solution.py:516
  197.6 252.8 %reduce-scatter.11.cloned.1.call-start = ((), (), s32[]{:S(2)}) async-start(), calls=%async_computation.11 | async-start | bytes 2621440 | tf_op jit(solution)/shard_map/reduce_scatter | solution.py:516
  198.3 405.1 %all-reduce.10.cloned.1.call-start = ((), (), s32[]{:S(2)}) async-start(), calls=%async_computation.7 | async-start | bytes 2097152 | tf_op jit(solution)/shard_map/psum | solution.py:519
  200.8 254.0 %collective-permute-start.3 = (bf16[6,84,256]{2,1,0:T(8,128)(2,1)S(1)}, bf16[6,84,256]{2,1,0:T(8,128)(2,1)}, u32[]{:S(2)}, u32[]{:S(2)}) collective-permute-start(bf16[6,84,256]{2,1,0:T(8,128)(2,1)S(1)} %slice.117), channel_id=1, source_target_pairs={{0,1},{1,2},{2,3},{3,4},{4,5},{5,6},{6,7},{7,8},{8,9},{9,10},{10,1... | collective-permute-start | bytes 774152 | tf_op jit(solution)/shard_map/ppermute | solution.py:482
  207.2 248.6 %all-to-all-start.1 = ((bf16[4,2,37632]{2,1,0:T(2,128)(2,1)}), bf16[4,2,37632]{2,1,0:T(2,128)(2,1)S(1)}, u32[]{:S(2)}, u32[]{:S(2)}) async-start(bf16[4,2,37632]{2,1,0:T(2,128)(2,1)} %reshape.160), calls=%async_computation.1 | async-start | bytes 1204224 | tf_op jit(solution)/shard_map/all_to_all | solution.py:509
  212.5 500.4 %all-reduce.14.cloned.1.call-start = ((), (), s32[]{:S(2)}) async-start(), calls=%async_computation.15 | async-start | bytes 3145728 | tf_op jit(solution)/shard_map/psum | solution.py:517
  336.8 114.8 %copy-start.10 = (f32[8,512]{1,0:T(8,128)S(1)}, f32[8,512]{1,0:T(8,128)}, u32[]{:S(2)}) copy-start(f32[8,512]{1,0:T(8,128)} %get-tuple-element.75) | copy-start | bytes 49156
  461.7 5.1 collective-permute-start.2
  712.8 2.2 copy-start.5
  712.8 3.3 copy-start.6
  (3 other events, 5.8 us)
Sparse Core Ops, SparseCore 0:
  10.3 36.8 all-gather.6
  48.8 32.6 all-gather.8
  83.1 29.2 all-gather.10
  195.8 140.9 all-reduce.11
  339.2 21.4 reduce-scatter.4
  363.7 20.5 reduce-scatter.6
  387.3 31.1 reduce-scatter.8
  420.9 29.3 reduce-scatter.10
  456.4 146.9 all-reduce.9
  607.6 105.2 all-reduce.13

commit v2 on v1

--- a/solution.py
+++ b/solution.py
@@ -147,19 +147,173 @@
     return jnp.concatenate([ref[c, first + i : first + i + 1, :] for i in range(count)], 1)
 
 
+MESH = pl.DeviceIdType.MESH
+HALF = 256
+PEERS = CHUNKS - 1
+
+
+class Sems:
+    def __init__(self):
+        self.count = 0
+
+    def take(self, n):
+        self.count += n
+        return self.count - n
+
+
+IDS = Sems()
+ID_PAGES = IDS.take(1)
+ID_SMALL = IDS.take(PEERS)
+ID_W = IDS.take(4 * PEERS)
+ID_WF = IDS.take(4 * PEERS)
+ID_COT_HALO = IDS.take(1)
+ID_COT = IDS.take(PEERS)
+ID_BLK = IDS.take(PEERS)
+ID_BLK_HALO = IDS.take(1)
+ID_CORE = IDS.take(4 * CHUNKS)
+ID_CORE_M = IDS.take(1)
+ID_Y = IDS.take(4 * PEERS)
+ID_Y_M = IDS.take(PEERS)
+ID_RZ = IDS.take(2 * PEERS)
+ID_RX = IDS.take(2 * PEERS)
+ID_GX = IDS.take(2 * PEERS)
+ID_GZ = IDS.take(2 * PEERS)
+ID_GC = IDS.take(2)
+ID_GY_M = IDS.take(PEERS)
+ID_GC_M = IDS.take(1)
+ID_PG = IDS.take(1)
+ID_SG_C = IDS.take(1)
+ID_SG_Y = IDS.take(PEERS)
+ID_SG_Z = IDS.take(PEERS)
+ID_SG_X = IDS.take(PEERS)
+LOCAL = 16
+QKV, OUT, UP, DOWN = 0, 1, 2, 3
+
+SG_CHUNK, SG_REPL, SG_SQ, SG_ROWS = 0, 64, 96, 104
+
+
+def chunk_off(j):
+    return lax.rem(3 * j, 5) - 2 * (j // 3)
+
+
+def back_off(j):
+    return lax.rem(j + 1, CHUNKS)
+
+
 def compute(
-    pages, cot, merge_w, qkv_w, out_w, up_w, down_w, small, repl,
+    pages_in, cot_in, merge_in, qkv_in, out_in, up_in, down_in, small_in, repl,
     pages_sel, pages_sel_t, token_sel, token_sel_t, table_sel,
-    block_o, pages_o, d_merge_o, d_qkv_o, d_out_o, d_up_o, d_down_o, d_small_o, d_repl_o, squares_o,
-    x0, inv0, mn, mt, u1, inv1, n1, qkv, prob, att, r1, u2, inv2, n2, g2, br2, dy2,
-    gelu_d, hid, dpre, bias, lmat, gsum, dqkv, dy1, g1, g1f, gz, tmp,
+    block_o, pages_o, mlp_o, attn_o, merge_o, small_o,
+    pages, cot_v, cot, merge_w, qkv_w, out_w, up_w, down_w, small,
+    x0, inv0, mn, mt, n1, qkv, prob, att, r1, u2, inv2, n2, g2, br2, dy2,
+    hid, dpre, bias, lmat, gsum, dqkv, g1, gz, tmp,
+    blk_tx, blk_rx, pg,
+    d_merge, d_qkv, d_out, d_up, d_down, d_small, d_repl,
+    l1_qkv, l1_out, l1_up, l1_down, l1_m, l2_qkv, l2_out, l2_up, l2_down, l2_m,
+    ga, rza, hza, rxa, gfa, gb, rzb, hzb, rxb, gfb, mf,
+    sg, sg_c, sg_y, sg_z, sg_x,
+    ssem, rsem, lsem,
 ):
     chan = lax.axis_index("chan")
+    space = lax.axis_index("space")
+    n_space = lax.axis_size("space")
+    core = lax.rem(space, 2)
+    z = lax.rem(space // 2, 4)
+    x = space // 8
     last_chan = chan == CHUNKS - 1
     valid = (iota((PAIR, 1), 0) % SLOT < WIN).astype(F32)
 
+    def at_y(d):
+        return (space, lax.rem(chan + d, CHUNKS))
+
+    def at_z(d):
+        return (x * 8 + lax.rem(z + d, 4) * 2 + core, chan)
+
+    def at_x(d):
+        return (lax.rem(x + d, 4) * 8 + z * 2 + core, chan)
+
+    sibling = (x * 8 + z * 2 + 1 - core, chan)
+    up_band = (lax.rem(space + n_space - 1, n_space), chan)
+    down_band = (lax.rem(space + 1, n_space), chan)
+    rank = space * CHUNKS + chan
+    n_rank = n_space * CHUNKS
+    before = lax.rem(rank + n_rank - 1, n_rank)
+    after = lax.rem(rank + 1, n_rank)
+    up_rank = (before // CHUNKS, lax.rem(before, CHUNKS))
+    down_rank = (after // CHUNKS, lax.rem(after, CHUNKS))
+
+    def send(src, dst, n, device):
+        return pltpu.make_async_remote_copy(
+            src_ref=src, dst_ref=dst, send_sem=ssem.at[n], recv_sem=rsem.at[n], device_id=device, device_id_type=MESH
+        )
+
+    def local(src, dst, n):
+        return pltpu.make_async_copy(src, dst, lsem.at[n])
+
+    own_pages = local(pages_in, pages.at[pl.ds(0, 2 * ROWS)], 0)
+    own_merge = local(merge_in, merge_w, 1)
+    own_w = [
+        local(src, dst.at[chan], 2 + i)
+        for i, (src, dst) in enumerate(((qkv_in, qkv_w), (out_in, out_w), (up_in, up_w), (down_in, down_w)))
+    ]
+    own_small = local(small_in, small.at[chan], 6)
+    own_cot = local(cot_in, cot_v.at[pl.ds(0, 4 * ROWS)], 7)
+    for copy in (own_pages, own_merge, own_small, own_w[QKV], own_w[OUT], own_cot, own_w[UP], own_w[DOWN]):
+        copy.start()
+
+    barrier = pltpu.get_barrier_semaphore()
+    greeted = [at_y(d) for d in (1, 2, 3)] + [at_z(d) for d in (1, 2, 3)] + [at_x(d) for d in (1, 2, 3)]
+    greeted += [sibling, up_band, down_band, up_rank, down_rank]
+    for device in greeted:
+        pl.semaphore_signal(barrier, inc=1, device_id=device, device_id_type=MESH)
+    pl.semaphore_wait(barrier, len(greeted))
+
+    halves = (HALF, CH // 2, HALF, HALF)
+
+    def half_of(ref, w, c, k):
+        rows = pl.ds(pl.multiple_of(k * halves[w], 16), halves[w])
+        return ref.at[c, :, rows] if w == QKV else ref.at[c, rows]
+
+    weights = (qkv_w, out_w, up_w, down_w)
+    sources = (qkv_in, out_in, up_in, down_in)
+
+    def weight_copy(w, d):
+        rows = pl.ds(pl.multiple_of(core * halves[w], 16), halves[w])
+        src = sources[w].at[:, rows] if w == QKV else sources[w].at[rows]
+        return send(src, half_of(weights[w], w, chan, core), ID_W + w * PEERS + d - 1, at_y(d))
+
+    def arrived(w, d, c):
+        part = half_of(weights[w], w, c, core)
+        send(part, part, ID_W + w * PEERS + d - 1, at_y(d)).wait_recv()
+
+    def forward_copy(w, d, c):
+        part = half_of(weights[w], w, c, core)
+        return send(part, part, ID_WF + w * PEERS + d - 1, sibling)
+
+    def forwarded(w, d, c):
+        part = half_of(weights[w], w, c, 1 - core)
+        send(part, part, ID_WF + w * PEERS + d - 1, sibling).wait_recv()
+
+    def pass_on(w, j):
+        off = chunk_off(j)
+        c, d = lax.rem(chan + off, CHUNKS), CHUNKS - off
+        arrived(w, d, c)
+        forward_copy(w, d, c).start()
+
+    def have(w, j):
+        off = chunk_off(j)
+        forwarded(w, CHUNKS - off, lax.rem(chan + off, CHUNKS))
+
+    pages_halo = send(pages_in.at[pl.ds(0, LIFT)], pages.at[pl.ds(2 * ROWS, LIFT)], ID_PAGES, up_rank)
+    pages_halo.start()
+    small_copies = [send(small_in, small.at[chan], ID_SMALL + d - 1, at_y(d)) for d in (1, 3, 2)]
+    cot_halo = send(cot_in.at[pl.ds(0, SHIFT)], cot_v.at[pl.ds(4 * ROWS, SHIFT)], ID_COT_HALO, up_band)
+    weight_copies = [[weight_copy(w, d) for d in (1, 3, 2)] for w in range(4)]
+    for copy in small_copies + weight_copies[QKV] + [cot_halo] + weight_copies[OUT]:
+        copy.start()
+
     def quads(i, _):
-        base = (i // WIN) * BAND + (i % WIN) * SLOT
+        base = (i // WIN) * BAND + lax.rem(i, WIN) * SLOT
         for q in range(2):
             y = dot(pages_sel[...], pages[2 * i + q + LIFT])
             for par in range(2):
@@ -168,13 +322,13 @@
                     at = pl.multiple_of(base + wc * WIN * SLOT, SLOT)
                     first = par * WC * SLOT + wc * SLOT
                     x0[pl.ds(at, SLOT), lanes : lanes + 256] = y[first : first + SLOT]
-        y = jnp.concatenate([dot(token_sel[...], cot[c, i]) for c in range(CHUNKS)], 1)
-        for wc in range(WC):
-            at = pl.multiple_of(base + wc * WIN * SLOT, SLOT)
-            tmp[pl.ds(at, SLOT), 0:D] = y[wc * SLOT : wc * SLOT + SLOT]
         return 0
 
-    lax.fori_loop(0, ROWS, quads, 0)
+    own_pages.wait()
+    whole = ROWS - LIFT // 2
+    lax.fori_loop(0, whole, quads, 0)
+    pages_halo.wait_recv()
+    lax.fori_loop(whole, ROWS, quads, 0)
 
     def norm0(p, _):
         r = rows_of(p)
@@ -182,10 +336,10 @@
         x0[r, :] = u
         inv0[r, :] = inverse
         mn[r, :] = (u * repl[RP_GAIN0 : RP_GAIN0 + 1, :] + repl[RP_SHIFT0 : RP_SHIFT0 + 1, :]).astype(BF16)
-        g2[r, :] = tmp[r, 0:D].astype(BF16)
         return 0
 
     lax.fori_loop(0, NPAIR, norm0, 0)
+    own_merge.wait()
     mt[...] = dot(mn[...], merge_w[...]).astype(BF16)
 
     gain = [repl[RP_GAIN + i : RP_GAIN + i + 1, 0:D] for i in range(2)]
@@ -193,15 +347,33 @@
 
     def norm1(p, _):
         r = rows_of(p)
-        u, inverse = unit_of(mt[r, :].astype(F32))
-        u1[r, :] = u
-        inv1[r, :] = inverse
+        u, _inverse = unit_of(mt[r, :].astype(F32))
         n1[r, :] = (u * gain[0] + shift[0]).astype(BF16)
         return 0
 
     lax.fori_loop(0, NPAIR, norm1, 0)
 
+    for copy in weight_copies[UP]:
+        copy.start()
+
+    own_cot.wait()
+    cot_halo.wait_recv()
+
+    def cot_rows(c):
+        return cot_v.at[pl.ds(ROWS * c + SHIFT, ROWS)]
+
+    cot_copies = [send(cot_rows(lax.rem(chan + d, CHUNKS)), cot.at[chan], ID_COT + d - 1, at_y(d)) for d in (1, 3, 2)]
+    for copy in cot_copies:
+        copy.start()
+    cot_own = local(cot_rows(chan), cot.at[chan], 8)
+    cot_own.start()
+
+    own_small.wait()
+    for d in (1, 2, 3):
+        part = small.at[lax.rem(chan + CHUNKS - d, CHUNKS)]
+        send(part, part, ID_SMALL + d - 1, at_y(d)).wait_recv()
     bias[...] = jnp.zeros_like(bias)
+    lmat[...] = jnp.zeros_like(lmat)
 
     def tables(c, _):
         table = jnp.concatenate([small[c, SM_TABLE : SM_TABLE + 4, :], small[c, SM_TABLE + 4 : SM_TABLE + 8, :]], 1)
@@ -222,14 +394,28 @@
                     bias[c, at : at + SLOT, h * 128 : h * 128 + 128] = both
         return 0
 
-    lmat[...] = jnp.zeros_like(lmat)
     lax.fori_loop(0, CHUNKS, tables, 0)
 
-    def attend(c, _):
-        projected = dot(n1[...], qkv_w[c])
+    def wide(c):
+        return jnp.concatenate([qkv_w[c, i] for i in range(3)], 1)
+
+    own_w[QKV].wait()
+
+    def attend(j, _):
+        c = lax.rem(chan + chunk_off(j), CHUNKS)
+
+        @pl.when(j > 0)
+        def _():
+            have(QKV, j)
+
+        projected = dot(n1[...], wide(c))
         zeros = jnp.zeros((1, CH), F32)
         offset = jnp.concatenate([small[c, SM_QV : SM_QV + 1, :], zeros, small[c, SM_QV + 1 : SM_QV + 2, :]], 1)
         qkv[c] = (projected + offset).astype(BF16)
+
+        @pl.when(j < PEERS)
+        def _():
+            pass_on(QKV, j + 1)
 
         def window_pair(p, _):
             r = rows_of(p)
@@ -246,15 +432,33 @@
             return 0
 
         lax.fori_loop(0, NPAIR, window_pair, 0)
+
+        @pl.when(j == 0)
+        def _():
+            for copy in weight_copies[DOWN]:
+                copy.start()
+
+        @pl.when(j < PEERS)
+        def _():
+            pass_on(OUT, j + 1)
+
         return 0
 
     lax.fori_loop(0, CHUNKS, attend, 0)
 
+    tmp[:, 0:D] = jnp.zeros((T, D), F32)
+    own_w[OUT].wait()
+
     def out_proj(j, _):
-        tmp[:, 0:D] += dot(att[j], out_w[j])
+        c = lax.rem(chan + chunk_off(j), CHUNKS)
+
+        @pl.when(j > 0)
+        def _():
+            have(OUT, j)
+
+        tmp[:, 0:D] += dot(att[c], out_w[c])
         return 0
 
-    tmp[:, 0:D] = jnp.zeros((T, D), F32)
     lax.fori_loop(0, CHUNKS, out_proj, 0)
     out_b = jnp.concatenate([small[c, SM_OUT_B : SM_OUT_B + 1, :] for c in range(CHUNKS)], 1)
     down_b = jnp.concatenate([small[c, SM_DOWN_B : SM_DOWN_B + 1, :] for c in range(CHUNKS)], 1)
@@ -272,12 +476,82 @@
 
     sq_one = lax.fori_loop(0, NPAIR, norm2, jnp.zeros((1, D), F32))
 
+    cot_own.wait()
+    for d in (1, 2, 3):
+        part = cot.at[lax.rem(chan + CHUNKS - d, CHUNKS)]
+        send(part, part, ID_COT + d - 1, at_y(d)).wait_recv()
+
+    def cot_slots(i, _):
+        base = (i // WIN) * BAND + lax.rem(i, WIN) * SLOT
+        y = jnp.concatenate([dot(token_sel[...], cot[c, i]) for c in range(CHUNKS)], 1)
+        for wc in range(WC):
+            at = pl.multiple_of(base + wc * WIN * SLOT, SLOT)
+            tmp[pl.ds(at, SLOT), 0:D] = y[wc * SLOT : wc * SLOT + SLOT]
+        return 0
+
+    lax.fori_loop(0, ROWS, cot_slots, 0)
+    g2[...] = tmp[:, 0:D].astype(BF16)
+
+    grads = (d_qkv, d_out, d_up, d_down)
+    firsts = (l1_qkv, l1_out, l1_up, l1_down)
+    seconds = (l2_qkv, l2_out, l2_up, l2_down)
+
+    def half_grad(w, c, k):
+        return grads[w].at[c, pl.ds(pl.multiple_of(k * halves[w], 16), halves[w])]
+
+    def core_copy(w, j, c):
+        return send(half_grad(w, c, 1 - core), firsts[w].at[j], ID_CORE + w * CHUNKS + j, sibling)
+
+    def owner_copy(w, off):
+        c = lax.rem(chan + off, CHUNKS)
+        return send(half_grad(w, c, core), seconds[w].at[off - 1], ID_Y + w * PEERS + off - 1, at_y(off))
+
+    def core_sum(w, j, off):
+        c = lax.rem(chan + off, CHUNKS)
+        core_copy(w, j, c).wait_recv()
+        step = min(halves[w], 64)
+        for t in range(0, halves[w], step):
+            r = pl.ds(pl.multiple_of(core * halves[w] + t, 16), step)
+            total = grads[w][c, r, :].astype(F32) + firsts[w][j, t : t + step, :].astype(F32)
+            grads[w][c, r, :] = total.astype(BF16)
+
+        @pl.when(off > 0)
+        def _():
+            owner_copy(w, off).start()
+
+    def owner_sum(w, t, step):
+        r = pl.ds(pl.multiple_of(core * halves[w] + t, 16), step)
+        total = grads[w][chan, r, :].astype(F32)
+        for d in range(PEERS):
+            total += seconds[w][d, t : t + step, :].astype(F32)
+        return total.astype(BF16)
+
+    def owner_wait(w):
+        for d in (1, 2, 3):
+            part = seconds[w].at[d - 1]
+            send(part, part, ID_Y + w * PEERS + d - 1, at_y(d)).wait_recv()
+
     br2[...] = jnp.zeros_like(br2)
     dy2[...] = jnp.zeros_like(dy2)
-
-    def feed(c, _):
+    own_w[UP].wait()
+    own_w[DOWN].wait()
+
+    def feed(j, _):
+        c = lax.rem(chan + chunk_off(j), CHUNKS)
+
+        @pl.when(j > 0)
+        def _():
+            have(UP, j)
+            have(DOWN, j)
+
         tmp[:, 0:512] = dot(n2[...], up_w[c])
         tmp[:, 512:1024] = dot_nt(g2[...], down_w[c])
+
+        @pl.when(j < PEERS)
+        def _():
+            pass_on(UP, j + 1)
+            pass_on(DOWN, j + 1)
+
         up_b = row_of(small, c, SM_UP_B, 4)
 
         def gelus(p, total):
@@ -290,11 +564,19 @@
 
         d_up_b = lax.fori_loop(0, NPAIR, gelus, jnp.zeros((1, 512), F32))
         for i in range(4):
-            d_small_o[c, SM_UP_B + i : SM_UP_B + i + 1, :] = d_up_b[:, i * 128 : i * 128 + 128]
+            d_small[c, SM_UP_B + i : SM_UP_B + i + 1, :] = d_up_b[:, i * 128 : i * 128 + 128]
+        d_down[c] = dot_tn(hid[...], g2[...]).astype(BF16)
+        core_copy(DOWN, j, c).start()
+        d_up[c] = dot_tn(n2[...], dpre[...]).astype(BF16)
+        core_copy(UP, j, c).start()
         br2[...] += dot(hid[...], down_w[c])
-        d_down_o[c] = dot_tn(hid[...], g2[...]).astype(BF16)
-        d_up_o[c] = dot_tn(n2[...], dpre[...]).astype(BF16)
         dy2[...] += dot_nt(dpre[...], up_w[c])
+
+        @pl.when(j > 0)
+        def _():
+            core_sum(DOWN, j - 1, chunk_off(j - 1))
+            core_sum(UP, j - 1, chunk_off(j - 1))
+
         return 0
 
     lax.fori_loop(0, CHUNKS, feed, 0)
@@ -309,7 +591,7 @@
         dy = dy2[r, :]
         g = g2[r, :].astype(F32)
         grad = g + norm_back(dy, u, inv2[r, :], gain[1])
-        g1f[r, :] = grad
+        tmp[r, 0:D] = grad
         g1[r, :] = grad.astype(BF16)
         return (
             sq_two + col_sum(branch * branch * valid),
@@ -323,24 +605,112 @@
     start = (jnp.zeros((1, D), F32),) * 6
     sq_two, sq_out, d_down_b, d_gain1, d_shift1, d_out_b = lax.fori_loop(0, NPAIR, norm2_back, start)
     for c in range(CHUNKS):
-        d_small_o[c, SM_DOWN_B : SM_DOWN_B + 1, :] = d_down_b[:, c * CH : c * CH + CH]
-        d_small_o[c, SM_OUT_B : SM_OUT_B + 1, :] = d_out_b[:, c * CH : c * CH + CH]
-    squares_o[...] = jnp.zeros_like(squares_o)
-    for i, sq in enumerate((sq_out, sq_one, sq_two)):
-        squares_o[i : i + 1, :] = sq
+        d_small[c, SM_DOWN_B : SM_DOWN_B + 1, :] = d_down_b[:, c * CH : c * CH + CH]
+        d_small[c, SM_OUT_B : SM_OUT_B + 1, :] = d_out_b[:, c * CH : c * CH + CH]
+
+    core_sum(DOWN, PEERS, 2)
+    core_sum(UP, PEERS, 2)
 
     def block_rows(i, _):
-        base = (i // WIN) * BAND + (i % WIN) * SLOT
+        base = (i // WIN) * BAND + lax.rem(i, WIN) * SLOT
         parts = [r1[pl.ds(pl.multiple_of(base + wc * WIN * SLOT, SLOT), SLOT), :] for wc in range(WC)]
-        block_o[i] = dot(token_sel_t[...], jnp.concatenate(parts, 0).astype(BF16)).astype(BF16)
+        y = dot(token_sel_t[...], jnp.concatenate(parts, 0).astype(BF16)).astype(BF16)
+        for c in range(CHUNKS):
+            blk_tx[c, i] = y[:, c * CH : c * CH + CH]
         return 0
 
     lax.fori_loop(0, ROWS, block_rows, 0)
 
-    dy1[...] = jnp.zeros_like(dy1)
-
-    def attend_back(c, _):
-        d_out_o[c] = dot_tn(att[c], g1[...]).astype(BF16)
+    def blk_rows(c):
+        return blk_rx.at[pl.ds(ROWS * c + SHIFT, ROWS)]
+
+    blk_copies = [
+        send(blk_tx.at[lax.rem(chan + d, CHUNKS)], blk_rows(chan), ID_BLK + d - 1, at_y(d)) for d in (1, 3, 2)
+    ]
+    for copy in blk_copies:
+        copy.start()
+    blk_own = local(blk_tx.at[chan], blk_rows(chan), 9)
+    blk_own.start()
+
+    planes = ((ga, rza, hza, rxa, gfa), (gb, rzb, hzb, rxb, gfb))
+
+    def rz_copy(i, d):
+        rows = pl.ds(pl.multiple_of(lax.rem(z + d, 4) * 64, 16), 64)
+        return send(planes[i][0].at[rows], planes[i][1].at[d - 1], ID_RZ + i * PEERS + d - 1, at_z(d))
+
+    def rx_copy(i, d):
+        rows = pl.ds(pl.multiple_of(lax.rem(x + d, 4) * 16, 16), 16)
+        return send(planes[i][2].at[rows], planes[i][3].at[d - 1], ID_RX + i * PEERS + d - 1, at_x(d))
+
+    def gx_copy(i, d):
+        part = planes[i][4].at[core, pl.ds(pl.multiple_of(z * 64 + x * 16, 16), 16)]
+        return send(part, part, ID_GX + i * PEERS + d - 1, at_x(d))
+
+    def gx_wait(i, d):
+        part = planes[i][4].at[core, pl.ds(pl.multiple_of(z * 64 + lax.rem(x + 4 - d, 4) * 16, 16), 16)]
+        send(part, part, ID_GX + i * PEERS + d - 1, at_x(d)).wait_recv()
+
+    def gz_copy(i, d):
+        part = planes[i][4].at[core, pl.ds(pl.multiple_of(z * 64, 16), 64)]
+        return send(part, part, ID_GZ + i * PEERS + d - 1, at_z(d))
+
+    def gz_wait(i, d):
+        part = planes[i][4].at[core, pl.ds(pl.multiple_of(lax.rem(z + 4 - d, 4) * 64, 16), 64)]
+        send(part, part, ID_GZ + i * PEERS + d - 1, at_z(d)).wait_recv()
+
+    def gc_copy(i):
+        part = planes[i][4].at[core]
+        return send(part, part, ID_GC + i, sibling)
+
+    def gc_wait(i):
+        part = planes[i][4].at[1 - core]
+        send(part, part, ID_GC + i, sibling).wait_recv()
+
+    order = (1, 3, 2)
+
+    def plane_rz(i):
+        for d in order:
+            rz_copy(i, d).start()
+
+    def plane_rx(i):
+        g, rz, hz = planes[i][0:3]
+        for d in order:
+            rz_copy(i, d).wait_recv()
+        total = g[pl.ds(pl.multiple_of(z * 64, 16), 64), :].astype(F32)
+        for d in range(PEERS):
+            total += rz[d].astype(F32)
+        hz[...] = total.astype(BF16)
+        for d in order:
+            rx_copy(i, d).start()
+
+    def plane_gx(i):
+        hz, rx, gf = planes[i][2:5]
+        for d in order:
+            rx_copy(i, d).wait_recv()
+        total = hz[pl.ds(pl.multiple_of(x * 16, 16), 16), :].astype(F32)
+        for d in range(PEERS):
+            total += rx[d].astype(F32)
+        gf[core, pl.ds(pl.multiple_of(z * 64 + x * 16, 16), 16), :] = total.astype(BF16)
+        for d in order:
+            gx_copy(i, d).start()
+
+    def plane_gz(i):
+        for d in order:
+            gx_wait(i, d)
+        for d in order:
+            gz_copy(i, d).start()
+
+    def plane_gc(i):
+        for d in order:
+            gz_wait(i, d)
+        gc_copy(i).start()
+
+    tmp[:, D : 2 * D] = jnp.zeros((T, D), F32)
+
+    def attend_back(j, _):
+        c = lax.rem(chan + back_off(j), CHUNKS)
+        d_out[c] = dot_tn(att[c], g1[...]).astype(BF16)
+        core_copy(OUT, j, c).start()
         hid[:, 0:CH] = dot_nt(g1[...], out_w[c]).astype(BF16)
         gsum[...] = jnp.zeros_like(gsum)
 
@@ -365,15 +735,16 @@
             return 0
 
         lax.fori_loop(0, NPAIR, window_pair, 0)
-        d_qkv_o[c] = dot_tn(n1[...], dqkv[...]).astype(BF16)
-        dy1[...] += dot_nt(dqkv[...], qkv_w[c])
+        d_qkv[c] = dot_tn(n1[...], dqkv[...]).astype(BF16)
+        core_copy(QKV, j, c).start()
+        tmp[:, D : 2 * D] += dot_nt(dqkv[...], wide(c))
 
         def sums(p, total):
             return total + col_sum(dqkv[rows_of(p), :].astype(F32))
 
         total = lax.fori_loop(0, NPAIR, sums, jnp.zeros((1, 3 * CH), F32))
-        d_small_o[c, SM_QV : SM_QV + 1, :] = total[:, 0:CH]
-        d_small_o[c, SM_QV + 1 : SM_QV + 2, :] = total[:, 2 * CH : 3 * CH]
+        d_small[c, SM_QV : SM_QV + 1, :] = total[:, 0:CH]
+        d_small[c, SM_QV + 1 : SM_QV + 2, :] = total[:, 2 * CH : 3 * CH]
 
         half = WIN * SLOT
         for h in range(HEADS_C):
@@ -390,8 +761,35 @@
             rows = [lmat[h * SLOT + b_q : h * SLOT + b_q + 1, :] for h in range(HEADS_C)]
             rows = jnp.concatenate(rows + [jnp.zeros((SLOT - HEADS_C, 128), F32)], 0)
             d_table += dot_nt(rows.astype(BF16), table_sel[:, b_q * 128 : b_q * 128 + 128])
-        d_small_o[c, SM_TABLE : SM_TABLE + 4, :] = d_table[0:4, 0:128]
-        d_small_o[c, SM_TABLE + 4 : SM_TABLE + 8, :] = d_table[0:4, 128:256]
+        d_small[c, SM_TABLE : SM_TABLE + 4, :] = d_table[0:4, 0:128]
+        d_small[c, SM_TABLE + 4 : SM_TABLE + 8, :] = d_table[0:4, 128:256]
+
+        @pl.when(j > 0)
+        def _():
+            core_sum(OUT, j - 1, back_off(j - 1))
+            core_sum(QKV, j - 1, back_off(j - 1))
+
+        @pl.when(j == 0)
+        def _():
+            owner_wait(DOWN)
+            owner_wait(UP)
+            for t in range(0, HALF, 64):
+                ga[t : t + 64, 0:512] = owner_sum(DOWN, t, 64)
+                ga[t : t + 64, 512:1024] = owner_sum(UP, t, 64)
+            plane_rz(0)
+
+        @pl.when(j == 1)
+        def _():
+            plane_rx(0)
+
+        @pl.when(j == 2)
+        def _():
+            plane_gx(0)
+
+        @pl.when(j == 3)
+        def _():
+            plane_gz(0)
+
         return 0
 
     lax.fori_loop(0, CHUNKS, attend_back, 0)
@@ -399,14 +797,42 @@
     def norm1_back(p, carry):
         d_gain, d_shift = carry
         r = rows_of(p)
-        u = u1[r, :]
-        dy = dy1[r, :]
-        gz[r, :] = (g1f[r, :] + norm_back(dy, u, inv1[r, :], gain[0])).astype(BF16)
+        u, inverse = unit_of(mt[r, :].astype(F32))
+        dy = tmp[r, D : 2 * D]
+        gz[r, :] = (tmp[r, 0:D] + norm_back(dy, u, inverse, gain[0])).astype(BF16)
         return d_gain + col_sum(dy * u), d_shift + col_sum(dy)
 
     d_gain0, d_shift0 = lax.fori_loop(0, NPAIR, norm1_back, start[:2])
 
-    d_merge_o[...] = dot_tn(mn[...], gz[...]).astype(BF16)
+    mine = pl.ds(pl.multiple_of(core * HALF, HALF), HALF)
+    other = pl.ds(pl.multiple_of((1 - core) * HALF, HALF), HALF)
+    merge_core = send(d_merge.at[:, other], l1_m, ID_CORE_M, sibling)
+    d_merge[:, other] = dot_tn(mn[...], gz[:, other]).astype(BF16)
+    merge_core.start()
+    d_merge[:, mine] = dot_tn(mn[...], gz[:, mine]).astype(BF16)
+    core_sum(OUT, PEERS, 0)
+    core_sum(QKV, PEERS, 0)
+    plane_gc(0)
+
+    blk_own.wait()
+    for d in (1, 2, 3):
+        part = blk_rows(lax.rem(chan + CHUNKS - d, CHUNKS))
+        send(part, part, ID_BLK + d - 1, at_y(d)).wait_recv()
+    blk_halo = send(blk_rx.at[pl.ds(4 * ROWS, SHIFT)], blk_rx.at[pl.ds(0, SHIFT)], ID_BLK_HALO, down_band)
+    blk_halo.start()
+
+    merge_core.wait_recv()
+    for t in range(0, 1024, 128):
+        total = d_merge[t : t + 128, mine].astype(F32) + l1_m[t : t + 128, :].astype(F32)
+        d_merge[t : t + 128, mine] = total.astype(BF16)
+
+    def merge_owner(d):
+        rows = pl.ds(pl.multiple_of(lax.rem(chan + d, CHUNKS) * HALF, HALF), HALF)
+        return send(d_merge.at[rows, mine], l2_m.at[d - 1], ID_Y_M + d - 1, at_y(d))
+
+    for d in order:
+        merge_owner(d).start()
+
     tmp[...] = dot_nt(gz[...], merge_w[...])
 
     def norm0_back(p, carry):
@@ -419,14 +845,60 @@
 
     start0 = (jnp.zeros((1, 1024), F32),) * 2
     d_gain_m, d_shift_m = lax.fori_loop(0, NPAIR, norm0_back, start0)
-    d_repl_o[0:1, :] = d_gain_m
-    d_repl_o[1:2, :] = d_shift_m
-    d_repl_o[2:3, :] = jnp.concatenate([d_gain0, d_gain1], 1)
-    d_repl_o[3:4, :] = jnp.concatenate([d_shift0, d_shift1], 1)
-    d_repl_o[4:8, :] = jnp.zeros((4, 1024), F32)
+
+    for c in range(CHUNKS):
+        sg[0, SG_CHUNK + 16 * c : SG_CHUNK + 16 * c + 16, :] = d_small[c]
+    rows = [d_gain_m, d_shift_m, d_gain0, d_gain1, d_shift0, d_shift1]
+    at = SG_REPL
+    for row in rows:
+        for i in range(row.shape[1] // 128):
+            sg[0, at : at + 1, :] = row[:, i * 128 : i * 128 + 128]
+            at += 1
+    squares = [sum(sq[:, i * 128 : i * 128 + 128] for i in range(4)) for sq in (sq_out, sq_one, sq_two)]
+    sg[0, SG_SQ:SG_ROWS, :] = jnp.concatenate(squares + [jnp.zeros((5, 128), F32)], 0)
+
+    def sg_copies(level):
+        if level == 0:
+            return [send(sg.at[0], sg_c.at[0], ID_SG_C, sibling)]
+        into, first, at = ((sg_y, ID_SG_Y, at_y), (sg_z, ID_SG_Z, at_z), (sg_x, ID_SG_X, at_x))[level - 1]
+        return [send(sg.at[level], into.at[d - 1], first + d - 1, at(d)) for d in order]
+
+    def sg_start(level):
+        for copy in sg_copies(level):
+            copy.start()
+
+    def sg_sum(level):
+        for copy in sg_copies(level):
+            copy.wait_recv()
+        into = (sg_c, sg_y, sg_z, sg_x)[level]
+        total = sg[level]
+        for d in range(into.shape[0]):
+            total += into[d]
+        sg[level + 1] = total
+
+    sg_start(0)
+
+    owner_wait(QKV)
+    owner_wait(OUT)
+    for t in range(0, HALF, 64):
+        gb[t : t + 64, 0:384] = owner_sum(QKV, t, 64)
+    out_half = owner_sum(OUT, 0, 64)
+    for g in range(4):
+        gb[g * 64 : g * 64 + 64, 384:512] = out_half[:, g * 128 : g * 128 + 128]
+    for d in order:
+        merge_owner(d).wait_recv()
+    for t in range(0, HALF, 64):
+        r = pl.ds(pl.multiple_of(chan * HALF + t, 16), 64)
+        total = d_merge[r, mine].astype(F32)
+        for d in range(PEERS):
+            total += l2_m[d, t : t + 64, :].astype(F32)
+        gb[t : t + 64, 512:768] = total.astype(BF16)
+    plane_rz(1)
+    sg_sum(0)
+    sg_start(1)
 
     def page_rows(i, _):
-        base = (i // WIN) * BAND + (i % WIN) * SLOT
+        base = (i // WIN) * BAND + lax.rem(i, WIN) * SLOT
         for q in range(2):
             parts = []
             for par in range(2):
@@ -434,52 +906,138 @@
                 for wc in range(WC):
                     at = pl.multiple_of(base + wc * WIN * SLOT, SLOT)
                     parts.append(tmp[pl.ds(at, SLOT), lanes : lanes + 256])
-            pages_o[2 * i + q] = dot(pages_sel_t[...], jnp.concatenate(parts, 0).astype(BF16))
+            y = dot(pages_sel_t[...], jnp.concatenate(parts, 0).astype(BF16))
+            pg[2 * i + q + LIFT] = y.astype(BF16)
         return 0
 
     lax.fori_loop(0, ROWS, page_rows, 0)
+    pg_halo = send(pg.at[pl.ds(2 * ROWS, LIFT)], pg.at[pl.ds(0, LIFT)], ID_PG, down_rank)
+    pg_halo.start()
+
+    plane_rx(1)
+    sg_sum(1)
+    sg_start(2)
+    plane_gx(1)
+    sg_sum(2)
+    sg_start(3)
+    plane_gz(1)
+
+    blk_halo.wait_recv()
+    block_copy = local(blk_rx.at[pl.ds(0, 4 * ROWS)], block_o, 10)
+    block_copy.start()
+    gc_wait(0)
+    mlp_copy = local(gfa, mlp_o, 11)
+    mlp_copy.start()
+    pg_halo.wait_recv()
+    pages_copy = local(pg.at[pl.ds(0, 2 * ROWS)], pages_o, 12)
+    pages_copy.start()
+    sg_sum(3)
+    small_copy = local(sg.at[4], small_o, 13)
+    small_copy.start()
+
+    plane_gc(1)
+    own_rows = pl.ds(pl.multiple_of(chan * HALF, HALF), HALF)
+    mf[own_rows, mine] = gfb[core, :, 512:768]
+    gy_copies = [send(mf.at[own_rows, mine], mf.at[own_rows, mine], ID_GY_M + d - 1, at_y(d)) for d in order]
+    for copy in gy_copies:
+        copy.start()
+    for d in order:
+        r = pl.ds(pl.multiple_of(lax.rem(chan + CHUNKS - d, CHUNKS) * HALF, HALF), HALF)
+        send(mf.at[r, mine], mf.at[r, mine], ID_GY_M + d - 1, at_y(d)).wait_recv()
+    gc_merge = send(mf.at[:, mine], mf.at[:, mine], ID_GC_M, sibling)
+    gc_merge.start()
+    gc_wait(1)
+    attn_copy = local(gfb, attn_o, 14)
+    attn_copy.start()
+    send(mf.at[:, other], mf.at[:, other], ID_GC_M, sibling).wait_recv()
+    merge_copy = local(mf, merge_o, 15)
+    merge_copy.start()
+
+    for copy in [pages_halo, cot_halo, blk_halo, pg_halo, merge_core, gc_merge] + small_copies + cot_copies + blk_copies:
+        copy.wait_send()
+    for w in range(4):
+        for copy in weight_copies[w]:
+            copy.wait_send()
+        for d in order:
+            forward_copy(w, d, lax.rem(chan + CHUNKS - d, CHUNKS)).wait_send()
+            owner_copy(w, d).wait_send()
+        for j in range(CHUNKS):
+            off = chunk_off(j) if w in (UP, DOWN) else back_off(j)
+            core_copy(w, j, lax.rem(chan + off, CHUNKS)).wait_send()
+    for i in range(2):
+        for d in order:
+            for make in (rz_copy, rx_copy, gx_copy, gz_copy):
+                make(i, d).wait_send()
+        gc_copy(i).wait_send()
+    for level in range(4):
+        for copy in sg_copies(level):
+            copy.wait_send()
+    for d in order:
+        merge_owner(d).wait_send()
+    for copy in gy_copies:
+        copy.wait_send()
+    for copy in (block_copy, mlp_copy, pages_copy, small_copy, attn_copy, merge_copy):
+        copy.wait()
 
 
 def kernel_call(args):
     vm = pl.BlockSpec(memory_space=pltpu.VMEM)
+    hbm = pl.BlockSpec(memory_space=pl.ANY)
     s = jax.ShapeDtypeStruct
     outs = [
-        s((ROWS, COLS, D), BF16),
-        s((2 * ROWS, 2 * COLS, 256), F32),
+        s((4 * ROWS, COLS, CH), BF16),
+        s((2 * ROWS, 2 * COLS, 256), BF16),
+        s((2, HALF, 1024), BF16),
+        s((2, HALF, 768), BF16),
         s((1024, D), BF16),
-        s((CHUNKS, D, 3 * CH), BF16),
-        s((CHUNKS, CH, D), BF16),
-        s((CHUNKS, D, 512), BF16),
-        s((CHUNKS, 512, D), BF16),
-        s((CHUNKS, 16, 128), F32),
-        s((8, 1024), F32),
-        s((8, D), F32),
+        s((SG_ROWS, 128), F32),
     ]
-    v = pltpu.VMEM
+
+    def v(shape, dtype):
+        return pltpu.VMEM(shape, dtype)
+
     scratch = [
-        v((T, 1024), F32), v((T, 1), F32), v((T, 1024), BF16), v((T, D), BF16),
-        v((T, D), F32), v((T, 1), F32), v((T, D), BF16),
+        v((2 * ROWS + LIFT, 2 * COLS, 256), BF16), v((4 * ROWS + SHIFT, COLS, CH), BF16), v((CHUNKS, ROWS, COLS, CH), BF16),
+        v((1024, D), BF16), v((CHUNKS, 3, D, CH), BF16), v((CHUNKS, CH, D), BF16),
+        v((CHUNKS, D, 512), BF16), v((CHUNKS, 512, D), BF16), v((CHUNKS, 16, 128), F32),
+        v((T, 1024), F32), v((T, 1), F32), v((T, 1024), BF16), v((T, D), BF16), v((T, D), BF16),
         v((CHUNKS, T, 3 * CH), BF16), v((CHUNKS, NPAIR, PAIR, 512), BF16), v((CHUNKS, T, CH), BF16),
         v((T, D), F32), v((T, D), F32), v((T, 1), F32), v((T, D), BF16), v((T, D), BF16),
         v((T, D), F32), v((T, D), F32),
-        v((8, 128), F32), v((T, 512), BF16), v((T, 512), BF16),
+        v((T, 512), BF16), v((T, 512), BF16),
         v((CHUNKS, PAIR, 512), F32), v((HEADS_C * SLOT, 128), F32), v((PAIR, 512), F32),
-        v((T, 3 * CH), BF16), v((T, D), F32), v((T, D), BF16), v((T, D), F32), v((T, D), BF16),
-        v((T, 1024), F32),
+        v((T, 3 * CH), BF16), v((T, D), BF16), v((T, D), BF16), v((T, 1024), F32),
+        v((CHUNKS, ROWS, COLS, CH), BF16), v((4 * ROWS + SHIFT, COLS, CH), BF16),
+        v((2 * ROWS + LIFT, 2 * COLS, 256), BF16),
+        v((1024, D), BF16), v((CHUNKS, D, 3 * CH), BF16), v((CHUNKS, CH, D), BF16),
+        v((CHUNKS, D, 512), BF16), v((CHUNKS, 512, D), BF16), v((CHUNKS, 16, 128), F32), v((8, 1024), F32),
+        v((CHUNKS, HALF, 3 * CH), BF16), v((CHUNKS, CH // 2, D), BF16), v((CHUNKS, HALF, 512), BF16),
+        v((CHUNKS, HALF, D), BF16), v((1024, HALF), BF16),
+        v((PEERS, HALF, 3 * CH), BF16), v((PEERS, CH // 2, D), BF16), v((PEERS, HALF, 512), BF16),
+        v((PEERS, HALF, D), BF16), v((PEERS, HALF, HALF), BF16),
+    ]
+    for lanes in (1024, 768):
+        scratch += [
+            v((HALF, lanes), BF16), v((PEERS, 64, lanes), BF16), v((64, lanes), BF16), v((PEERS, 16, lanes), BF16),
+            v((2, HALF, lanes), BF16),
+        ]
+    scratch += [v((1024, D), BF16), v((5, SG_ROWS, 128), F32), v((1, SG_ROWS, 128), F32)]
+    scratch += [v((PEERS, SG_ROWS, 128), F32)] * 3
+    scratch += [
+        pltpu.SemaphoreType.DMA((IDS.count,)),
+        pltpu.SemaphoreType.DMA((IDS.count,)),
+        pltpu.SemaphoreType.DMA((LOCAL,)),
     ]
     return pl.pallas_call(
         compute,
         out_shape=outs,
-        in_specs=[vm] * len(args),
-        out_specs=[vm] * len(outs),
+        in_specs=[hbm] * 8 + [vm] * (len(args) - 8),
+        out_specs=[hbm] * len(outs),
         scratch_shapes=scratch,
-        compiler_params=pltpu.CompilerParams(vmem_limit_bytes=60 * 1024 * 1024),
+        compiler_params=pltpu.CompilerParams(
+            vmem_limit_bytes=63 * 1024 * 1024, collective_id=0, has_side_effects=True
+        ),
     )(*args)
-
-
-def shifted(shard, axis, by):
-    count = lax.axis_size(axis)
-    return lax.ppermute(shard, axis, [(i, (i + by) % count) for i in range(count)])
 
 
 def pack_small(qv_bias, rel_table, out_bias, up_bias, down_bias):
@@ -497,34 +1055,22 @@
         [merge_gain[None], merge_shift[None], jnp.pad(norm_gain, ((0, 0), (0, 512))), jnp.pad(norm_shift, ((0, 0), (0, 512)))], 0
     ).astype(F32)
     repl = jnp.pad(repl, ((0, 2), (0, 0)))
-    gather = functools.partial(lax.all_gather, axis_name="chan", axis=0, tiled=False)
-    pages_ext = jnp.concatenate([pages, shifted(pages[:LIFT], ("space", "chan"), -1)], 0)
-    cot_ext = jnp.concatenate([cotangent[SHIFT:], shifted(cotangent[:SHIFT], "space", -1)], 0)
-    cot = lax.all_to_all(cot_ext.reshape(CHUNKS, ROWS, COLS, CH), "chan", split_axis=0, concat_axis=0, tiled=True)
     args = [
-        pages_ext, cot, merge_weight, gather(qkv_weight.reshape(D, 3 * CH)), gather(out_weight),
-        gather(up_weight), gather(down_weight), gather(small), repl, *constants(),
+        pages, cotangent, merge_weight, qkv_weight.transpose(1, 0, 2), out_weight,
+        up_weight, down_weight, small, repl, *constants(),
     ]
-    block, grad_pages, d_merge, d_qkv, d_out, d_up, d_down, d_small, d_repl, squares = kernel_call(args)
-    block = lax.all_to_all(block, "chan", split_axis=2, concat_axis=0, tiled=True)
-    block = jnp.concatenate([shifted(block[-SHIFT:], "space", 1), block[:-SHIFT]], 0).astype(F32)
-    grad_pages = jnp.concatenate(
-        [shifted(grad_pages[-LIFT:].astype(BF16), ("space", "chan"), 1).astype(F32), grad_pages[:-LIFT]], 0
-    )
-
-    def reduced(chunked):
-        mine = lax.psum_scatter(chunked, "chan", scatter_dimension=0, tiled=False)
-        return lax.psum(mine, "space").astype(F32)
-
-    d_merge, d_repl, squares, d_small = lax.psum((d_merge, d_repl, squares, d_small), ("space", "chan"))
-    d_small = lax.dynamic_index_in_dim(d_small, lax.axis_index("chan"), 0, keepdims=False)
-    rms = jnp.sqrt(jnp.sum(squares[:3], 1) / float(1792 * COLS * D))
-    table = jnp.concatenate([d_small[2:6], d_small[6:10]], 1)[:, :169]
+    block, grad_pages, mlp, attn, d_merge, sums = kernel_call(args)
+    chunk = lax.dynamic_slice_in_dim(sums, lax.axis_index("chan") * 16, 16, 0)
+    rms = jnp.sqrt(jnp.sum(sums[SG_SQ : SG_SQ + 3], 1) / float(1792 * COLS * D))
+    table = jnp.concatenate([chunk[2:6], chunk[6:10]], 1)[:, :169]
+    norms = sums[SG_REPL : SG_REPL + 32].reshape(4, 1024)
+    d_out = attn[:, :, 384:512].reshape(2, 4, 64, 128).transpose(0, 2, 1, 3).reshape(CH, D)
     return (
-        block, grad_pages, d_repl[0], d_repl[1], d_merge.astype(F32),
-        d_repl[2].reshape(2, D), d_repl[3].reshape(2, D),
-        reduced(d_qkv).reshape(D, 3, CH), d_small[0:2], table, reduced(d_out), d_small[10],
-        reduced(d_up), d_small[11:15].reshape(512), reduced(d_down), d_small[15], rms,
+        block.astype(F32), grad_pages.astype(F32), norms[0], norms[1], d_merge.astype(F32),
+        norms[2].reshape(2, D), norms[3].reshape(2, D),
+        attn[:, :, 0:384].reshape(D, 3, CH).astype(F32), chunk[0:2], table, d_out.astype(F32), chunk[10],
+        mlp[:, :, 512:1024].reshape(D, 512).astype(F32), chunk[11:15].reshape(512),
+        mlp[:, :, 0:512].reshape(512, D).astype(F32), chunk[15], rms,
     )
 
 

time: 726 us -> 188 us (0.26)
  waiting for transfers between devices: 531 us -> 0 us
  Pallas kernels: 83.2 us -> 163 us
  blocking collectives: 33 us -> 0 us
  starting transfers between devices: 21.2 us -> 0 us
  between operations: 14.5 us -> 0.8 us
  local copies, waits for them, and re-layouts: 26.7 us -> 15.7 us
  other arithmetic: 15.6 us -> 8.16 us
    psum x3 -> x0, waiting for transfers between devices: 366 us -> none  [the longest x2 260 us: body(): lax.psum((d_merge, d_repl, squares, d_small), ('space', 'chan'))]
    reduce_scatter x4 -> x0, waiting for transfers between devices: 108 us -> none  [reduced(): mine = lax.psum_scatter(chunked, 'chan', scatter_dimension=0, tiled=False)]
    pallas_call x1, Pallas kernels: 83.2 us -> 163 us  [kernel_call(): pl.pallas_call(compute, out_shape=outs, in_specs=[hbm] * 8 + [vm] * (len(...]
    all_gather x3 -> x0, waiting for transfers between devices: 51 us -> none  [the longest x1 31 us: body(): gather(down_weight)]
    all_gather x2 -> x0, blocking collectives: 33 us -> none  [the longest x1 21.3 us: body(): gather(small)]
    ppermute x4 -> x0, starting transfers between devices: 12.1 us -> none  [shifted(): lax.ppermute(shard, axis, [(i, (i + by) % count) for i in range(count)])]
    all_to_all x2 -> x0, starting transfers between devices: 8.77 us -> none  [the longest x1 5.28 us: body(): lax.all_to_all(block, 'chan', split_axis=2, concat_axis=0, tiled=True)]
  transfers between devices with their start and end apart: 16 -> 0, of which waited for: 10 -> 0; matrix products, arithmetic and copies ran while one was open for 5% -> 0% of each run, Pallas kernels for 0% -> 0%
where the time goes in v2:
time: 188 us; the launch traced here: 187 us
  Pallas kernels  163 us (87%)
  local copies, waits for them, and re-layouts  15.7 us (8%)
  other arithmetic  8.16 us (4%)
    pallas_call x1, Pallas kernels, kernel_call(): pl.pallas_call(compute, out_shape=outs, in_specs=[hbm] * 8 + [vm] * (len(...  163 us
    unnamed x20, local copies, waits for them, and re-layouts  5.28 us

profile of v2, /device:TPU:1, one launch (start us, length us, event | category | flops | bytes accessed | tf_op | source)
XLA Modules:
  0.0 187.3 jit_solution(16672577334195324512)
XLA Ops:
  0.7 0.0 copy-start.6
  0.7 0.0 copy-start.7
  0.7 0.0 copy-start.5
  0.7 0.0 copy-start.4
  0.7 0.7 pad_slice_fusion
  1.4 1.5 concatenate.9
  2.9 0.6 convert_element_type.50.small_in
  3.5 2.0 %copy.42.cot_in = bf16[56,42,128]{2,1,0:T(8,128)(2,1)} copy(bf16[56,42,128]{2,0,1:T(8,128)(2,1)} %param.36) | data formatting | bytes 1204224 | tf_op args[15]
  5.5 0.0 copy-done.6
  5.5 0.0 copy-done.7
  5.6 0.6 pad_convert_fusion.repl
  6.2 162.7 %shard_map.332 = (bf16[56,42,128]{2,1,0:T(8,128)(2,1)}, bf16[28,84,256]{2,1,0:T(8,128)(2,1)}, bf16[2,256,1024]{2,1,0:T(8,128)(2,1)}, bf16[2,256,768]{2,1,0:T(8,1...) custom-call(bf16[28,84,256]{2,1,0:T(8,128)(2,1)} %pages_in.1, bf16[56,42,128]{2,1,0:T(8,128)(2,1)} %copy.42.cot_in, ...), custom_call_target="tpu_custom_call" | custom-call | tf_op jit(solution)/shard_map/pallas_call | solution.py:1031
  169.0 1.4 dynamic-slice_bitcast_fusion
  170.4 0.6 pad_maximum_fusion
  171.0 1.3 fusion.5
  172.2 1.2 constant_dynamic-slice_fusion.3
  173.5 1.3 fusion.7
  174.7 1.7 bitcast_convert_fusion
  176.4 1.3 fusion.8
  177.7 0.6 reshape_squeeze.6
  178.3 0.6 reshape_squeeze.7
  178.9 0.8 slice_reduce_fusion
  179.7 0.5 multiply_sqrt_fusion
  180.2 0.1 slice_convert_fusion
  180.3 0.3 reshape.71
  180.6 0.9 copy.46
  181.6 0.2 copy.44
  181.8 0.7 copy.51
  182.5 0.4 copy-done
  182.9 1.7 convert_element_type.52
  184.6 1.6 convert_element_type.53
  186.2 1.1 copy.45
  (14 shorter events, 0.1 us)
Async XLA Ops:
  0.7 4.8 %copy-start.6 = (bf16[1024]{0:T(1024)(128)(2,1)S(1)}, bf16[1024]{0:T(1024)(128)(2,1)}, u32[]{:S(2)}) copy-start(bf16[1024]{0:T(1024)(128)(2,1)} %param.22) | copy-start | bytes 6148
  0.7 4.8 %copy-start.7 = (bf16[1024]{0:T(1024)(128)(2,1)S(1)}, bf16[1024]{0:T(1024)(128)(2,1)}, u32[]{:S(2)}) copy-start(bf16[1024]{0:T(1024)(128)(2,1)} %param.23) | copy-start | bytes 6148
  0.7 4.9 %copy-start.5 = (bf16[2,512]{1,0:T(2,128)(2,1)S(1)}, bf16[2,512]{1,0:T(2,128)(2,1)}, u32[]{:S(2)}) copy-start(bf16[2,512]{1,0:T(2,128)(2,1)} %param.25) | copy-start | bytes 6148
  0.7 4.9 %copy-start.4 = (bf16[2,512]{1,0:T(2,128)(2,1)S(1)}, bf16[2,512]{1,0:T(2,128)(2,1)}, u32[]{:S(2)}) copy-start(bf16[2,512]{1,0:T(2,128)(2,1)} %param.26) | copy-start | bytes 6148
  174.7 5.5 %copy-start.3 = (bf16[2,256,768]{2,1,0:T(8,128)(2,1)S(1)}, bf16[2,256,768]{2,1,0:T(8,128)(2,1)}, u32[]{:S(2)}) copy-start(bf16[2,256,768]{2,1,0:T(8,128)(2,1)} %get-tuple-element.27) | copy-start | bytes 2359300
  181.5 1.4 copy-start
  182.9 1.7 copy-start.1
  184.6 1.6 copy-start.2

commit v3 on v1

v3 whole, which is shorter than its diff:
```python
import functools

import jax
import jax.numpy as jnp
import numpy as np
from jax import lax
from jax.experimental import pallas as pl
from jax.experimental.pallas import tpu as pltpu
from jax.sharding import PartitionSpec as P

D = 512
HEADS = 16
HD = 32
FF = 2048
WIN = 7
SHIFT = 3
COLS = 42
ROWS = 14
WC = COLS // WIN
SLOT = 8
PAIR = 2 * WIN * SLOT
NPAIR = WC
T = PAIR * NPAIR
BAND = WC * WIN * SLOT
CHUNKS = 4
CH = D // CHUNKS
HEADS_C = HEADS // CHUNKS
LIFT = 2 * SHIFT
EPS = 1e-05
MASKED = -1e9
SCALE = HD ** (-0.5)
F32 = jnp.float32
BF16 = jnp.bfloat16


def dot(a, b):
    return jnp.dot(a, b, preferred_element_type=F32)


def dot_nt(a, b):
    return lax.dot_general(a, b, (((1,), (1,)), ((), ())), preferred_element_type=F32)


def dot_tn(a, b):
    return lax.dot_general(a, b, (((0,), (0,)), ((), ())), preferred_element_type=F32)


def constants():
    slots = np.arange(WC * SLOT)
    column = slots // SLOT * WIN + slots % SLOT
    real = slots % SLOT < WIN
    pages_sel = np.zeros((2, WC * SLOT, 2 * COLS), np.float32)
    for parity in range(2):
        source = (2 * column + parity + LIFT) % (2 * COLS)
        pages_sel[parity, slots[real], source[real]] = 1
    pages_sel = pages_sel.reshape(2 * WC * SLOT, 2 * COLS)
    table_sel = np.zeros((256, SLOT, 128), np.float32)
    for b_q in range(WIN):
        for i in range(2 * WIN - 1):
            for b_k in range(WIN):
                code = (12 - i) * 13 + b_q - b_k + 6
                table_sel[code, b_q, i * SLOT + b_k] = 1
    table_sel = table_sel.reshape(256, SLOT * 128)
    table_sel_t = np.zeros((256, SLOT, 128), np.float32)
    for b_k in range(WIN):
        for i in range(2 * WIN - 1):
            for b_q in range(WIN):
                table_sel_t[i * 13 + b_q - b_k + 6, b_k, i * SLOT + b_q] = 1
    table_sel_t = table_sel_t.reshape(256, SLOT * 128)
    arrays = (pages_sel, pages_sel.T, table_sel, table_sel_t)
    return [jnp.asarray(a, BF16) for a in arrays]


def iota(shape, dim):
    return lax.broadcasted_iota(jnp.int32, shape, dim)


def gelu_parts(x):
    z = jnp.abs(x) * (0.5**0.5)
    t = 1.0 / (1.0 + 0.3275911 * z)
    e = jnp.exp(-z * z)
    poly = t * (0.254829592 + t * (-0.284496736 + t * (1.421413741 + t * (-1.453152027 + t * 1.061405429))))
    tail = 0.5 * poly * e
    cdf = jnp.where(x >= 0, 1.0 - tail, tail)
    return x * cdf, cdf + x * e * 0.3989422804014327


def unit_of(x):
    centered = x - jnp.mean(x, -1, keepdims=True)
    inverse = lax.rsqrt(jnp.mean(centered * centered, -1, keepdims=True) + EPS)
    return centered * inverse, inverse


def norm_back(dy, u, inverse, gain):
    scaled = dy * gain
    first = jnp.mean(scaled, -1, keepdims=True)
    second = jnp.mean(scaled * u, -1, keepdims=True)
    return inverse * (scaled - first - u * second)


def col_sum(x):
    return jnp.sum(x, 0, keepdims=True)


def pair_mask(row_cut, col_cut):
    k, q = iota((128, 128), 0), iota((128, 128), 1)
    half = PAIR // 2
    win_q, win_k = q // half, k // half
    a_q, a_k = (q % half) // SLOT, (k % half) // SLOT
    b_q, b_k = q % SLOT, k % SLOT
    ok = (win_q == win_k) & (k < PAIR) & (b_k < WIN)
    cut = WIN - SHIFT
    if row_cut:
        ok &= (a_q < cut) == (a_k < cut)
    if col_cut:
        ok &= ((b_q < cut) == (b_k < cut)) | (win_q == 0)
    return jnp.where(ok, 0.0, MASKED)


def head_lanes(x, h):
    lane = iota((1, CH), 1)
    return jnp.where(lane // HD == h, x, jnp.zeros_like(x))


def spread(x):
    padded = jnp.concatenate([x, jnp.zeros((128 - PAIR, CH), x.dtype)], 0)
    return jnp.concatenate([head_lanes(padded, h) for h in range(HEADS_C)], 0)


def stacked(x):
    return jnp.concatenate([head_lanes(x, h) for h in range(HEADS_C)], 0)


def by_head(x):
    return jnp.concatenate([x[:, 128 * h : 128 * h + 128] for h in range(HEADS_C)], 0)


def rows_of(p, count=PAIR):
    return pl.ds(pl.multiple_of(p * count, 16), count)


SM_QV, SM_TABLE, SM_OUT_B, SM_UP_B, SM_DOWN_B = 0, 2, 10, 11, 15
RP_GAIN0, RP_SHIFT0, RP_GAIN, RP_SHIFT = 0, 1, 2, 4


def row_of(ref, c, first, count):
    return jnp.concatenate([ref[c, first + i : first + i + 1, :] for i in range(count)], 1)


MESH = pl.DeviceIdType.MESH
HALF = 256
PEERS = CHUNKS - 1
PLANE = 15


class Sems:
    def __init__(self):
        self.count = 0

    def take(self, n):
        self.count += n
        return self.count - n


IDS = Sems()
ID_PAGES = IDS.take(1)
ID_SMALL = IDS.take(PEERS)
ID_W = IDS.take(4 * PEERS)
ID_WF = IDS.take(4 * PEERS)
ID_WN = IDS.take(4 * PEERS * 4)
ID_COT_HALO = IDS.take(1)
ID_COT = IDS.take(PEERS)
ID_BLK = IDS.take(PEERS)
ID_BLK_HALO = IDS.take(1)
ID_CORE = IDS.take(4 * CHUNKS)
ID_CORE_M = IDS.take(1)
ID_Y = IDS.take(2 * PEERS)
ID_Y_M = IDS.take(PEERS)
ID_FIRST = IDS.take(3 * CHUNKS * PLANE)
ID_THIRD = IDS.take(3 * PEERS)
ID_BACK_Y = IDS.take(2 * PEERS)
ID_BACK = IDS.take(3 * PLANE)
ID_A = IDS.take(2 * 2 * PLANE)
ID_GC = IDS.take(6)
ID_PG = IDS.take(1)
ID_MN = IDS.take(1)
ID_SG = IDS.take(2 * (1 + 3 * PEERS))
LOCAL = 56
UNROLL = 3
QKV, OUT, UP, DOWN = 0, 1, 2, 3

EARLY = 10
SE_NORM, SE_SQ, SE_ROWS = CHUNKS * (16 - EARLY), CHUNKS * (16 - EARLY) + 8, 40
SL_NORM, SL_MERGE, SL_ROWS = CHUNKS * EARLY, CHUNKS * EARLY + 8, 64


def chunk_off(j):
    return lax.rem(3 * j, 5) - 2 * (j // 3)


def feed_off(j):
    return lax.rem(2 * j, 5) - (j // 2 - j // 3)


def back_off(j):
    return lax.rem(j + 1, CHUNKS)


def compute(
    pages_in, cot_in, merge_in, qkv_in, out_in, up_in, down_in,
    qv_in, table_in, out_b_in, up_b_in, down_b_in, gain_m_in, shift_m_in, gain_in, shift_in,
    pages_sel_in, pages_sel_t_in, table_sel_in, table_sel_t_in,
    block_o, block_halo_o, pages_o, down_o, up_o, qkv_o, out_o, merge_o, early_o, late_o,
    qv_v, table_v, out_b_v, up_b_v, down_b_v, gain_m_v, shift_m_v, gain_v, shift_v,
    pages_sel, pages_sel_t, table_sel, table_sel_t, repl,
    pages, m_htx, m_hrx, g_htx, g_hrx, mn_htx, mn_hrx, cot_v, cot_tx, cot_hf, cot_htx, cot_hrx, merge_w, qkv_w, out_w, up_w, down_w, small,
    x0, inv, mn, mt, n1, qkv, prob, att, norm, r1, u2, n2, g2,
    hid, dpre, bias, ones, unit, lmat, gsum, dqkv, g1, gz, tmp,
    blk_rx, blk_htx, blk_hrx, pg,
    d_merge, d_qkv, d_out, d_up, d_down, d_small,
    l1_qkv, l1_out, l1_up, l1_down, l1_m, l2_out, l2_down, l2_m,
    up_1, up_h, up_3, qkv_1, qkv_h, qkv_3, mb_1, mb_h, mb_3,
    ga, rxa, gf_down, gb, rxb, gfb, gf_up, gf_qkv, gf_out, mf,
    se, se_c, se_y, se_z, se_x, sl, sl_c, sl_y, sl_z, sl_x,
    ssem, rsem, lsem,
):
    chan = lax.axis_index("chan")
    space = lax.axis_index("space")
    n_space = lax.axis_size("space")
    core = lax.rem(space, 2)
    z = lax.rem(space // 2, 4)
    x = space // 8
    last_chan = chan == CHUNKS - 1
    valid = (iota((PAIR, 1), 0) % SLOT < WIN).astype(F32)

    def at_y(d):
        return (space, lax.rem(chan + d, CHUNKS))

    def at_z(d):
        return (x * 8 + lax.rem(z + d, 4) * 2 + core, chan)

    def at_x(d):
        return (lax.rem(x + d, 4) * 8 + z * 2 + core, chan)

    def at_plane(m):
        return (lax.rem(x + m // 4, 4) * 8 + lax.rem(z + m % 4, 4) * 2 + core, chan)

    def place_of(m):
        return lax.rem(x + m // 4, 4) * 4 + lax.rem(z + m % 4, 4)

    def place_before(m):
        return lax.rem(x + 4 - m // 4, 4) * 4 + lax.rem(z + 4 - m % 4, 4)

    sibling = (x * 8 + z * 2 + 1 - core, chan)
    up_band = (lax.rem(space + n_space - 1, n_space), chan)
    down_band = (lax.rem(space + 1, n_space), chan)
    rank = space * CHUNKS + chan
    n_rank = n_space * CHUNKS
    before = lax.rem(rank + n_rank - 1, n_rank)
    after = lax.rem(rank + 1, n_rank)
    up_rank = (before // CHUNKS, lax.rem(before, CHUNKS))
    down_rank = (after // CHUNKS, lax.rem(after, CHUNKS))

    def send(src, dst, n, device, into=None):
        return pltpu.make_async_remote_copy(
            src_ref=src, dst_ref=dst, send_sem=ssem.at[n], recv_sem=rsem.at[n if into is None else into],
            device_id=device, device_id_type=MESH,
        )

    def local(src, dst, n):
        return pltpu.make_async_copy(src, dst, lsem.at[n])

    own_pages = local(pages_in, pages, 0)
    own_merge = local(merge_in, merge_w, 1)
    own_w = [
        local(src, dst.at[chan], 2 + i)
        for i, (src, dst) in enumerate(((qkv_in, qkv_w), (out_in, out_w)))
    ]
    own_mlp = [
        local(src.at[pl.ds(64 * i, 64)], dst.at[chan, i // 2, i % 2], 40 + 8 * n + i)
        for n, (src, dst) in enumerate(((up_in, up_w), (down_in, down_w)))
        for i in range(8)
    ]
    own_cot = local(cot_in, cot_v, 6)
    tiny = (qv_in, table_in, out_b_in, up_b_in, down_b_in, gain_m_in, shift_m_in, gain_in, shift_in)
    tiny_v = (qv_v, table_v, out_b_v, up_b_v, down_b_v, gain_m_v, shift_m_v, gain_v, shift_v)
    tiny_copies = [local(src, dst, 24 + i) for i, (src, dst) in enumerate(zip(tiny, tiny_v))]
    tables_in = (pages_sel_in, pages_sel_t_in, table_sel_in, table_sel_t_in)
    sel_copies = [
        local(src, dst, 33 + i) for i, (src, dst) in enumerate(zip(tables_in, (pages_sel, pages_sel_t, table_sel, table_sel_t)))
    ]
    for copy in tiny_copies + sel_copies[0:1] + [own_pages, own_cot, own_merge, sel_copies[3], own_w[QKV]]:
        copy.start()
    for copy in [own_w[OUT]] + own_mlp + [sel_copies[1], sel_copies[2]]:
        copy.start()

    barrier = pltpu.get_barrier_semaphore()
    greeted = [at_y(d) for d in (1, 2, 3)] + [at_plane(m) for m in range(1, PLANE + 1)]
    greeted += [sibling, up_band, down_band, up_rank, down_rank]
    for by in (1, 3):
        greeted.append((lax.rem(x + by, 4) * 8 + z * 2 + 1 - core, chan))
        greeted.append((x * 8 + lax.rem(z + by, 4) * 2 + 1 - core, chan))
    for device in greeted:
        pl.semaphore_signal(barrier, inc=1, device_id=device, device_id_type=MESH)

    for copy in tiny_copies:
        copy.wait()
    lane_rows = lambda ref, n: ref[...].astype(F32).reshape(1, n)
    small[chan, SM_QV : SM_QV + 2, :] = qv_v[...].astype(F32)
    table = table_v[...].astype(F32)
    small[chan, SM_TABLE : SM_TABLE + 4, :] = table[:, 0:128]
    small[chan, SM_TABLE + 4 : SM_TABLE + 8, :] = jnp.concatenate([table[:, 128:169], jnp.zeros((4, 87), F32)], 1)
    small[chan, SM_OUT_B : SM_OUT_B + 1, :] = lane_rows(out_b_v, 128)
    up_row = lane_rows(up_b_v, 512)
    for i in range(4):
        small[chan, SM_UP_B + i : SM_UP_B + i + 1, :] = up_row[:, i * 128 : i * 128 + 128]
    small[chan, SM_DOWN_B : SM_DOWN_B + 1, :] = lane_rows(down_b_v, 128)
    repl[RP_GAIN0 : RP_GAIN0 + 1, :] = lane_rows(gain_m_v, 1024)
    repl[RP_SHIFT0 : RP_SHIFT0 + 1, :] = lane_rows(shift_m_v, 1024)
    repl[RP_GAIN : RP_GAIN + 2, 0:D] = gain_v[...].astype(F32)
    repl[RP_SHIFT : RP_SHIFT + 2, 0:D] = shift_v[...].astype(F32)
    pl.semaphore_wait(barrier, len(greeted))

    halves = (HALF, CH // 2, HALF, HALF)
    weights = (qkv_w, out_w, up_w, down_w)
    sources = (qkv_in, out_in, up_in, down_in)

    def axis_of(w):
        return (x, lambda d, k: (lax.rem(x + d, 4) * 8 + z * 2 + k, chan)) if w in (QKV, UP) else (
            z, lambda d, k: (x * 8 + lax.rem(z + d, 4) * 2 + k, chan)
        )

    def rows_in(ref, w, first, n, c=None):
        rows = pl.ds(pl.multiple_of(first, 16), n)
        if c is None:
            return ref.at[:, rows] if w == QKV else ref.at[rows]
        return ref.at[c, :, rows] if w == QKV else ref.at[c, rows]

    def quarter(w, k):
        return lax.rem(axis_of(w)[0], 2) * halves[w] + k * (halves[w] // 2)

    def weight_copy(w, d):
        n = halves[w] // 2
        src = rows_in(sources[w], w, quarter(w, core), n)
        return send(src, rows_in(weights[w], w, quarter(w, core), n, chan), ID_W + w * PEERS + d - 1, at_y(d))

    def arrived(w, d, c):
        part = rows_in(weights[w], w, quarter(w, core), halves[w] // 2, c)
        send(part, part, ID_W + w * PEERS + d - 1, at_y(d)).wait_recv()

    def forward_copies(w, d, c):
        part = rows_in(weights[w], w, quarter(w, core), halves[w] // 2, c)
        yield send(part, part, ID_WF + w * PEERS + d - 1, sibling)
        n = halves[w] // 4
        base = ID_WN + (w * PEERS + d - 1) * 4
        for i, by in enumerate((1, 3)):
            part = rows_in(weights[w], w, quarter(w, core) + i * n, n, c)
            for same in range(2):
                device = axis_of(w)[1](by, core if same else 1 - core)
                yield send(part, part, base + i * 2 + same, device, base + i * 2 + core)

    def forwarded(w, d, c):
        part = rows_in(weights[w], w, quarter(w, 1 - core), halves[w] // 2, c)
        send(part, part, ID_WF + w * PEERS + d - 1, sibling).wait_recv()
        n = halves[w] // 4
        base = ID_WN + (w * PEERS + d - 1) * 4
        half = (1 - lax.rem(axis_of(w)[0], 2)) * halves[w]
        for i in range(2):
            for k in range(2):
                part = rows_in(weights[w], w, half + (k * 2 + i) * n, n, c)
                send(part, part, base + i * 2 + k, sibling).wait_recv()

    fourth = lax.rem(x + 2 * z, 4)

    def eighth_copy(w, d):
        part = weights[w].at[chan, fourth, core]
        src = sources[w].at[pl.ds(pl.multiple_of(fourth * 128 + core * 64, 64), 64)]
        return send(src, part, ID_W + w * PEERS + d - 1, at_y(d))

    def around_copies(w, d, c):
        part = weights[w].at[c, fourth, core]
        base = ID_WN + (w * PEERS + d - 1) * 4
        yield send(part, part, base, at_x(1))
        yield send(part, part, base + 1, at_x(3))
        for i, by in enumerate((1, 3)):
            half = part.at[pl.ds(32 * i, 32)]
            yield send(half, half, base + 2 + i, at_z(by))

    def across_copy(w, d, c):
        part = weights[w].at[c, :, core]
        return send(part, part, ID_WF + w * PEERS + d - 1, sibling)

    def chunk_peer(j):
        off = feed_off(j)
        return CHUNKS - off, lax.rem(chan + off, CHUNKS)

    def pass_around(w, j):
        d, c = chunk_peer(j)
        part = weights[w].at[c, fourth, core]
        send(part, part, ID_W + w * PEERS + d - 1, at_y(d)).wait_recv()
        for copy in around_copies(w, d, c):
            copy.start()

    def pass_across(w, j):
        d, c = chunk_peer(j)
        base = ID_WN + (w * PEERS + d - 1) * 4
        for i, by in enumerate((3, 1)):
            part = weights[w].at[c, lax.rem(fourth + by, 4), core]
            send(part, part, base + i, sibling).wait_recv()
        for i in range(2):
            part = weights[w].at[c, lax.rem(fourth + 2, 4), core, pl.ds(32 * i, 32)]
            send(part, part, base + 2 + i, sibling).wait_recv()
        across_copy(w, d, c).start()

    def have_across(w, j):
        d, c = chunk_peer(j)
        part = weights[w].at[c, :, 1 - core]
        send(part, part, ID_WF + w * PEERS + d - 1, sibling).wait_recv()

    def pass_on(w, j):
        off = chunk_off(j)
        c, d = lax.rem(chan + off, CHUNKS), CHUNKS - off
        arrived(w, d, c)
        for copy in forward_copies(w, d, c):
            copy.start()

    def have(w, j):
        off = chunk_off(j)
        forwarded(w, CHUNKS - off, lax.rem(chan + off, CHUNKS))

    small_copies = [send(small.at[chan], small.at[chan], ID_SMALL + d - 1, at_y(d)) for d in (1, 3, 2)]
    weight_copies = [[(weight_copy if w in (QKV, OUT) else eighth_copy)(w, d) for d in (1, 3, 2)] for w in range(4)]
    for copy in small_copies + weight_copies[QKV][0:1]:
        copy.start()

    def quads(i, _):
        base = (i // WIN) * BAND + lax.rem(i, WIN) * SLOT
        for q in range(2):
            y = dot(pages_sel[...], pages[lax.rem(2 * i + q + LIFT, 2 * ROWS)])
            for par in range(2):
                for wc in range(WC):
                    lanes = par * 512 + q * 256
                    at = pl.multiple_of(base + wc * WIN * SLOT, SLOT)
                    first = par * WC * SLOT + wc * SLOT
                    tmp[pl.ds(at, SLOT), lanes : lanes + 256] = y[first : first + SLOT]
        return 0

    own_pages.wait()
    sel_copies[0].wait()
    gain = [repl[RP_GAIN + i : RP_GAIN + i + 1, 0:D] for i in range(2)]
    shift = [repl[RP_SHIFT + i : RP_SHIFT + i + 1, 0:D] for i in range(2)]
    three = range(NPAIR // 2)
    cut_rows = WIN - SHIFT
    n_halo = SHIFT * SLOT

    def pair_rows(half, i):
        return slice(half * BAND + i * PAIR, half * BAND + i * PAIR + PAIR)

    def band(half):
        return slice(half * BAND, half * BAND + BAND)

    def merge_rows(half):
        lax.fori_loop(half * WIN, half * WIN + WIN, quads, 0)
        for i in three:
            r = pair_rows(half, i)
            u, inverse = unit_of(tmp[r, :])
            x0[r, :] = u.astype(BF16)
            inv[r, 0:1] = inverse
            mn[r, :] = (u * repl[RP_GAIN0 : RP_GAIN0 + 1, :] + repl[RP_SHIFT0 : RP_SHIFT0 + 1, :]).astype(BF16)
        return dot(mn[band(half), :], merge_w[...])

    def norm1(half):
        for i in three:
            r = pair_rows(half, i)
            u, _inverse = unit_of(mt[r, :].astype(F32))
            n1[r, :] = (u * gain[0] + shift[0]).astype(BF16)

    def halo_of(rows):
        starts = [wc * WIN * SLOT + cut_rows * SLOT for wc in range(WC)]
        return jnp.concatenate([rows[at : at + n_halo] for at in starts], 0)

    def with_halo(rows, halo):
        parts = []
        for wc in range(WC):
            at = wc * WIN * SLOT
            parts += [rows[at : at + cut_rows * SLOT], halo[wc * n_halo : wc * n_halo + n_halo]]
        return jnp.concatenate(parts, 0)

    own_merge.wait()
    merged_last = merge_rows(1)
    mt[band(1), :] = merged_last.astype(BF16)
    m_htx[...] = halo_of(merged_last).astype(BF16)
    merged_halo = send(m_htx, m_hrx, ID_PAGES, up_rank)
    merged_halo.start()
    for copy in weight_copies[QKV][1:] + weight_copies[OUT]:
        copy.start()
    for i in (2, 0, 1):
        for w in (UP, DOWN):
            weight_copies[w][i].start()
    mt[band(0), :] = merge_rows(0).astype(BF16)
    norm1(0)

    own_cot.wait()
    norm[...] = jnp.zeros_like(norm)
    cot_hf[...] = jnp.zeros_like(cot_hf)
    for wc in range(WC):
        for b in range(WIN):
            column = cot_v[(wc * WIN + b + SHIFT) % COLS].astype(F32)
            cot_hf[pl.ds(wc * SHIFT * SLOT + b, SHIFT, stride=SLOT), :] = column[0:SHIFT]
            for m in range(4 * ROWS // WIN):
                c, wr = m // 2, m % 2
                n = cut_rows if m == 4 * ROWS // WIN - 1 else WIN
                slot = wr * BAND + wc * WIN * SLOT + b
                norm[c, pl.ds(slot, n, stride=SLOT), :] = column[SHIFT + WIN * m : SHIFT + WIN * m + n]
    cot_htx[...] = cot_hf[...].astype(BF16)
    cot_halo = send(cot_htx, cot_hrx, ID_COT_HALO, up_band)
    cot_halo.start()

    sel_copies[3].wait()
    for d in (1, 2, 3):
        part = small.at[lax.rem(chan + CHUNKS - d, CHUNKS)]
        send(part, part, ID_SMALL + d - 1, at_y(d)).wait_recv()
    lmat[...] = jnp.zeros_like(lmat)
    masks = [pair_mask(kind // 2, kind % 2) for kind in range(4)]
    for h in range(HEADS_C):
        lanes = jnp.where(iota((128, CH), 1) // HD == h, 1.0, 0.0)
        ones[h * 128 : h * 128 + 128, :] = lanes.astype(BF16)
    unit[...] = jnp.where(iota((PAIR, 128), 0) == iota((PAIR, 128), 1), 1.0, 0.0).astype(BF16)

    def tables(c, _):
        table = jnp.concatenate([small[c, SM_TABLE : SM_TABLE + 4, :], small[c, SM_TABLE + 4 : SM_TABLE + 8, :]], 1)
        table = jnp.concatenate([table, jnp.zeros_like(table)], 0).astype(BF16)
        placed = dot(table, table_sel_t[...])
        for b_k in range(WIN):
            for h in range(HEADS_C):
                lmat[h * SLOT + b_k : h * SLOT + b_k + 1, :] = placed[h : h + 1, b_k * 128 : b_k * 128 + 128]
        for h in range(HEADS_C):
            tab = lmat[h * SLOT : h * SLOT + SLOT, :]
            lane = iota((SLOT, 128), 1)
            slabs = []
            for a in range(WIN):
                moved = pltpu.roll(tab, (128 - (WIN - 1 - a) * SLOT) % 128, 1) if a < WIN - 1 else tab
                low = jnp.where(lane < WIN * SLOT, moved, 0.0)
                slabs.append(low + pltpu.roll(low, WIN * SLOT, 1))
            one = jnp.concatenate(slabs * 2 + [jnp.zeros((128 - PAIR, 128), F32)], 0)
            for kind in range(4):
                bias[kind, c, h * 128 : h * 128 + 128, :] = (one + masks[kind]).astype(BF16)
        return 0

    lax.fori_loop(0, CHUNKS, tables, 0)

    pass_on(QKV, 1)
    merged_halo.wait_recv()
    mt[band(1), :] = with_halo(mt[band(1), :].astype(F32), m_hrx[...].astype(F32)).astype(BF16)
    norm1(1)
    pass_on(QKV, 2)

    cot_halo.wait_recv()
    norm[PEERS, BAND:T, :] = with_halo(norm[PEERS, BAND:T, :], cot_hrx[...].astype(F32))
    cot_tx[...] = norm[...].astype(BF16)
    lanes_here = pl.ds(pl.multiple_of(chan * CH, CH), CH)
    cot_copies = [
        send(cot_tx.at[lax.rem(chan + d, CHUNKS)], g2.at[:, lanes_here], ID_COT + d - 1, at_y(d)) for d in (1, 3, 2)
    ]
    for copy in cot_copies:
        copy.start()
    g2[:, lanes_here] = cot_tx[chan]

    mn_htx[...] = halo_of(mn[band(1), :].astype(F32)).astype(BF16)
    normed_halo = send(mn_htx, mn_hrx, ID_MN, up_rank)
    normed_halo.start()

    def wide(c):
        return jnp.concatenate([qkv_w[c, i] for i in range(3)], 1)

    own_w[QKV].wait()

    def attend(j, _):
        c = lax.rem(chan + chunk_off(j), CHUNKS)
        heads = pl.ds(pl.multiple_of(c * CH, CH), CH)

        @pl.when(j > 0)
        def _():
            have(QKV, j)

        projected = dot(n1[...], wide(c))
        zeros = jnp.zeros((1, CH), F32)
        offset = jnp.concatenate([small[c, SM_QV : SM_QV + 1, :], zeros, small[c, SM_QV + 1 : SM_QV + 2, :]], 1)
        scaled = jnp.concatenate([jnp.full((1, CH), SCALE, F32), jnp.ones((1, 2 * CH), F32)], 1)
        qkv[c] = ((projected + offset) * scaled).astype(BF16)

        @pl.when(j == 0)
        def _():
            pass_on(QKV, 3)

        def window_pairs(t, _):
            pairs = [UNROLL * t + i for i in range(UNROLL)]
            parts = [[qkv[c, rows_of(p), i * CH : i * CH + CH] for i in range(3)] for p in pairs]
            results = []
            for i, (q, k, v) in enumerate(parts):
                table = bias[2 * (chan // PEERS) * t + i // (UNROLL - 1), c]
                s = dot_nt(jnp.concatenate([q, unit[...]], 1), jnp.concatenate([spread(k), table], 1))
                weights = []
                for h in range(HEADS_C):
                    sh = s[:, 128 * h : 128 * h + 128]
                    weights.append(jnp.exp(sh - jnp.max(sh, -1, keepdims=True)).astype(BF16))
                w = jnp.concatenate(weights, 1)
                o = dot(w, jnp.concatenate([spread(v), ones[...]], 1))
                inverse = 1.0 / o[:, CH:]
                results.append((w, o[:, 0:CH] * inverse, inverse))
            for p, (w, o, inverse) in zip(pairs, results):
                prob[c, p] = w
                att[rows_of(p), heads] = o.astype(BF16)
                norm[c, rows_of(p), :] = inverse
            return 0

        lax.fori_loop(0, NPAIR // UNROLL, window_pairs, 0)

        @pl.when(j == 1)
        def _():
            for i in range(1, CHUNKS):
                pass_on(OUT, i)
            for w in (UP, DOWN):
                pass_around(w, 1)

        @pl.when(j == 2)
        def _():
            for w in (UP, DOWN):
                pass_around(w, 2)

        @pl.when(j == 3)
        def _():
            for w in (UP, DOWN):
                pass_around(w, 3)
                pass_across(w, 1)

        return 0

    lax.fori_loop(0, CHUNKS, attend, 0)

    own_w[OUT].wait()
    for j in range(1, CHUNKS):
        have(OUT, j)
    tmp[:, 0:D] = dot(att[...], out_w[...].reshape(D, D))
    out_b = jnp.concatenate([small[c, SM_OUT_B : SM_OUT_B + 1, :] for c in range(CHUNKS)], 1)
    down_b = jnp.concatenate([small[c, SM_DOWN_B : SM_DOWN_B + 1, :] for c in range(CHUNKS)], 1)

    def norm2(half):
        total = 0.0
        for i in three:
            r = pair_rows(half, i)
            branch = tmp[r, 0:D] + out_b
            resid = mt[r, :].astype(F32) + branch
            r1[r, :] = resid
            u, inverse = unit_of(resid.astype(BF16).astype(F32))
            u2[r, :] = u.astype(BF16)
            inv[r, 1:2] = inverse
            n2[r, :] = (u * gain[1] + shift[1]).astype(BF16)
            total = total + col_sum(branch * branch * valid)
        return total

    sq_one = norm2(0) + norm2(1)
    for w in (UP, DOWN):
        pass_across(w, 2)

    for d in (1, 2, 3):
        part = g2.at[:, pl.ds(pl.multiple_of(lax.rem(chan + CHUNKS - d, CHUNKS) * CH, CH), CH)]
        send(part, part, ID_COT + d - 1, at_y(d)).wait_recv()

    grads = (d_qkv, d_out, d_up, d_down)
    firsts = (l1_qkv, l1_out, l1_up, l1_down)
    order = (1, 3, 2)
    around = range(1, PLANE + 1)
    here = x * 4 + z

    def step(n, lead=0):
        return pl.ds(pl.multiple_of(lead, 16), n)

    def half_grad(w, c, k):
        return grads[w].at[c, step(halves[w], k * halves[w])]

    def core_copy(w, j, c):
        return send(half_grad(w, c, 1 - core), firsts[w].at[j], ID_CORE + w * CHUNKS + j, sibling)

    def core_sum(w, j, off):
        c = lax.rem(chan + off, CHUNKS)
        core_copy(w, j, c).wait_recv()
        size = min(halves[w], 64)
        for t in range(0, halves[w], size):
            r = step(size, core * halves[w] + t)
            total = grads[w][c, r, :].astype(F32) + firsts[w][j, t : t + size, :].astype(F32)
            grads[w][c, r, :] = total.astype(BF16)

    owners = {DOWN: (0, l2_down), OUT: (1, l2_out)}

    def owner_copy(w, off):
        n, into = owners[w]
        c = lax.rem(chan + off, CHUNKS)
        return send(half_grad(w, c, core), into.at[off - 1], ID_Y + n * PEERS + off - 1, at_y(off))

    def to_owner(w, off):
        @pl.when(off > 0)
        def _():
            owner_copy(w, off).start()

    def owner_wait(w):
        n, into = owners[w]
        for d in order:
            send(into.at[d - 1], into.at[d - 1], ID_Y + n * PEERS + d - 1, at_y(d)).wait_recv()

    def owner_sum(w, t, size):
        total = grads[w][chan, step(size, core * halves[w] + t), :].astype(F32)
        for d in range(PEERS):
            total += owners[w][1][d, t : t + size, :].astype(F32)
        return total.astype(BF16)

    class Plane:
        def __init__(self, n, g, rx, gf):
            self.n, self.g, self.rx, self.gf = n, g, rx, gf

        def out_copies(self):
            for m in around:
                src = self.g.at[step(16, place_of(m) * 16)]
                yield send(src, self.rx.at[m - 1], ID_A + self.n * 2 * PLANE + m - 1, at_plane(m))

        def back_copies(self, wait):
            for m in around:
                part = self.gf.at[core, step(16, (place_before(m) if wait else here) * 16)]
                yield send(part, part, ID_A + (self.n * 2 + 1) * PLANE + m - 1, at_plane(m))

        def start(self):
            for copy in self.out_copies():
                copy.start()

        def back_start(self):
            for copy in self.out_copies():
                copy.wait_recv()
            total = self.g[step(16, here * 16), :].astype(F32)
            for m in around:
                total += self.rx[m - 1].astype(F32)
            self.gf[core, step(16, here * 16), :] = total.astype(BF16)
            for copy in self.back_copies(False):
                copy.start()

        def finish(self):
            for copy in self.back_copies(True):
                copy.wait_recv()

        def left(self):
            for copy in [*self.out_copies(), *self.back_copies(False)]:
                copy.wait_send()

    plane_a = Plane(0, ga, rxa, gf_down)
    plane_b = Plane(1, gb, rxb, gfb)

    class Spread:
        def __init__(self, n, src, first, h, third, into):
            self.n, self.src, self.first, self.h, self.third, self.into = n, src, first, h, third, into

        def first_copies(self, j, c):
            for m in around:
                src = self.src(c, place_of(m) * 16, 16)
                n = ID_FIRST + (self.n * CHUNKS + j) * PLANE + m - 1
                yield send(src, self.first.at[c, m - 1], n, at_plane(m))

        def first_start(self, j, c):
            for copy in self.first_copies(j, c):
                copy.start()

        def third_copies(self):
            for d in order:
                src = self.h.at[lax.rem(chan + d, CHUNKS)]
                yield send(src, self.third.at[d - 1], ID_THIRD + self.n * PEERS + d - 1, at_y(d))

        def third_start(self, chunk_of):
            for j in range(CHUNKS):
                c = chunk_of(j)
                for copy in self.first_copies(j, c):
                    copy.wait_recv()
                total = self.src(c, here * 16, 16)[...].astype(F32)
                for m in around:
                    total += self.first[c, m - 1].astype(F32)
                self.h[c] = total.astype(BF16)
            for copy in self.third_copies():
                copy.start()

        def third_sum(self):
            for copy in self.third_copies():
                copy.wait_recv()
            total = self.h[chan].astype(F32)
            for d in range(PEERS):
                total += self.third[d].astype(F32)
            self.into(chan, here * 16, 16)[...] = total.astype(BF16)

        def back_y(self, wait):
            for d in order:
                part = self.into(lax.rem(chan + (CHUNKS - d if wait else 0), CHUNKS), here * 16, 16)
                yield send(part, part, ID_BACK_Y + d - 1, at_y(d))

        def back_copies(self, wait):
            for m in around:
                part = self.into(None, (place_before(m) if wait else here) * 16, 16)
                yield send(part, part, ID_BACK + self.n * PLANE + m - 1, at_plane(m))

        def back_start(self):
            for copy in self.back_copies(False):
                copy.start()

        def finish(self):
            for copy in self.back_copies(True):
                copy.wait_recv()

        def left(self, chunk_of):
            for j in range(CHUNKS):
                for copy in self.first_copies(j, chunk_of(j)):
                    copy.wait_send()
            for copy in [*self.third_copies(), *self.back_copies(False)]:
                copy.wait_send()

    def half_rows(w):
        return lambda c, row, n: grads[w].at[c, step(n, core * halves[w] + row)]

    group_a, group_b = 2 * core, 2 * core + 1
    spread_up = Spread(0, half_rows(UP), up_1, up_h, up_3, lambda c, row, n: gf_up.at[core, step(n, row)])
    spread_qkv = Spread(1, half_rows(QKV), qkv_1, qkv_h, qkv_3, lambda c, row, n: gf_qkv.at[core, step(n, row)])
    spread_m = Spread(
        2, lambda c, row, n: d_merge.at[group_b, c, step(n, row)], mb_1, mb_h, mb_3,
        lambda c, row, n: mf.at[group_b, slice(None) if c is None else c, step(n, row)],
    )

    def core_out(n, part):
        return send(part, part, ID_GC + n, sibling)

    def feed_chunk(j):
        return lax.rem(chan + feed_off(j), CHUNKS)

    def back_chunk(j):
        return lax.rem(chan + back_off(j), CHUNKS)

    def feed_sums(j):
        core_sum(DOWN, j, feed_off(j))
        to_owner(DOWN, feed_off(j))
        core_sum(UP, j, feed_off(j))
        spread_up.first_start(j, feed_chunk(j))

    def back_sums(j):
        core_sum(OUT, j, back_off(j))
        to_owner(OUT, back_off(j))
        core_sum(QKV, j, back_off(j))
        spread_qkv.first_start(j, back_chunk(j))

    class Small:
        def __init__(self, n, own, into):
            self.n, self.own, self.into = n, own, into

        def copies(self, level):
            base = ID_SG + self.n * (1 + 3 * PEERS)
            if level == 0:
                return [send(self.own.at[0], self.into[0].at[0], base, sibling)]
            at = (at_y, at_z, at_x)[level - 1]
            base += (level - 1) * PEERS
            return [send(self.own.at[level], self.into[level].at[d - 1], base + d, at(d)) for d in order]

        def start(self, level):
            for copy in self.copies(level):
                copy.start()

        def sum(self, level):
            for copy in self.copies(level):
                copy.wait_recv()
            total = self.own[level]
            for d in range(self.into[level].shape[0]):
                total += self.into[level][d]
            self.own[level + 1] = total

    small_early = Small(0, se, (se_c, se_y, se_z, se_x))
    small_late = Small(1, sl, (sl_c, sl_y, sl_z, sl_x))

    def lay(ref, at, row):
        for i in range(row.shape[1] // 128):
            ref[0, at + i : at + i + 1, :] = row[:, i * 128 : i * 128 + 128]

    tmp[...] = jnp.zeros_like(tmp)
    for copy in own_mlp:
        copy.wait()

    def feed(j, _):
        c = feed_chunk(j)

        @pl.when(j > 0)
        def _():
            have_across(UP, j)
            have_across(DOWN, j)

        @pl.when(j == 0)
        def _():
            for w in (UP, DOWN):
                pass_across(w, 3)

        up_c, down_c = up_w[c].reshape(D, 512), down_w[c].reshape(512, D)
        up_b = row_of(small, c, SM_UP_B, 4)
        d_up_b = 0.0
        for first in range(0, T, T // 3):
            r = slice(first, first + T // 3)
            value, slope = gelu_parts(dot(n2[r, :], up_c) + up_b)
            hid[r, :] = value.astype(BF16)
            d = slope * dot_nt(g2[r, :], down_c)
            dpre[r, :] = d.astype(BF16)
            d_up_b = d_up_b + col_sum(d)
        for i in range(4):
            d_small[c, SM_UP_B + i : SM_UP_B + i + 1, :] = d_up_b[:, i * 128 : i * 128 + 128]
        d_down[c] = dot_tn(hid[...], g2[...]).astype(BF16)
        core_copy(DOWN, j, c).start()
        d_up[c] = dot_tn(n2[...], dpre[...]).astype(BF16)
        core_copy(UP, j, c).start()
        tmp[:, 0:D] += dot(hid[...], down_c)
        tmp[:, D : 2 * D] += dot_nt(dpre[...], up_c)

        feed_sums(j)
        return 0

    lax.fori_loop(0, CHUNKS, feed, 0)

    for copy in [cot_halo] + cot_copies:
        copy.wait_send()
    blk_tx = cot_tx
    def norm2_back(half):
        totals = [0.0] * 6
        for i in three:
            r = pair_rows(half, i)
            branch = tmp[r, 0:D] + down_b
            result = r1[r, :] + branch
            for c in range(CHUNKS):
                blk_tx[c, r, :] = result[:, c * CH : c * CH + CH].astype(BF16)
            u = u2[r, :].astype(F32)
            dy = tmp[r, D : 2 * D]
            g = g2[r, :].astype(F32)
            grad = g + norm_back(dy, u, inv[r, 1:2], gain[1])
            tmp[r, 0:D] = grad
            g1[r, :] = grad.astype(BF16)
            terms = (branch * branch * valid, result * result * valid, g, dy * u, dy, grad)
            totals = [total + col_sum(term) for total, term in zip(totals, terms)]
        return totals

    sq_two, sq_out, d_down_b, d_gain1, d_shift1, d_out_b = (a + b for a, b in zip(norm2_back(0), norm2_back(1)))
    for c in range(CHUNKS):
        d_small[c, SM_DOWN_B : SM_DOWN_B + 1, :] = d_down_b[:, c * CH : c * CH + CH]
        d_small[c, SM_OUT_B : SM_OUT_B + 1, :] = d_out_b[:, c * CH : c * CH + CH]

    for c in range(CHUNKS):
        se[0, c * 6 : c * 6 + 6, :] = d_small[c, EARLY:16, :]
    lay(se, SE_NORM, d_gain1)
    lay(se, SE_NORM + 4, d_shift1)
    squares = [sum(sq[:, i * 128 : i * 128 + 128] for i in range(4)) for sq in (sq_out, sq_one, sq_two)]
    se[0, SE_SQ:SE_ROWS, :] = jnp.concatenate(squares + [jnp.zeros((5, 128), F32)], 0)
    small_early.start(0)

    blk_copies = [
        send(blk_tx.at[lax.rem(chan + d, CHUNKS)], blk_rx.at[chan], ID_BLK + d - 1, at_y(d)) for d in (1, 3, 2)
    ]
    blk_rx[chan] = blk_tx[chan]

    normed_halo.wait_recv()
    mn[band(1), :] = with_halo(mn[band(1), :].astype(F32), mn_hrx[...].astype(F32)).astype(BF16)

    sel_copies[2].wait()
    d_out[...] = dot_tn(att[...], g1[...]).astype(BF16).reshape(CHUNKS, CH, D)
    hid[...] = dot_nt(g1[...], out_w[...].reshape(D, D)).astype(BF16)

    def attend_back(j, _):
        c = lax.rem(chan + back_off(j), CHUNKS)
        heads = pl.ds(pl.multiple_of(c * CH, CH), CH)
        core_copy(OUT, j, c).start()
        gsum[...] = jnp.zeros_like(gsum)

        def window_pairs(t, _):
            pairs = [UNROLL * t + i for i in range(UNROLL)]
            parts = [[qkv[c, rows_of(p), i * CH : i * CH + CH] for i in range(3)] for p in pairs]
            d_atts = [hid[rows_of(p), heads].astype(F32) * norm[c, rows_of(p), :] for p in pairs]
            outs = [att[rows_of(p), heads] for p in pairs]
            probs = [prob[c, p] for p in pairs]
            results, total = [], 0.0
            for (q, k, v), d_att, o, w in zip(parts, d_atts, outs, probs):
                left = jnp.concatenate([d_att, -d_att * o.astype(F32)], 1).astype(BF16)
                d_s = w.astype(F32) * dot_nt(left, jnp.concatenate([spread(v), ones[...]], 1))
                total = total + d_s
                d_s = d_s.astype(BF16)
                d_q = dot(d_s, spread(k)) * SCALE
                d_k = dot_tn(by_head(d_s), stacked(q))[0:PAIR]
                d_v = dot_tn(by_head(w), stacked(left[:, 0:CH]))[0:PAIR]
                results.append(jnp.concatenate([d_q, d_k, d_v], 1).astype(BF16))
            for p, result in zip(pairs, results):
                dqkv[c, rows_of(p), :] = result
            gsum[...] += total
            return 0

        lax.fori_loop(0, NPAIR // UNROLL, window_pairs, 0)
        d_qkv[c] = dot_tn(n1[...], dqkv[c]).astype(BF16)
        core_copy(QKV, j, c).start()

        def sums(p, total):
            return total + col_sum(dqkv[c, rows_of(p), :].astype(F32))

        total = lax.fori_loop(0, NPAIR, sums, jnp.zeros((1, 3 * CH), F32))
        d_small[c, SM_QV : SM_QV + 1, :] = total[:, 0:CH]
        d_small[c, SM_QV + 1 : SM_QV + 2, :] = total[:, 2 * CH : 3 * CH]

        half = WIN * SLOT
        for h in range(HEADS_C):
            lanes = slice(h * 128, h * 128 + 128)
            folded = gsum[0:half, lanes] + pltpu.roll(gsum[half:PAIR, lanes], 128 - half, 1)
            acc = jnp.zeros((SLOT, 128), F32)
            for a in range(WIN):
                slab = folded[a * SLOT : a * SLOT + SLOT]
                moved = (WIN - 1 - a) * SLOT
                acc += pltpu.roll(slab, moved, 1) if moved else slab
            lmat[h * SLOT : h * SLOT + SLOT, :] = acc
        d_table = jnp.zeros((SLOT, 256), F32)
        for b_q in range(WIN):
            rows = [lmat[h * SLOT + b_q : h * SLOT + b_q + 1, :] for h in range(HEADS_C)]
            rows = jnp.concatenate(rows + [jnp.zeros((SLOT - HEADS_C, 128), F32)], 0)
            d_table += dot_nt(rows.astype(BF16), table_sel[:, b_q * 128 : b_q * 128 + 128])
        d_small[c, SM_TABLE : SM_TABLE + 4, :] = d_table[0:4, 0:128]
        d_small[c, SM_TABLE + 4 : SM_TABLE + 8, :] = d_table[0:4, 128:256]

        @pl.when(j > 0)
        def _():
            back_sums(j - 1)

        @pl.when(j == 0)
        def _():
            small_early.sum(0)
            small_early.start(1)

        @pl.when(j == 1)
        def _():
            owner_wait(DOWN)
            for t in range(0, HALF, 64):
                ga[t : t + 64, :] = owner_sum(DOWN, t, 64)
            plane_a.start()
            spread_up.third_start(feed_chunk)
            for copy in blk_copies:
                copy.start()

        @pl.when(j == 2)
        def _():
            small_early.sum(1)
            small_early.start(2)

        @pl.when(j == 3)
        def _():
            plane_a.back_start()
            spread_up.third_sum()
            spread_up.back_start()

        return 0

    lax.fori_loop(0, CHUNKS, attend_back, 0)

    def norm1_back(half):
        rows = band(half)
        tmp[rows, D : 2 * D] = sum(dot_nt(dqkv[c, rows, :], wide(c)) for c in range(CHUNKS))
        d_gain, d_shift = 0.0, 0.0
        for i in three:
            r = pair_rows(half, i)
            u, inverse = unit_of(mt[r, :].astype(F32))
            dy = tmp[r, D : 2 * D]
            gz[r, :] = (tmp[r, 0:D] + norm_back(dy, u, inverse, gain[0])).astype(BF16)
            d_gain, d_shift = d_gain + col_sum(dy * u), d_shift + col_sum(dy)
        return d_gain, d_shift

    d_gain0, d_shift0 = norm1_back(1)
    g_htx[...] = halo_of(gz[band(1), :].astype(F32)).astype(BF16)
    grad_halo = send(g_htx, g_hrx, ID_PG, down_rank)
    grad_halo.start()
    more_gain, more_shift = norm1_back(0)
    d_gain0, d_shift0 = d_gain0 + more_gain, d_shift0 + more_shift
    back_sums(PEERS)

    merge_core = send(d_merge.at[pl.ds(2 - 2 * core, 2)], l1_m, ID_CORE_M, sibling)

    def merge_grad(k):
        lanes = pl.ds(pl.multiple_of(k * HALF, HALF), HALF)
        total = dot_tn(mn[...], gz[:, lanes]).astype(BF16)
        for i in range(2):
            d_merge[2 * k + i] = total[:, i * 128 : i * 128 + 128].reshape(CHUNKS, HALF, 128)

    merge_grad(1 - core)
    merge_core.start()
    merge_grad(core)
    small_early.sum(2)
    small_early.start(3)

    for d in (1, 2, 3):
        part = blk_rx.at[lax.rem(chan + CHUNKS - d, CHUNKS)]
        send(part, part, ID_BLK + d - 1, at_y(d)).wait_recv()
    blk_htx[...] = halo_of(blk_rx[PEERS, BAND:T, :].astype(F32)).astype(BF16)
    blk_halo = send(blk_htx, blk_hrx, ID_BLK_HALO, down_band)
    blk_halo.start()

    merge_core.wait_recv()
    for i in range(2):
        for c in range(CHUNKS):
            total = d_merge[2 * core + i, c].astype(F32) + l1_m[i, c].astype(F32)
            d_merge[2 * core + i, c] = total.astype(BF16)

    def merge_owner(d):
        return send(d_merge.at[group_a, lax.rem(chan + d, CHUNKS)], l2_m.at[d - 1], ID_Y_M + d - 1, at_y(d))

    for d in order:
        merge_owner(d).start()
    for c in range(CHUNKS):
        spread_m.first_start(c, c)
    spread_qkv.third_start(back_chunk)

    grad_halo.wait_recv()
    gz[band(1), :] = with_halo(gz[band(1), :].astype(F32), g_hrx[...].astype(F32)).astype(BF16)
    sel_copies[1].wait()
    tmp[...] = dot_nt(gz[...], merge_w[...])
    d_gain_m, d_shift_m = 0.0, 0.0
    for half in range(2):
        for i in three:
            r = pair_rows(half, i)
            u = x0[r, :].astype(F32)
            dy = tmp[r, :]
            tmp[r, :] = norm_back(dy, u, inv[r, 0:1], repl[RP_GAIN0 : RP_GAIN0 + 1, :])
            d_gain_m, d_shift_m = d_gain_m + col_sum(dy * u), d_shift_m + col_sum(dy)

    for c in range(CHUNKS):
        sl[0, EARLY * c : EARLY * c + EARLY, :] = d_small[c, 0:EARLY, :]
    lay(sl, SL_NORM, d_gain0)
    lay(sl, SL_NORM + 4, d_shift0)
    lay(sl, SL_MERGE, d_gain_m)
    lay(sl, SL_MERGE + 8, d_shift_m)
    small_late.start(0)
    plane_a.finish()
    spread_up.finish()
    core_out(0, gf_down.at[core]).start()
    core_out(1, gf_up.at[core]).start()
    small_early.sum(3)

    owner_wait(OUT)
    out_half = owner_sum(OUT, 0, 64)
    for g in range(4):
        gb[g * 64 : g * 64 + 64, 0:128] = out_half[:, g * 128 : g * 128 + 128]
    for d in order:
        merge_owner(d).wait_recv()
    total = d_merge[group_a, chan].astype(F32)
    for d in range(PEERS):
        total += l2_m[d].astype(F32)
    gb[:, 128:256] = total.astype(BF16)
    plane_b.start()
    spread_m.third_start(lambda c: c)
    spread_qkv.third_sum()
    spread_qkv.back_start()
    small_late.sum(0)
    small_late.start(1)

    def page_rows(i, _):
        base = (i // WIN) * BAND + lax.rem(i, WIN) * SLOT
        for q in range(2):
            parts = []
            for par in range(2):
                lanes = par * 512 + q * 256
                for wc in range(WC):
                    at = pl.multiple_of(base + wc * WIN * SLOT, SLOT)
                    parts.append(tmp[pl.ds(at, SLOT), lanes : lanes + 256])
            y = dot(pages_sel_t[...], jnp.concatenate(parts, 0).astype(BF16))
            pg[lax.rem(2 * i + q + LIFT, 2 * ROWS)] = y.astype(BF16)
        return 0

    lax.fori_loop(0, ROWS, page_rows, 0)
    pages_copy = local(pg, pages_o, 14)
    pages_copy.start()

    plane_b.back_start()
    spread_m.third_sum()
    for copy in spread_m.back_y(False):
        copy.start()
    spread_qkv.finish()
    core_out(2, gf_qkv.at[core]).start()
    small_late.sum(1)
    small_late.start(2)

    blk_halo.wait_recv()
    outs = [local(blk_rx, block_o, 10), local(blk_hrx, block_halo_o, 9), local(se.at[4], early_o, 11)]
    core_out(0, gf_down.at[1 - core]).wait_recv()
    outs.append(local(gf_down, down_o, 12))
    core_out(1, gf_up.at[1 - core]).wait_recv()
    outs.append(local(gf_up, up_o, 13))
    for copy in outs:
        copy.start()

    plane_b.finish()
    gf_out[core] = gfb[core, :, 0:128]
    mf[group_a, chan] = gfb[core, :, 128:256]

    def merge_back(c, d):
        part = mf.at[group_a, c]
        return send(part, part, ID_BACK_Y + PEERS + d - 1, at_y(d))

    for d in order:
        merge_back(chan, d).start()
    core_out(3, gf_out.at[core]).start()
    for copy in spread_m.back_y(True):
        copy.wait_recv()
    spread_m.back_start()
    small_late.sum(2)
    small_late.start(3)
    late = [local(sl.at[4], late_o, 15)]
    core_out(2, gf_qkv.at[1 - core]).wait_recv()
    late.append(local(gf_qkv, qkv_o, 16))
    late[1].start()
    for d in order:
        merge_back(lax.rem(chan + CHUNKS - d, CHUNKS), d).wait_recv()
    core_out(4, mf.at[group_a]).start()
    spread_m.finish()
    core_out(5, mf.at[group_b]).start()
    core_out(3, gf_out.at[1 - core]).wait_recv()
    last = [local(gf_out, out_o, 17)]
    last[0].start()
    small_late.sum(3)
    late[0].start()
    for i in range(2):
        core_out(4 + i, mf.at[2 - 2 * core + i]).wait_recv()
    last.append(local(mf, merge_o, 18))
    last[1].start()

    for copy in [merged_halo, normed_halo, blk_halo, grad_halo, merge_core] + small_copies + blk_copies:
        copy.wait_send()
    for w in range(4):
        for copy in weight_copies[w]:
            copy.wait_send()
        for d in order:
            c = lax.rem(chan + CHUNKS - d, CHUNKS)
            if w in (QKV, OUT):
                copies = forward_copies(w, d, c)
            else:
                copies = [*around_copies(w, d, c), across_copy(w, d, c)]
            for copy in copies:
                copy.wait_send()
        for j in range(CHUNKS):
            core_copy(w, j, feed_chunk(j) if w in (UP, DOWN) else back_chunk(j)).wait_send()
    for d in order:
        owner_copy(DOWN, d).wait_send()
        owner_copy(OUT, d).wait_send()
        merge_owner(d).wait_send()
        merge_back(chan, d).wait_send()
    plane_a.left()
    plane_b.left()
    spread_up.left(feed_chunk)
    spread_qkv.left(back_chunk)
    spread_m.left(lambda c: c)
    for copy in spread_m.back_y(False):
        copy.wait_send()
    for group in (small_early, small_late):
        for level in range(4):
            for copy in group.copies(level):
                copy.wait_send()
    parts = (gf_down.at[core], gf_up.at[core], gf_qkv.at[core], gf_out.at[core], mf.at[group_a], mf.at[group_b])
    for n, part in enumerate(parts):
        core_out(n, part).wait_send()
    for copy in outs + late + last + [pages_copy]:
        copy.wait()


def kernel_call(args):
    hbm = pl.BlockSpec(memory_space=pl.ANY)
    s = jax.ShapeDtypeStruct
    outs = [
        s((CHUNKS, T, CH), BF16),
        s((WC * SHIFT * SLOT, CH), BF16),
        s((2 * ROWS, 2 * COLS, 256), BF16),
        s((2, HALF, D), BF16),
        s((2, HALF, 512), BF16),
        s((2, HALF, 3 * CH), BF16),
        s((2, HALF, 128), BF16),
        s((CHUNKS, CHUNKS, HALF, 128), BF16),
        s((SE_ROWS, 128), F32),
        s((SL_ROWS, 128), F32),
    ]

    def v(shape, dtype):
        return pltpu.VMEM(shape, dtype)

    scratch = [
        *[v(a.shape, BF16) for a in args[7:20]], v((8, 1024), F32),
        v((2 * ROWS, 2 * COLS, 256), BF16), *[v((WC * SHIFT * SLOT, D), BF16)] * 4, *[v((WC * SHIFT * SLOT, 2 * D), BF16)] * 2, v((COLS, 4 * ROWS, CH), BF16), v((CHUNKS, T, CH), BF16),
        v((WC * SHIFT * SLOT, CH), F32), v((WC * SHIFT * SLOT, CH), BF16), v((WC * SHIFT * SLOT, CH), BF16),
        v((1024, D), BF16), v((CHUNKS, 3, D, CH), BF16), v((CHUNKS, CH, D), BF16),
        v((CHUNKS, 4, 2, 64, 512), BF16), v((CHUNKS, 4, 2, 64, D), BF16), v((CHUNKS, 16, 128), F32),
        v((T, 1024), BF16), v((T, 2), F32), v((T, 1024), BF16), v((T, D), BF16), v((T, D), BF16),
        v((CHUNKS, T, 3 * CH), BF16), v((CHUNKS, NPAIR, PAIR, 512), BF16), v((T, D), BF16), v((CHUNKS, T, CH), F32),
        v((T, D), F32), v((T, D), BF16), v((T, D), BF16), v((T, D), BF16),
        v((T, 512), BF16), v((T, 512), BF16),
        v((4, CHUNKS, 512, 128), BF16), v((512, CH), BF16), v((PAIR, 128), BF16), v((HEADS_C * SLOT, 128), F32), v((PAIR, 512), F32),
        v((CHUNKS, T, 3 * CH), BF16), v((T, D), BF16), v((T, D), BF16), v((T, 1024), F32),
        v((CHUNKS, T, CH), BF16), v((WC * SHIFT * SLOT, CH), BF16), v((WC * SHIFT * SLOT, CH), BF16),
        v((2 * ROWS, 2 * COLS, 256), BF16),
        v((CHUNKS, CHUNKS, HALF, 128), BF16), v((CHUNKS, D, 3 * CH), BF16), v((CHUNKS, CH, D), BF16),
        v((CHUNKS, D, 512), BF16), v((CHUNKS, 512, D), BF16), v((CHUNKS, 16, 128), F32),
        v((CHUNKS, HALF, 3 * CH), BF16), v((CHUNKS, CH // 2, D), BF16), v((CHUNKS, HALF, 512), BF16),
        v((CHUNKS, HALF, D), BF16), v((2, CHUNKS, HALF, 128), BF16),
        v((PEERS, CH // 2, D), BF16), v((PEERS, HALF, D), BF16), v((PEERS, HALF, 128), BF16),
    ]
    for lanes in (512, 384, 128):
        scratch += [v((CHUNKS, PLANE, 16, lanes), BF16), v((CHUNKS, 16, lanes), BF16), v((PEERS, 16, lanes), BF16)]
    for lanes in (512, 256):
        scratch += [v((HALF, lanes), BF16), v((PLANE, 16, lanes), BF16), v((2, HALF, lanes), BF16)]
    scratch += [v((2, HALF, 512), BF16), v((2, HALF, 384), BF16), v((2, HALF, 128), BF16), v((CHUNKS, CHUNKS, HALF, 128), BF16)]
    for rows in (SE_ROWS, SL_ROWS):
        scratch += [v((5, rows, 128), F32), v((1, rows, 128), F32)] + [v((PEERS, rows, 128), F32)] * 3
    scratch += [
        pltpu.SemaphoreType.DMA((IDS.count,)),
        pltpu.SemaphoreType.DMA((IDS.count,)),
        pltpu.SemaphoreType.DMA((LOCAL,)),
    ]
    return pl.pallas_call(
        compute,
        out_shape=outs,
        in_specs=[hbm] * len(args),
        out_specs=[hbm] * len(outs),
        scratch_shapes=scratch,
        compiler_params=pltpu.CompilerParams(
            vmem_limit_bytes=63 * 1024 * 1024, collective_id=0, has_side_effects=True
        ),
    )(*args)


def finish(
    block, pages, down, up, qkv, out, merge, block_halo, early, late,
    block_o, pages_o, gain_m_o, shift_m_o, merge_o, gain_o, shift_o, qkv_o, qv_o, table_o, out_o, out_b_o, up_o, up_b_o,
    down_o, down_b_o, rms_o,
    block_i, pages_i, down_i, up_i, qkv_i, out_i, merge_i, block_f, pages_f, down_f, up_f, qkv_f, out_f, merge_f, slots_f, halo_f, isem, osem,
):
    chan = lax.axis_index("chan")
    ins = (down, up, qkv, merge, pages, block, out)
    bufs = (down_i, up_i, qkv_i, merge_i, pages_i, block_i, out_i)
    copies = [pltpu.make_async_copy(a, b, isem.at[i]) for i, (a, b) in enumerate(zip(ins, bufs))]
    for copy in copies:
        copy.start()

    def early_row(i):
        return early[pl.ds(chan * 6 + i - EARLY, 1), :]

    def late_row(i):
        return late[pl.ds(chan * EARLY + i, 1), :]

    def joined(ref, at, n):
        return jnp.concatenate([ref[at + i : at + i + 1, :] for i in range(n)], 1)

    gain_m_o[...] = late[SL_MERGE : SL_MERGE + 8, :]
    shift_m_o[...] = late[SL_MERGE + 8 : SL_MERGE + 16, :]
    gain_o[...] = jnp.concatenate([joined(late, SL_NORM, 4), joined(early, SE_NORM, 4)], 0)
    shift_o[...] = jnp.concatenate([joined(late, SL_NORM + 4, 4), joined(early, SE_NORM + 4, 4)], 0)
    qv_o[...] = jnp.concatenate([late_row(SM_QV), late_row(SM_QV + 1)], 0)
    for h in range(HEADS_C):
        table_o[h : h + 1, 0:128] = late_row(SM_TABLE + h)
        table_o[h : h + 1, 128:169] = late_row(SM_TABLE + HEADS_C + h)[:, 0:41]
    out_b_o[...] = early_row(SM_OUT_B)
    for i in range(4):
        up_b_o[i : i + 1, :] = early_row(SM_UP_B + i)
    down_b_o[...] = early_row(SM_DOWN_B)
    sums = jnp.sum(early[SE_SQ : SE_SQ + 8, :], 1, keepdims=True)
    roots = jnp.sqrt(sums * (1.0 / (1792 * COLS * D)))
    for i in range(3):
        rms_o[i] = roots[i, 0]

    outs = (down_o, up_o, qkv_o, merge_o, pages_o, block_o, out_o)
    stages = (down_f, up_f, qkv_f, merge_f, pages_f, block_f, out_f)
    done = [pltpu.make_async_copy(a, b, osem.at[i]) for i, (a, b) in enumerate(zip(stages, outs))]

    for n, (i, f) in enumerate(((down_i, down_f), (up_i, up_f))):
        copies[n].wait()
        f[...] = i[...].astype(F32)
        done[n].start()
    copies[2].wait()
    for i in range(3):
        qkv_f[i] = qkv_i[:, i * CH : i * CH + CH].astype(F32)
    done[2].start()
    copies[3].wait()
    for i in range(CHUNKS):
        merge_f[:, i * 128 : i * 128 + 128] = merge_i[i].astype(F32)
    done[3].start()
    copies[4].wait()

    def page(i, _):
        pages_f[i] = pages_i[i].astype(F32)
        return 0

    lax.fori_loop(0, 2 * ROWS, page, 0)
    done[4].start()
    copies[5].wait()
    slots_f[...] = block_i[...].astype(F32)
    halo_f[...] = block_halo[...].astype(F32)
    for wc in range(WC):
        for b in range(WIN):
            j = (wc * WIN + b + SHIFT) % COLS
            block_f[j, 0:SHIFT, :] = halo_f[pl.ds(wc * SHIFT * SLOT + b, SHIFT, stride=SLOT), :]
            for m in range(4 * ROWS // WIN):
                c, wr = m // 2, m % 2
                n = WIN - SHIFT if m == 4 * ROWS // WIN - 1 else WIN
                slot = wr * BAND + wc * WIN * SLOT + b
                block_f[j, SHIFT + WIN * m : SHIFT + WIN * m + n, :] = slots_f[c, pl.ds(slot, n, stride=SLOT), :]
    done[5].start()
    copies[6].wait()
    for k in range(2):
        for g in range(4):
            out_f[k * 64 : k * 64 + 64, g * 128 : g * 128 + 128] = out_i[k, g * 64 : g * 64 + 64, :].astype(F32)
    done[6].start()
    for copy in done:
        copy.wait()


def finish_call(parts):
    block, block_halo, pages, down, up, qkv, out, merge, early, late = parts
    vm = pl.BlockSpec(memory_space=pltpu.VMEM)
    hbm = pl.BlockSpec(memory_space=pl.ANY)

    def s(*shape):
        return jax.ShapeDtypeStruct(shape, F32)

    big = {
        "block": s(COLS, 4 * ROWS, CH), "pages": s(2 * ROWS, 2 * COLS, 256), "merge": s(1024, D),
        "qkv": s(3, D, CH), "out": s(CH, D), "up": s(D, 512), "down": s(512, D),
    }
    shapes = [
        big["block"], big["pages"], s(8, 128), s(8, 128), big["merge"], s(2, D), s(2, D), big["qkv"], s(2, CH), s(HEADS_C, 169),
        big["out"], s(1, 128), big["up"], s(4, 128), big["down"], s(1, 128), s(3),
    ]
    large = [any(shape is b for b in big.values()) for shape in shapes]
    ins = [block, pages, down.reshape(512, D), up.reshape(D, 512), qkv.reshape(D, 3 * CH), out, merge.reshape(CHUNKS, 1024, 128)]
    results = pl.pallas_call(
        finish,
        out_shape=shapes,
        in_specs=[hbm] * 7 + [vm] * 3,
        out_specs=[hbm if b else vm for b in large[:-1]] + [pl.BlockSpec(memory_space=pltpu.SMEM)],
        scratch_shapes=[pltpu.VMEM(a.shape, BF16) for a in ins]
        + [pltpu.VMEM(big[n].shape, F32) for n in ("block", "pages", "down", "up", "qkv", "out", "merge")]
        + [pltpu.VMEM(block.shape, F32), pltpu.VMEM(block_halo.shape, F32)]
        + [pltpu.SemaphoreType.DMA((7,)), pltpu.SemaphoreType.DMA((7,))],
        compiler_params=pltpu.CompilerParams(vmem_limit_bytes=63 * 1024 * 1024),
    )(*ins, block_halo, early, late)
    r = list(results)
    r[0] = r[0].transpose(1, 0, 2)
    r[2], r[3] = r[2].reshape(1024), r[3].reshape(1024)
    r[7] = r[7].transpose(1, 0, 2)
    r[11], r[13], r[15] = r[11].reshape(CH), r[13].reshape(512), r[15].reshape(CH)
    return tuple(r)


def body(
    pages, merge_gain, merge_shift, merge_weight, norm_gain, norm_shift, qkv_weight, qv_bias, rel_table,
    out_weight, out_bias, up_weight, up_bias, down_weight, down_bias, cotangent,
):
    args = [
        pages, cotangent.transpose(1, 0, 2), merge_weight, qkv_weight.transpose(1, 0, 2), out_weight, up_weight, down_weight,
        qv_bias, rel_table, out_bias, up_bias, down_bias, merge_gain, merge_shift, norm_gain, norm_shift, *constants(),
    ]
    return finish_call(kernel_call(args))


def solution(mesh):
    placed = (
        P(("space", "chan"), None, None), P(), P(), P(), P(), P(), P(None, None, "chan"), P(None, "chan"),
        P("chan", None), P("chan", None), P("chan"), P(None, "chan"), P("chan"), P("chan", None), P("chan"),
        P("space", None, "chan"),
    )
    outs = (
        P("space", None, "chan"), P(("space", "chan"), None, None), P(), P(), P(), P(), P(),
        P(None, None, "chan"), P(None, "chan"), P("chan", None), P("chan", None), P("chan"),
        P(None, "chan"), P("chan"), P("chan", None), P("chan"), P(),
    )
    return jax.shard_map(body, mesh=mesh, in_specs=placed, out_specs=outs, check_vma=False)
```

time: 726 us -> 126 us (0.17)
  waiting for transfers between devices: 531 us -> 0 us
  Pallas kernels: 83.2 us -> 125 us
  blocking collectives: 33 us -> 0 us
  local copies, waits for them, and re-layouts: 26.7 us -> 0 us
  starting transfers between devices: 21.2 us -> 0 us
  other arithmetic: 15.6 us -> 0 us
  between operations: 14.5 us -> 0.85 us
    psum x3 -> x0, waiting for transfers between devices: 366 us -> none  [the longest x2 260 us: body(): lax.psum((d_merge, d_repl, squares, d_small), ('space', 'chan'))]
    reduce_scatter x4 -> x0, waiting for transfers between devices: 108 us -> none  [reduced(): mine = lax.psum_scatter(chunked, 'chan', scatter_dimension=0, tiled=False)]
    all_gather x3 -> x0, waiting for transfers between devices: 51 us -> none  [the longest x1 31 us: body(): gather(down_weight)]
    pallas_call x1 -> x2, Pallas kernels: 83.2 us -> 125 us  [the longest x1 118 us: kernel_call(): pl.pallas_call(compute, out_shape=outs, in_specs=[hbm] * len(args), out_s...]
    all_gather x2 -> x0, blocking collectives: 33 us -> none  [the longest x1 21.3 us: body(): gather(small)]
    ppermute x4 -> x0, starting transfers between devices: 12.1 us -> none  [shifted(): lax.ppermute(shard, axis, [(i, (i + by) % count) for i in range(count)])]
    unnamed x42 -> x0, local copies, waits for them, and re-layouts: 9.74 us -> none
    convert_element_type x7 -> x0, other arithmetic: 9.09 us -> none  [the longest x3 4.05 us: reduced(): return lax.psum(mine, 'space').astype(F32)]
  transfers between devices with their start and end apart: 16 -> 0, of which waited for: 10 -> 0; matrix products, arithmetic and copies ran while one was open for 5% -> 0% of each run, Pallas kernels for 0% -> 0%
where the time goes in v3:
time: 126 us; the launch traced here: 125 us
  Pallas kernels  125 us (99%)
    pallas_call x1, Pallas kernels, kernel_call(): pl.pallas_call(compute, out_shape=outs, in_specs=[hbm] * len(args), out_s...  118 us
    pallas_call x1, Pallas kernels, finish_call(): pl.pallas_call(finish, out_shape=shapes, in_specs=[hbm] * 7 + [vm] * 3, o...  6.14 us

profile of v3, /device:TPU:1, one launch (start us, length us, event | category | flops | bytes accessed | tf_op | source)
XLA Modules:
  0.0 125.4 jit_solution(7708059492624019361)
XLA Ops:
  0.7 118.4 %shard_map.323 = (bf16[4,672,128]{2,1,0:T(8,128)(2,1)}, bf16[144,128]{1,0:T(8,128)(2,1)}, bf16[28,84,256]{2,1,0:T(8,128)(2,1)}, bf16[2,256,512]{2,1,0:T(8,128)(2...) custom-call(bf16[28,84,256]{2,1,0:T(8,128)(2,1)} %pages_in.1, ...), custom_call_target="tpu_custom_call" | custom-call | tf_op jit(solution)/shard_map/pallas_call | solution.py:1318
  119.1 6.1 %shard_map.324 = (f32[42,56,128]{2,1,0:T(8,128)}, f32[28,84,256]{2,1,0:T(8,128)}, f32[8,128]{1,0:T(8,128)}, f32[8,128]{1,0:T(8,128)}, f32[1024,512]{1,0:T(8,128)...) custom-call(bf16[4,672,128]{2,1,0:T(8,128)(2,1)} %get-tuple-element., ...), custom_call_target="tpu_custom_call" | custom-call | tf_op jit(solution)/shard_map/pallas_call | solution.py:1433

commit v4 on v3

--- a/solution.py
+++ b/solution.py
@@ -215,7 +215,7 @@
     pages_sel, pages_sel_t, table_sel, table_sel_t, repl,
     pages, m_htx, m_hrx, g_htx, g_hrx, mn_htx, mn_hrx, cot_v, cot_tx, cot_hf, cot_htx, cot_hrx, merge_w, qkv_w, out_w, up_w, down_w, small,
     x0, inv, mn, mt, n1, qkv, prob, att, norm, r1, u2, n2, g2,
-    hid, dpre, bias, ones, unit, lmat, gsum, dqkv, g1, gz, tmp,
+    hid, dpre, bias, ones, unit, lmat, dqkv, g1, gz, tmp,
     blk_rx, blk_htx, blk_hrx, pg,
     d_merge, d_qkv, d_out, d_up, d_down, d_small,
     l1_qkv, l1_out, l1_up, l1_down, l1_m, l2_out, l2_down, l2_m,
@@ -430,7 +430,7 @@
 
     small_copies = [send(small.at[chan], small.at[chan], ID_SMALL + d - 1, at_y(d)) for d in (1, 3, 2)]
     weight_copies = [[(weight_copy if w in (QKV, OUT) else eighth_copy)(w, d) for d in (1, 3, 2)] for w in range(4)]
-    for copy in small_copies + weight_copies[QKV][0:1]:
+    for copy in small_copies + weight_copies[QKV][0:2]:
         copy.start()
 
     def quads(i, _):
@@ -492,7 +492,7 @@
     m_htx[...] = halo_of(merged_last).astype(BF16)
     merged_halo = send(m_htx, m_hrx, ID_PAGES, up_rank)
     merged_halo.start()
-    for copy in weight_copies[QKV][1:] + weight_copies[OUT]:
+    for copy in weight_copies[QKV][2:] + weight_copies[OUT]:
         copy.start()
     for i in (2, 0, 1):
         for w in (UP, DOWN):
@@ -892,7 +892,7 @@
             have_across(UP, j)
             have_across(DOWN, j)
 
-        @pl.when(j == 0)
+        @pl.when(j == 1)
         def _():
             for w in (UP, DOWN):
                 pass_across(w, 3)
@@ -971,9 +971,9 @@
         c = lax.rem(chan + back_off(j), CHUNKS)
         heads = pl.ds(pl.multiple_of(c * CH, CH), CH)
         core_copy(OUT, j, c).start()
-        gsum[...] = jnp.zeros_like(gsum)
-
-        def window_pairs(t, _):
+        sum_rows = pl.ds(pl.multiple_of(c * PAIR, 16), PAIR)
+
+        def window_pairs(t, carry):
             pairs = [UNROLL * t + i for i in range(UNROLL)]
             parts = [[qkv[c, rows_of(p), i * CH : i * CH + CH] for i in range(3)] for p in pairs]
             d_atts = [hid[rows_of(p), heads].astype(F32) * norm[c, rows_of(p), :] for p in pairs]
@@ -991,24 +991,125 @@
                 results.append(jnp.concatenate([d_q, d_k, d_v], 1).astype(BF16))
             for p, result in zip(pairs, results):
                 dqkv[c, rows_of(p), :] = result
-            gsum[...] += total
-            return 0
-
-        lax.fori_loop(0, NPAIR // UNROLL, window_pairs, 0)
+            return carry + total
+
+        r1[sum_rows, :] = lax.fori_loop(0, NPAIR // UNROLL, window_pairs, jnp.zeros((PAIR, 512), F32))
         d_qkv[c] = dot_tn(n1[...], dqkv[c]).astype(BF16)
         core_copy(QKV, j, c).start()
 
-        def sums(p, total):
-            return total + col_sum(dqkv[c, rows_of(p), :].astype(F32))
-
-        total = lax.fori_loop(0, NPAIR, sums, jnp.zeros((1, 3 * CH), F32))
+        @pl.when(j > 0)
+        def _():
+            back_sums(j - 1)
+
+        @pl.when(j == 0)
+        def _():
+            small_early.sum(0)
+            small_early.start(1)
+
+        @pl.when(j == 1)
+        def _():
+            owner_wait(DOWN)
+            for t in range(0, HALF, 64):
+                ga[t : t + 64, :] = owner_sum(DOWN, t, 64)
+            plane_a.start()
+            spread_up.third_start(feed_chunk)
+            for copy in blk_copies:
+                copy.start()
+
+        @pl.when(j == 2)
+        def _():
+            small_early.sum(1)
+            small_early.start(2)
+
+        @pl.when(j == 3)
+        def _():
+            plane_a.back_start()
+            spread_up.third_sum()
+            spread_up.back_start()
+
+        return 0
+
+    lax.fori_loop(0, CHUNKS, attend_back, 0)
+
+    def norm1_back(half):
+        rows = band(half)
+        tmp[rows, D : 2 * D] = sum(dot_nt(dqkv[c, rows, :], wide(c)) for c in range(CHUNKS))
+        d_gain, d_shift = 0.0, 0.0
+        for i in three:
+            r = pair_rows(half, i)
+            u, inverse = unit_of(mt[r, :].astype(F32))
+            dy = tmp[r, D : 2 * D]
+            gz[r, :] = (tmp[r, 0:D] + norm_back(dy, u, inverse, gain[0])).astype(BF16)
+            d_gain, d_shift = d_gain + col_sum(dy * u), d_shift + col_sum(dy)
+        return d_gain, d_shift
+
+    d_gain0, d_shift0 = norm1_back(1)
+    g_htx[...] = halo_of(gz[band(1), :].astype(F32)).astype(BF16)
+    grad_halo = send(g_htx, g_hrx, ID_PG, down_rank)
+    grad_halo.start()
+    more_gain, more_shift = norm1_back(0)
+    d_gain0, d_shift0 = d_gain0 + more_gain, d_shift0 + more_shift
+    back_sums(PEERS)
+
+    merge_core = send(d_merge.at[pl.ds(2 - 2 * core, 2)], l1_m, ID_CORE_M, sibling)
+
+    def merge_grad(k):
+        lanes = pl.ds(pl.multiple_of(k * HALF, HALF), HALF)
+        total = dot_tn(mn[...], gz[:, lanes]).astype(BF16)
+        for i in range(2):
+            d_merge[2 * k + i] = total[:, i * 128 : i * 128 + 128].reshape(CHUNKS, HALF, 128)
+
+    merge_grad(1 - core)
+    merge_core.start()
+    merge_grad(core)
+    small_early.sum(2)
+    small_early.start(3)
+
+    for d in (1, 2, 3):
+        part = blk_rx.at[lax.rem(chan + CHUNKS - d, CHUNKS)]
+        send(part, part, ID_BLK + d - 1, at_y(d)).wait_recv()
+    blk_htx[...] = halo_of(blk_rx[PEERS, BAND:T, :].astype(F32)).astype(BF16)
+    blk_halo = send(blk_htx, blk_hrx, ID_BLK_HALO, down_band)
+    blk_halo.start()
+
+    merge_core.wait_recv()
+    for i in range(2):
+        for c in range(CHUNKS):
+            total = d_merge[2 * core + i, c].astype(F32) + l1_m[i, c].astype(F32)
+            d_merge[2 * core + i, c] = total.astype(BF16)
+
+    def merge_owner(d):
+        return send(d_merge.at[group_a, lax.rem(chan + d, CHUNKS)], l2_m.at[d - 1], ID_Y_M + d - 1, at_y(d))
+
+    for d in order:
+        merge_owner(d).start()
+    for c in range(CHUNKS):
+        spread_m.first_start(c, c)
+
+    grad_halo.wait_recv()
+    gz[band(1), :] = with_halo(gz[band(1), :].astype(F32), g_hrx[...].astype(F32)).astype(BF16)
+    sel_copies[1].wait()
+    tmp[...] = dot_nt(gz[...], merge_w[...])
+    d_gain_m, d_shift_m = 0.0, 0.0
+    for half in range(2):
+        for i in three:
+            r = pair_rows(half, i)
+            u = x0[r, :].astype(F32)
+            dy = tmp[r, :]
+            tmp[r, :] = norm_back(dy, u, inv[r, 0:1], repl[RP_GAIN0 : RP_GAIN0 + 1, :])
+            d_gain_m, d_shift_m = d_gain_m + col_sum(dy * u), d_shift_m + col_sum(dy)
+
+    def head_sums(c, _):
+        total = jnp.zeros((1, 3 * CH), F32)
+        for i in range(NPAIR):
+            total += col_sum(dqkv[c, i * PAIR : i * PAIR + PAIR, :].astype(F32))
         d_small[c, SM_QV : SM_QV + 1, :] = total[:, 0:CH]
         d_small[c, SM_QV + 1 : SM_QV + 2, :] = total[:, 2 * CH : 3 * CH]
-
         half = WIN * SLOT
+        both = r1[c * PAIR : c * PAIR + PAIR, :]
         for h in range(HEADS_C):
             lanes = slice(h * 128, h * 128 + 128)
-            folded = gsum[0:half, lanes] + pltpu.roll(gsum[half:PAIR, lanes], 128 - half, 1)
+            folded = both[0:half, lanes] + pltpu.roll(both[half:PAIR, lanes], 128 - half, 1)
             acc = jnp.zeros((SLOT, 128), F32)
             for a in range(WIN):
                 slab = folded[a * SLOT : a * SLOT + SLOT]
@@ -1022,110 +1123,10 @@
             d_table += dot_nt(rows.astype(BF16), table_sel[:, b_q * 128 : b_q * 128 + 128])
         d_small[c, SM_TABLE : SM_TABLE + 4, :] = d_table[0:4, 0:128]
         d_small[c, SM_TABLE + 4 : SM_TABLE + 8, :] = d_table[0:4, 128:256]
-
-        @pl.when(j > 0)
-        def _():
-            back_sums(j - 1)
-
-        @pl.when(j == 0)
-        def _():
-            small_early.sum(0)
-            small_early.start(1)
-
-        @pl.when(j == 1)
-        def _():
-            owner_wait(DOWN)
-            for t in range(0, HALF, 64):
-                ga[t : t + 64, :] = owner_sum(DOWN, t, 64)
-            plane_a.start()
-            spread_up.third_start(feed_chunk)
-            for copy in blk_copies:
-                copy.start()
-
-        @pl.when(j == 2)
-        def _():
-            small_early.sum(1)
-            small_early.start(2)
-
-        @pl.when(j == 3)
-        def _():
-            plane_a.back_start()
-            spread_up.third_sum()
-            spread_up.back_start()
-
         return 0
 
-    lax.fori_loop(0, CHUNKS, attend_back, 0)
-
-    def norm1_back(half):
-        rows = band(half)
-        tmp[rows, D : 2 * D] = sum(dot_nt(dqkv[c, rows, :], wide(c)) for c in range(CHUNKS))
-        d_gain, d_shift = 0.0, 0.0
-        for i in three:
-            r = pair_rows(half, i)
-            u, inverse = unit_of(mt[r, :].astype(F32))
-            dy = tmp[r, D : 2 * D]
-            gz[r, :] = (tmp[r, 0:D] + norm_back(dy, u, inverse, gain[0])).astype(BF16)
-            d_gain, d_shift = d_gain + col_sum(dy * u), d_shift + col_sum(dy)
-        return d_gain, d_shift
-
-    d_gain0, d_shift0 = norm1_back(1)
-    g_htx[...] = halo_of(gz[band(1), :].astype(F32)).astype(BF16)
-    grad_halo = send(g_htx, g_hrx, ID_PG, down_rank)
-    grad_halo.start()
-    more_gain, more_shift = norm1_back(0)
-    d_gain0, d_shift0 = d_gain0 + more_gain, d_shift0 + more_shift
-    back_sums(PEERS)
-
-    merge_core = send(d_merge.at[pl.ds(2 - 2 * core, 2)], l1_m, ID_CORE_M, sibling)
-
-    def merge_grad(k):
-        lanes = pl.ds(pl.multiple_of(k * HALF, HALF), HALF)
-        total = dot_tn(mn[...], gz[:, lanes]).astype(BF16)
-        for i in range(2):
-            d_merge[2 * k + i] = total[:, i * 128 : i * 128 + 128].reshape(CHUNKS, HALF, 128)
-
-    merge_grad(1 - core)
-    merge_core.start()
-    merge_grad(core)
-    small_early.sum(2)
-    small_early.start(3)
-
-    for d in (1, 2, 3):
-        part = blk_rx.at[lax.rem(chan + CHUNKS - d, CHUNKS)]
-        send(part, part, ID_BLK + d - 1, at_y(d)).wait_recv()
-    blk_htx[...] = halo_of(blk_rx[PEERS, BAND:T, :].astype(F32)).astype(BF16)
-    blk_halo = send(blk_htx, blk_hrx, ID_BLK_HALO, down_band)
-    blk_halo.start()
-
-    merge_core.wait_recv()
-    for i in range(2):
-        for c in range(CHUNKS):
-            total = d_merge[2 * core + i, c].astype(F32) + l1_m[i, c].astype(F32)
-            d_merge[2 * core + i, c] = total.astype(BF16)
-
-    def merge_owner(d):
-        return send(d_merge.at[group_a, lax.rem(chan + d, CHUNKS)], l2_m.at[d - 1], ID_Y_M + d - 1, at_y(d))
-
-    for d in order:
-        merge_owner(d).start()
     for c in range(CHUNKS):
-        spread_m.first_start(c, c)
-    spread_qkv.third_start(back_chunk)
-
-    grad_halo.wait_recv()
-    gz[band(1), :] = with_halo(gz[band(1), :].astype(F32), g_hrx[...].astype(F32)).astype(BF16)
-    sel_copies[1].wait()
-    tmp[...] = dot_nt(gz[...], merge_w[...])
-    d_gain_m, d_shift_m = 0.0, 0.0
-    for half in range(2):
-        for i in three:
-            r = pair_rows(half, i)
-            u = x0[r, :].astype(F32)
-            dy = tmp[r, :]
-            tmp[r, :] = norm_back(dy, u, inv[r, 0:1], repl[RP_GAIN0 : RP_GAIN0 + 1, :])
-            d_gain_m, d_shift_m = d_gain_m + col_sum(dy * u), d_shift_m + col_sum(dy)
-
+        head_sums(c, 0)
     for c in range(CHUNKS):
         sl[0, EARLY * c : EARLY * c + EARLY, :] = d_small[c, 0:EARLY, :]
     lay(sl, SL_NORM, d_gain0)
@@ -1151,8 +1152,7 @@
     gb[:, 128:256] = total.astype(BF16)
     plane_b.start()
     spread_m.third_start(lambda c: c)
-    spread_qkv.third_sum()
-    spread_qkv.back_start()
+    spread_qkv.third_start(back_chunk)
     small_late.sum(0)
     small_late.start(1)
 
@@ -1177,8 +1177,8 @@
     spread_m.third_sum()
     for copy in spread_m.back_y(False):
         copy.start()
-    spread_qkv.finish()
-    core_out(2, gf_qkv.at[core]).start()
+    spread_qkv.third_sum()
+    spread_qkv.back_start()
     small_late.sum(1)
     small_late.start(2)
 
@@ -1205,6 +1205,8 @@
     for copy in spread_m.back_y(True):
         copy.wait_recv()
     spread_m.back_start()
+    spread_qkv.finish()
+    core_out(2, gf_qkv.at[core]).start()
     small_late.sum(2)
     small_late.start(3)
     late = [local(sl.at[4], late_o, 15)]
@@ -1293,7 +1295,7 @@
         v((CHUNKS, T, 3 * CH), BF16), v((CHUNKS, NPAIR, PAIR, 512), BF16), v((T, D), BF16), v((CHUNKS, T, CH), F32),
         v((T, D), F32), v((T, D), BF16), v((T, D), BF16), v((T, D), BF16),
         v((T, 512), BF16), v((T, 512), BF16),
-        v((4, CHUNKS, 512, 128), BF16), v((512, CH), BF16), v((PAIR, 128), BF16), v((HEADS_C * SLOT, 128), F32), v((PAIR, 512), F32),
+        v((4, CHUNKS, 512, 128), BF16), v((512, CH), BF16), v((PAIR, 128), BF16), v((HEADS_C * SLOT, 128), F32),
         v((CHUNKS, T, 3 * CH), BF16), v((T, D), BF16), v((T, D), BF16), v((T, 1024), F32),
         v((CHUNKS, T, CH), BF16), v((WC * SHIFT * SLOT, CH), BF16), v((WC * SHIFT * SLOT, CH), BF16),
         v((2 * ROWS, 2 * COLS, 256), BF16),

time: 126 us -> 119 us (0.944)
  Pallas kernels: 125 us -> 118 us
    pallas_call x1, Pallas kernels: 118 us -> 112 us  [kernel_call(): pl.pallas_call(compute, out_shape=outs, in_specs=[hbm] * len(args), out_s...]
where the time goes in v4:
time: 119 us
  Pallas kernels  118 us (99%)
    pallas_call x1, Pallas kernels, kernel_call(): pl.pallas_call(compute, out_shape=outs, in_specs=[hbm] * len(args), out_s...  112 us
    pallas_call x1, Pallas kernels, finish_call(): pl.pallas_call(finish, out_shape=shapes, in_specs=[hbm] * 7 + [vm] * 3, o...  6.14 us

profile of v4, /device:TPU:1, one launch (start us, length us, event | category | flops | bytes accessed | tf_op | source)
XLA Modules:
  0.0 118.9 jit_solution(7012854868946768540)
XLA Ops:
  0.7 111.9 %shard_map.323 = (bf16[4,672,128]{2,1,0:T(8,128)(2,1)}, bf16[144,128]{1,0:T(8,128)(2,1)}, bf16[28,84,256]{2,1,0:T(8,128)(2,1)}, bf16[2,256,512]{2,1,0:T(8,128)(2...) custom-call(bf16[28,84,256]{2,1,0:T(8,128)(2,1)} %pages_in.1, ...), custom_call_target="tpu_custom_call" | custom-call | tf_op jit(solution)/shard_map/pallas_call | solution.py:1320
  112.6 6.1 %shard_map.324 = (f32[42,56,128]{2,1,0:T(8,128)}, f32[28,84,256]{2,1,0:T(8,128)}, f32[8,128]{1,0:T(8,128)}, f32[8,128]{1,0:T(8,128)}, f32[1024,512]{1,0:T(8,128)...) custom-call(bf16[4,672,128]{2,1,0:T(8,128)(2,1)} %get-tuple-element., ...), custom_call_target="tpu_custom_call" | custom-call | tf_op jit(solution)/shard_map/pallas_call | solution.py:1435

commit v5 on v4

--- a/solution.py
+++ b/solution.py
@@ -173,7 +173,7 @@
 ID_BLK = IDS.take(PEERS)
 ID_BLK_HALO = IDS.take(1)
 ID_CORE = IDS.take(4 * CHUNKS)
-ID_CORE_M = IDS.take(1)
+ID_CORE_M = IDS.take(2)
 ID_Y = IDS.take(2 * PEERS)
 ID_Y_M = IDS.take(PEERS)
 ID_FIRST = IDS.take(3 * CHUNKS * PLANE)
@@ -199,7 +199,7 @@
 
 
 def feed_off(j):
-    return lax.rem(2 * j, 5) - (j // 2 - j // 3)
+    return lax.rem(CHUNKS - j, CHUNKS)
 
 
 def back_off(j):
@@ -494,7 +494,7 @@
     merged_halo.start()
     for copy in weight_copies[QKV][2:] + weight_copies[OUT]:
         copy.start()
-    for i in (2, 0, 1):
+    for i in (0, 2, 1):
         for w in (UP, DOWN):
             weight_copies[w][i].start()
     mt[band(0), :] = merge_rows(0).astype(BF16)
@@ -810,12 +810,18 @@
             for copy in self.back_copies(True):
                 copy.wait_recv()
 
-        def left(self, chunk_of):
+        def left_first(self, chunk_of):
             for j in range(CHUNKS):
                 for copy in self.first_copies(j, chunk_of(j)):
                     copy.wait_send()
+
+        def left_later(self):
             for copy in [*self.third_copies(), *self.back_copies(False)]:
                 copy.wait_send()
+
+        def left(self, chunk_of):
+            self.left_first(chunk_of)
+            self.left_later()
 
     def half_rows(w):
         return lambda c, row, n: grads[w].at[c, step(n, core * halves[w] + row)]
@@ -1008,24 +1014,18 @@
 
         @pl.when(j == 1)
         def _():
+            for copy in blk_copies:
+                copy.start()
+
+        @pl.when(j == 2)
+        def _():
             owner_wait(DOWN)
             for t in range(0, HALF, 64):
                 ga[t : t + 64, :] = owner_sum(DOWN, t, 64)
             plane_a.start()
             spread_up.third_start(feed_chunk)
-            for copy in blk_copies:
-                copy.start()
-
-        @pl.when(j == 2)
-        def _():
             small_early.sum(1)
             small_early.start(2)
-
-        @pl.when(j == 3)
-        def _():
-            plane_a.back_start()
-            spread_up.third_sum()
-            spread_up.back_start()
 
         return 0
 
@@ -1051,7 +1051,7 @@
     d_gain0, d_shift0 = d_gain0 + more_gain, d_shift0 + more_shift
     back_sums(PEERS)
 
-    merge_core = send(d_merge.at[pl.ds(2 - 2 * core, 2)], l1_m, ID_CORE_M, sibling)
+    merge_core = [send(d_merge.at[2 - 2 * core + i], l1_m.at[i], ID_CORE_M + i, sibling) for i in range(2)]
 
     def merge_grad(k):
         lanes = pl.ds(pl.multiple_of(k * HALF, HALF), HALF)
@@ -1060,8 +1060,29 @@
             d_merge[2 * k + i] = total[:, i * 128 : i * 128 + 128].reshape(CHUNKS, HALF, 128)
 
     merge_grad(1 - core)
-    merge_core.start()
+    for copy in merge_core:
+        copy.start()
     merge_grad(core)
+
+    def merge_sum(i):
+        merge_core[i].wait_recv()
+        for c in range(CHUNKS):
+            total = d_merge[2 * core + i, c].astype(F32) + l1_m[i, c].astype(F32)
+            d_merge[2 * core + i, c] = total.astype(BF16)
+
+    def merge_owner(d):
+        return send(d_merge.at[group_a, lax.rem(chan + d, CHUNKS)], l2_m.at[d - 1], ID_Y_M + d - 1, at_y(d))
+
+    merge_sum(0)
+    for d in order:
+        merge_owner(d).start()
+    merge_sum(1)
+    for c in range(CHUNKS):
+        spread_m.first_start(c, c)
+
+    plane_a.back_start()
+    spread_up.third_sum()
+    spread_up.back_start()
     small_early.sum(2)
     small_early.start(3)
 
@@ -1071,20 +1092,6 @@
     blk_htx[...] = halo_of(blk_rx[PEERS, BAND:T, :].astype(F32)).astype(BF16)
     blk_halo = send(blk_htx, blk_hrx, ID_BLK_HALO, down_band)
     blk_halo.start()
-
-    merge_core.wait_recv()
-    for i in range(2):
-        for c in range(CHUNKS):
-            total = d_merge[2 * core + i, c].astype(F32) + l1_m[i, c].astype(F32)
-            d_merge[2 * core + i, c] = total.astype(BF16)
-
-    def merge_owner(d):
-        return send(d_merge.at[group_a, lax.rem(chan + d, CHUNKS)], l2_m.at[d - 1], ID_Y_M + d - 1, at_y(d))
-
-    for d in order:
-        merge_owner(d).start()
-    for c in range(CHUNKS):
-        spread_m.first_start(c, c)
 
     grad_halo.wait_recv()
     gz[band(1), :] = with_halo(gz[band(1), :].astype(F32), g_hrx[...].astype(F32)).astype(BF16)
@@ -1134,11 +1141,6 @@
     lay(sl, SL_MERGE, d_gain_m)
     lay(sl, SL_MERGE + 8, d_shift_m)
     small_late.start(0)
-    plane_a.finish()
-    spread_up.finish()
-    core_out(0, gf_down.at[core]).start()
-    core_out(1, gf_up.at[core]).start()
-    small_early.sum(3)
 
     owner_wait(OUT)
     out_half = owner_sum(OUT, 0, 64)
@@ -1182,6 +1184,34 @@
     small_late.sum(1)
     small_late.start(2)
 
+    for copy in spread_m.back_y(True):
+        copy.wait_recv()
+    spread_m.back_start()
+    plane_b.finish()
+    gf_out[core] = gfb[core, :, 0:128]
+    mf[group_a, chan] = gfb[core, :, 128:256]
+
+    def merge_back(c, d):
+        part = mf.at[group_a, c]
+        return send(part, part, ID_BACK_Y + PEERS + d - 1, at_y(d))
+
+    for d in order:
+        merge_back(chan, d).start()
+    core_out(3, gf_out.at[core]).start()
+    spread_qkv.finish()
+    core_out(2, gf_qkv.at[core]).start()
+    small_late.sum(2)
+    small_late.start(3)
+    late = [local(sl.at[4], late_o, 15)]
+    core_out(2, gf_qkv.at[1 - core]).wait_recv()
+    late.append(local(gf_qkv, qkv_o, 16))
+    late[1].start()
+    plane_a.finish()
+    spread_up.finish()
+    core_out(0, gf_down.at[core]).start()
+    core_out(1, gf_up.at[core]).start()
+    small_early.sum(3)
+
     blk_halo.wait_recv()
     outs = [local(blk_rx, block_o, 10), local(blk_hrx, block_halo_o, 9), local(se.at[4], early_o, 11)]
     core_out(0, gf_down.at[1 - core]).wait_recv()
@@ -1191,44 +1221,7 @@
     for copy in outs:
         copy.start()
 
-    plane_b.finish()
-    gf_out[core] = gfb[core, :, 0:128]
-    mf[group_a, chan] = gfb[core, :, 128:256]
-
-    def merge_back(c, d):
-        part = mf.at[group_a, c]
-        return send(part, part, ID_BACK_Y + PEERS + d - 1, at_y(d))
-
-    for d in order:
-        merge_back(chan, d).start()
-    core_out(3, gf_out.at[core]).start()
-    for copy in spread_m.back_y(True):
-        copy.wait_recv()
-    spread_m.back_start()
-    spread_qkv.finish()
-    core_out(2, gf_qkv.at[core]).start()
-    small_late.sum(2)
-    small_late.start(3)
-    late = [local(sl.at[4], late_o, 15)]
-    core_out(2, gf_qkv.at[1 - core]).wait_recv()
-    late.append(local(gf_qkv, qkv_o, 16))
-    late[1].start()
-    for d in order:
-        merge_back(lax.rem(chan + CHUNKS - d, CHUNKS), d).wait_recv()
-    core_out(4, mf.at[group_a]).start()
-    spread_m.finish()
-    core_out(5, mf.at[group_b]).start()
-    core_out(3, gf_out.at[1 - core]).wait_recv()
-    last = [local(gf_out, out_o, 17)]
-    last[0].start()
-    small_late.sum(3)
-    late[0].start()
-    for i in range(2):
-        core_out(4 + i, mf.at[2 - 2 * core + i]).wait_recv()
-    last.append(local(mf, merge_o, 18))
-    last[1].start()
-
-    for copy in [merged_halo, normed_halo, blk_halo, grad_halo, merge_core] + small_copies + blk_copies:
+    for copy in [merged_halo, normed_halo, blk_halo, grad_halo] + merge_core + small_copies + blk_copies:
         copy.wait_send()
     for w in range(4):
         for copy in weight_copies[w]:
@@ -1247,22 +1240,45 @@
         owner_copy(DOWN, d).wait_send()
         owner_copy(OUT, d).wait_send()
         merge_owner(d).wait_send()
+    plane_a.left()
+    spread_up.left(feed_chunk)
+    spread_qkv.left_first(back_chunk)
+    spread_m.left_first(lambda c: c)
+    for level in range(4):
+        for copy in small_early.copies(level):
+            copy.wait_send()
+
+    for d in order:
+        merge_back(lax.rem(chan + CHUNKS - d, CHUNKS), d).wait_recv()
+    core_out(4, mf.at[group_a]).start()
+    spread_m.finish()
+    core_out(5, mf.at[group_b]).start()
+    here_merge = local(mf.at[pl.ds(2 * core, 2)], merge_o.at[pl.ds(2 * core, 2)], 18)
+    here_merge.start()
+    core_out(3, gf_out.at[1 - core]).wait_recv()
+    last = [local(gf_out, out_o, 17)]
+    last[0].start()
+    for i in range(2):
+        core_out(4 + i, mf.at[2 - 2 * core + i]).wait_recv()
+    last.append(local(mf.at[pl.ds(2 - 2 * core, 2)], merge_o.at[pl.ds(2 - 2 * core, 2)], 19))
+    last[1].start()
+    small_late.sum(3)
+    late[0].start()
+
+    for d in order:
         merge_back(chan, d).wait_send()
-    plane_a.left()
     plane_b.left()
-    spread_up.left(feed_chunk)
-    spread_qkv.left(back_chunk)
-    spread_m.left(lambda c: c)
+    spread_qkv.left_later()
+    spread_m.left_later()
     for copy in spread_m.back_y(False):
         copy.wait_send()
-    for group in (small_early, small_late):
-        for level in range(4):
-            for copy in group.copies(level):
-                copy.wait_send()
+    for level in range(4):
+        for copy in small_late.copies(level):
+            copy.wait_send()
     parts = (gf_down.at[core], gf_up.at[core], gf_qkv.at[core], gf_out.at[core], mf.at[group_a], mf.at[group_b])
     for n, part in enumerate(parts):
         core_out(n, part).wait_send()
-    for copy in outs + late + last + [pages_copy]:
+    for copy in outs + late + last + [pages_copy, here_merge]:
         copy.wait()
 
 

time: 119 us -> 117 us (0.983)
  Pallas kernels: 118 us -> 116 us
    pallas_call x1, Pallas kernels: 112 us -> 110 us  [kernel_call(): pl.pallas_call(compute, out_shape=outs, in_specs=[hbm] * len(args), out_s...]
where the time goes in v5:
time: 117 us
  Pallas kernels  116 us (99%)
    pallas_call x1, Pallas kernels, kernel_call(): pl.pallas_call(compute, out_shape=outs, in_specs=[hbm] * len(args), out_s...  110 us
    pallas_call x1, Pallas kernels, finish_call(): pl.pallas_call(finish, out_shape=shapes, in_specs=[hbm] * 7 + [vm] * 3, o...  6.14 us

profile of v5, /device:TPU:1, one launch (start us, length us, event | category | flops | bytes accessed | tf_op | source)
XLA Modules:
  0.0 117.1 jit_solution(15078113316456645534)
XLA Ops:
  0.7 110.1 %shard_map.323 = (bf16[4,672,128]{2,1,0:T(8,128)(2,1)}, bf16[144,128]{1,0:T(8,128)(2,1)}, bf16[28,84,256]{2,1,0:T(8,128)(2,1)}, bf16[2,256,512]{2,1,0:T(8,128)(2...) custom-call(bf16[28,84,256]{2,1,0:T(8,128)(2,1)} %pages_in.1, ...), custom_call_target="tpu_custom_call" | custom-call | tf_op jit(solution)/shard_map/pallas_call | solution.py:1336
  110.8 6.1 %shard_map.324 = (f32[42,56,128]{2,1,0:T(8,128)}, f32[28,84,256]{2,1,0:T(8,128)}, f32[8,128]{1,0:T(8,128)}, f32[8,128]{1,0:T(8,128)}, f32[1024,512]{1,0:T(8,128)...) custom-call(bf16[4,672,128]{2,1,0:T(8,128)(2,1)} %get-tuple-element., ...), custom_call_target="tpu_custom_call" | custom-call | tf_op jit(solution)/shard_map/pallas_call | solution.py:1451
